TPU v7x, 32 devices: a whole 2x2x4 slice. The times are simulated.
32 devices in a mesh: grp: 2 (over x), tile: 16 (over z, y, core).
Axes of the slice: x: 2, y: 2, z: 4, core: 2. Of those that a mesh axis runs over, the one named last changes fastest.
Arguments:
- ocean_state: float32 [3, 24, 256, 4096], P(None, None, 'tile', 'grp'), may hold values from -6 to 6
- biharmonic: float32 [256, 4096], P('tile', 'grp'), may hold values from 0.004 to 0.014
- prev_stress: float32 [2, 256, 4096], P(None, 'tile', 'grp'), may hold values from -4 to 4
- ice_state: float32 [5, 256, 4096], P(None, 'tile', 'grp'), may hold values from -2 to 2
- strength: float32 [256, 4096], P('tile', 'grp'), may hold values from 0.5 to 2
- ice_mass: float32 [256, 4096], P('tile', 'grp'), may hold values from 0.5 to 2
- ice_fraction: float32 [256, 4096], P('tile', 'grp'), may hold values from 0.15 to 1
- wind_stress: float32 [2, 256, 4096], P(None, 'tile', 'grp'), may hold values from -2 to 2
- ice_count: int32 [32], P(('grp', 'tile')), may hold values from 0 to 16, as said below
- ice_list: int32 [32, 16], P(('grp', 'tile')), may hold values from 0 to 15, as said below
Outputs:
- ocean_out: float32 [3, 24, 256, 4096], P(None, None, 'tile', 'grp')
- ice_out: float32 [5, 256, 4096], P(None, 'tile', 'grp')
- stress_out: float32 [2, 256, 4096], P(None, 'tile', 'grp')
Inputs may be any that keep to these rules, and one draw needn't show every extreme that they name: `ice_count`: the tiles g * 16 + t and g * 16 + (t + 16 / 2) % 16 together have at most 16 ice-covered blocks, and some such pair has exactly 16; tiles near the first and last rows have the most. `ice_list`: each row is an ordering of the tile's 16 block numbers.
All inputs are finite; a program needn't handle non-finite values.
Results may differ from a plain program's by a relative error of at most 0.00002.
Values sent between devices are 32-bit elements; how exact they have to be, the bound alone decides.
No kernel may reach another device: no remote copies, remote signals or barrier semaphores. Data moves between devices by JAX's collectives and lax.ppermute only.
A program may use at most 192 MiB of HBM per device.

v0:
```python
import jax
import jax.numpy as jnp
from jax import lax
from jax.sharding import PartitionSpec as P

BY = 16
BX = 128
SUBCYCLES = 64


kv_mix = 0.2
relax_rate = 0.5
sub_step = 0.3
drag_coef = 1.0
turning = 0.3
delta_min = 0.5
coriolis_scale = 0.2


def padded_2(x, sides, width, wrap):
    for axis, dim in sides:
        size, length = (lax.axis_size(axis), x.shape[dim])
        up = [(i, (i + 1) % size) for i in range(size if wrap else size - 1)]
        down = [(j, i) for i, j in up]
        last = lax.slice_in_dim(x, length - width, length, axis=dim)
        leading = lax.slice_in_dim(x, 0, width, axis=dim)
        before = lax.ppermute(last, axis, up)
        after = lax.ppermute(leading, axis, down)
        x = jnp.concatenate([before, x, after], axis=dim)
    return x


def ahead_diff(field, axis):
    length = field.shape[axis]
    inner = lax.slice_in_dim(field, 1, length, axis=axis) - lax.slice_in_dim(
        field, 0, length - 1, axis=axis
    )
    return jnp.concatenate(
        [inner, jnp.zeros_like(lax.slice_in_dim(field, 0, 1, axis=axis))], axis=axis
    )


def behind_diff(field, axis):
    length = field.shape[axis]
    inner = lax.slice_in_dim(field, 1, length, axis=axis) - lax.slice_in_dim(
        field, 0, length - 1, axis=axis
    )
    return jnp.concatenate([lax.slice_in_dim(field, 0, 1, axis=axis), inner], axis=axis)


def ice_dynamics(fields, y_axis, x_axis):
    (
        vel_x,
        vel_y,
        stress_xx,
        stress_yy,
        stress_xy,
        ice_strength,
        mass,
        fraction,
        wind_x,
        wind_y,
        ocean_x,
        ocean_y,
    ) = fields
    pressure = relax_rate * ice_strength
    inertia = mass + sub_step * drag_coef

    def subcycle(step_index, carry):
        vel_x, vel_y, stress_xx, stress_yy, stress_xy = carry
        du_dx = ahead_diff(vel_x, x_axis)
        du_dy = ahead_diff(vel_x, y_axis)
        dv_dx = ahead_diff(vel_y, x_axis)
        dv_dy = ahead_diff(vel_y, y_axis)
        divergence = du_dx + dv_dy
        tension = du_dx - dv_dy
        shearing = du_dy + dv_dx
        deform = jnp.sqrt(
            divergence * divergence
            + 0.25 * (tension * tension + shearing * shearing)
            + delta_min * delta_min
        )
        sigma_one = (stress_xx + stress_yy + pressure * (divergence / deform - 1.0)) / (
            1.0 + relax_rate
        )
        sigma_two = (stress_xx - stress_yy + 0.25 * pressure * tension / deform) / (
            1.0 + relax_rate
        )
        stress_xy = (stress_xy + 0.125 * pressure * shearing / deform) / (1.0 + relax_rate)
        stress_xx = 0.5 * (sigma_one + sigma_two)
        stress_yy = 0.5 * (sigma_one - sigma_two)
        force_x = behind_diff(stress_xx, x_axis) + behind_diff(stress_xy, y_axis)
        force_y = behind_diff(stress_xy, x_axis) + behind_diff(stress_yy, y_axis)
        new_x = (
            mass * vel_x
            + sub_step * (force_x + wind_x + drag_coef * ocean_x + turning * mass * vel_y)
        ) / inertia
        new_y = (
            mass * vel_y
            + sub_step * (force_y + wind_y + drag_coef * ocean_y - turning * mass * vel_x)
        ) / inertia
        return (new_x, new_y, stress_xx, stress_yy, stress_xy)

    vel_x, vel_y, stress_xx, stress_yy, stress_xy = lax.fori_loop(
        0, SUBCYCLES, subcycle, (vel_x, vel_y, stress_xx, stress_yy, stress_xy)
    )
    drag_x = fraction * drag_coef * (vel_x - ocean_x) + (1.0 - fraction) * wind_x
    drag_y = fraction * drag_coef * (vel_y - ocean_y) + (1.0 - fraction) * wind_y
    return (vel_x, vel_y, stress_xx, stress_yy, stress_xy, drag_x, drag_y)


def run_blocks(blocks):
    return jnp.stack(ice_dynamics([blocks[:, index] for index in range(12)], 1, 2), axis=1)


def laplace(padded):
    return (
        padded[..., 1:-1, 2:]
        + padded[..., 1:-1, :-2]
        + padded[..., 2:, 1:-1]
        + padded[..., :-2, 1:-1]
        - 4.0 * padded[..., 1:-1, 1:-1]
    )


def vertical(field):
    upper = jnp.concatenate([field[:1], field[:-1]], axis=0)
    lower = jnp.concatenate([field[1:], field[-1:]], axis=0)
    return upper + lower - 2.0 * field


def ocean_field(padded, field, biharmonic):
    return field - biharmonic * laplace(laplace(padded)) + kv_mix * vertical(field)


def per_device(
    ocean_state,
    biharmonic,
    prev_stress,
    ice_state,
    strength,
    ice_mass,
    ice_fraction,
    wind_stress,
    ice_count,
    ice_list,
):
    tile_rows = ocean_state.shape[2]
    tile_cols = ocean_state.shape[3]
    total_rows = tile_rows * lax.axis_size("tile")
    row_padded = padded_2(ocean_state, (("tile", 2),), 2, False)
    padded = padded_2(row_padded, (("grp", 3),), 2, True)
    rows = (lax.axis_index("tile") * tile_rows + jnp.arange(tile_rows)).astype(jnp.float32) + 0.5
    coriolis = (coriolis_scale * (2.0 * rows / total_rows - 1.0))[:, None]
    mixed = [ocean_field(padded[index], ocean_state[index], biharmonic) for index in range(3)]
    east = mixed[0] + coriolis * ocean_state[1]
    north = mixed[1] - coriolis * ocean_state[0]
    east = east.at[0].add(prev_stress[0])
    north = north.at[0].add(prev_stress[1])
    ocean_out = jnp.stack([east, north, mixed[2]])
    row_blocks = tile_rows // BY
    col_blocks = tile_cols // BX
    block_total = row_blocks * col_blocks
    stacked = jnp.stack(
        [
            ice_state[0],
            ice_state[1],
            ice_state[2],
            ice_state[3],
            ice_state[4],
            strength,
            ice_mass,
            ice_fraction,
            wind_stress[0],
            wind_stress[1],
            ocean_state[0, 0],
            ocean_state[1, 0],
        ]
    )
    blocks = (
        stacked.reshape(12, row_blocks, BY, col_blocks, BX)
        .transpose(1, 3, 0, 2, 4)
        .reshape(block_total, 12, BY, BX)
    )
    count = ice_count[0]
    listed_blocks = ice_list[0]
    slots = jnp.arange(block_total, dtype=jnp.int32)
    position = jnp.sum(
        jnp.where(listed_blocks[:, None] == slots[None, :], slots[:, None], 0), axis=0
    )
    covered = position < count
    results = run_blocks(blocks)
    mask = covered[:, None, None, None]
    new_state = jnp.where(mask, results[:, :5], blocks[:, :5])
    new_stress = jnp.where(mask, results[:, 5:7], blocks[:, 8:10])
    combined = jnp.concatenate([new_state, new_stress], axis=1)
    combined = (
        combined.reshape(row_blocks, col_blocks, 7, BY, BX)
        .transpose(2, 0, 3, 1, 4)
        .reshape(7, tile_rows, tile_cols)
    )
    return (ocean_out, combined[:5], combined[5:])


def solution(mesh):
    placed = (
        P(None, None, "tile", "grp"),
        P("tile", "grp"),
        P(None, "tile", "grp"),
        P(None, "tile", "grp"),
        P("tile", "grp"),
        P("tile", "grp"),
        P("tile", "grp"),
        P(None, "tile", "grp"),
        P(("grp", "tile")),
        P(("grp", "tile"), None),
    )
    return jax.shard_map(
        per_device,
        mesh=mesh,
        in_specs=placed,
        out_specs=(P(None, None, "tile", "grp"), P(None, "tile", "grp"), P(None, "tile", "grp")),
        check_vma=False,
    )
```

profile of v0, /device:TPU:24, one launch (start us, length us, event | category | flops | bytes accessed | tf_op | source)
XLA Modules:
  0.0 218.4 jit_solution(5854892747731397742)
XLA Ops:
  0.6 6.5 %fusion.42 = (f32[3,24,2,2048]{3,2,1,0:T(2,128)}, f32[3,24,2,2048]{3,2,1,0:T(2,128)}) fusion(f32[3,24,16,2048]{3,2,1,0:T(8,128)} %param.16), kind=kLoop, calls=%fused_computation.148 | loop fusion | bytes 4718592 | tf_op jit(solution)/shard_map/slice | solution.py:25
  7.1 2.9 %collective-permute-start.1 = (f32[3,24,2,2048]{3,2,1,0:T(2,128)}, f32[3,24,2,2048]{3,2,1,0:T(2,128)}, u32[]{:S(2)}, u32[]{:S(2)}) collective-permute-start(f32[3,24,2,2048]{3,2,1,0:T(2,128)} %get-tuple-element.308), channel_id=1, source_target_pairs={{1,0},{2,1},{3,2},{4,3},{5,4},{6,5},{7,6},{8,7},{9,8},{10,9},{11,1... | collective-permute-start | bytes 3538952 | tf_op jit(solution)/shard_map/ppermute | solution.py:28
  10.0 1.9 collective-permute-start
  12.0 2.0 slice_bitcast_fusion.24
  15.4 58.5 %while.22 = (s32[]{:T(128)}, f32[16,16,128]{2,1,0:T(8,128)S(1)}, f32[16,16,128]{2,1,0:T(8,128)S(1)}, f32[16,16,128]{2,1,0:T(8,128)S(1)}, f32[16,16,128]{2,1,0:T(...) while((s32[]{:T(128)}, f32[16,16,128]{2,1,0:T(8,128)S(1)}, ...), condition=%wide.region_2.3_spmd, body=%wide.region_1.0_spmd.sunk | while | flops 2022402 | bytes 6850693 | solution.py:104
  75.4 14.1 %slice_bitcast_fusion.7 = (f32[23,16,2048]{2,1,0:T(8,128)}, f32[23,16,2048]{2,1,0:T(8,128)}, f32[23,16,2048]{2,1,0:T(8,128)}, f32[23,16,2048]{2,1,0:T(8,128)}, f...) fusion(f32[3,24,16,2048]{3,2,1,0:T(8,128)} %param.16), kind=kLoop, calls=%fused_computation.96 | loop fusion | bytes 36175872 | tf_op jit(solution)/shard_map/slice | solution.py:128
  89.7 0.8 slice-done.2
  90.5 3.9 %pad_maximum_fusion = f32[3,24,20,2048]{3,2,1,0:T(8,128)S(1)} fusion(f32[3,24,2,2048]{3,2,1,0:T(2,128)} %collective-permute-done.1, f32[3,24,16,2048]{3,2,1,0:T(8,128)S(1)} %bitcast.181, f32[3,24,2,2048]{3,2,1,0:T(2,128)} %collective-permute-done), kind=kLoop, calls=%fused_computation.31 | loop fusion | flops 5898240 | bytes 23592960 | tf_op jit(solution)/shard_map/concatenate | solution.py:29
  94.4 5.0 %copy-done = f32[3,24,20,2048]{3,2,1,0:T(8,128)} copy-done((f32[3,24,20,2048]{3,2,1,0:T(8,128)}, f32[3,24,20,2048]{3,2,1,0:T(8,128)S(1)}, u32[]{:S(2)}) %copy-start) | copy-done | bytes 11796504
  99.4 0.3 fusion.41
  99.7 0.4 copy.102
  100.2 1.5 collective-permute-start.2
  101.7 0.4 copy.103
  102.1 0.6 collective-permute-start.3
  102.8 0.9 slice.528
  103.8 0.7 slice.530
  104.5 0.4 collective-permute-done.2
  104.9 0.5 copy.104
  105.4 1.2 collective-permute-done.3
  106.6 0.5 copy.105
  107.1 18.3 %concatenate.71 = f32[3,24,20,2052]{3,2,1,0:T(8,128)} concatenate(f32[3,24,20,2]{3,2,1,0:T(8,128)S(1)} %copy.104, f32[3,24,20,2048]{3,2,1,0:T(8,128)} %copy-done, f32[3,24,20,2]{3,2,1,0:T(8,128)S(1)} %copy.105), dimensions={3} | concatenate | bytes 23639040 | tf_op jit(solution)/shard_map/concatenate | solution.py:29
  125.3 11.1 %slice_bitcast_fusion.2 = (f32[24,20,2052]{2,1,0:T(8,128)}, f32[24,20,2052]{2,1,0:T(8,128)}, f32[24,20,2052]{2,1,0:T(8,128)}) fusion(f32[3,24,20,2052]{3,2,1,0:T(8,128)} %concatenate.71), kind=kLoop, calls=%fused_computation.50 | loop fusion | bytes 23639040 | tf_op jit(solution)/shard_map/squeeze | solution.py:155
  136.5 15.5 %fusion.14 = f32[24,18,2050]{2,1,0:T(8,128)S(1)} fusion(f32[24,20,2052]{2,1,0:T(8,128)} %get-tuple-element.288), kind=kLoop, calls=%fused_computation.46 | loop fusion | flops 4428000 | bytes 21254400 | tf_op jit(solution)/shard_map/sub | solution.py:118
  152.1 6.8 %fusion.29 = f32[24,16,2048]{2,1,0:T(8,128)} fusion(f32[24,18,2050]{2,1,0:T(8,128)S(1)} %fusion.14, f32[23,16,2048]{2,1,0:T(8,128)} %get-tuple-element.305, f32[1,16,2048]{2,1,0:T(8,128)S(1)} %copy-done.4, f32[1,16,2048]{2,1,0:T(8,128)S(1)} %copy-done.3, f32[23,16,2048]{2,1,0:T(8,128)} %get-tuple-element.301, f32[3,24,16,2048]{3,2,1,0:T(8,128)S(1)} %bitcast.183, ...), kind=kLoop, calls=%fused_computation.74 | loop fusion | flops 12582912 | bytes 31588416 | tf_op jit(solution)/shard_map/add | solution.py:156
  158.9 1.9 copy.144
  160.8 31.4 %fusion.12 = (f32[24,18,2050]{2,1,0:T(8,128)}, f32[24,18,2050]{2,1,0:T(8,128)}) fusion(f32[24,20,2052]{2,1,0:T(8,128)} %get-tuple-element.289, f32[24,20,2052]{2,1,0:T(8,128)} %get-tuple-element.290), kind=kLoop, calls=%fused_computation.34 | loop fusion | flops 8856000 | bytes 42508800 | tf_op jit(solution)/shard_map/sub | solution.py:118
  192.2 13.7 %fusion.24 = f32[24,16,2048]{2,1,0:T(8,128)S(1)} fusion(f32[24,18,2050]{2,1,0:T(8,128)} %get-tuple-element.325, f32[23,16,2048]{2,1,0:T(8,128)} %get-tuple-element.304, f32[1,16,2048]{2,1,0:T(8,128)} %get-tuple-element.297, f32[1,16,2048]{2,1,0:T(8,128)} %get-tuple-element.296, f32[23,16,2048]{2,1,0:T(8,128)} %get-tuple-element.303, ...), kind=kLoop, calls=%fused_computation.65 | loop fusion | flops 12582912 | bytes 31588416 | tf_op jit(solution)/shard_map/sub | solution.py:157
  206.0 0.3 copy.145
  206.3 0.6 copy-done.5
  206.9 0.9 fusion.40
  207.9 5.9 %fusion.19 = f32[1,24,16,2048]{3,2,1,0:T(8,128)S(1)} fusion(f32[24,18,2050]{2,1,0:T(8,128)S(1)} %bitcast.186, f32[23,16,2048]{2,1,0:T(8,128)} %get-tuple-element.302, f32[1,16,2048]{2,1,0:T(8,128)S(1)} %get-tuple-element.295, f32[1,16,2048]{2,1,0:T(8,128)S(1)} %get-tuple-element.300, f32[23,16,2048]{2,1,0:T(8,128)} %get-tuple-element.306, ...), kind=kLoop, calls=%fused_computation.56 | loop fusion | flops 11010048 | bytes 28442624 | tf_op jit(solution)/shard_map/stack | solution.py:160
  213.8 4.6 %pad_maximum_fusion.1 = f32[3,24,16,2048]{3,2,1,0:T(8,128)} fusion(f32[1,24,16,2048]{3,2,1,0:T(8,128)S(1)} %fusion.19, f32[1,24,16,2048]{3,2,1,0:T(8,128)S(1)} %get-tuple-element.323, f32[1,24,16,2048]{3,2,1,0:T(8,128)S(1)} %get-tuple-element.322), kind=kLoop, calls=%fused_computation.32 | loop fusion | flops 4718592 | bytes 18874368 | tf_op jit(solution)/shard_map/stack | solution.py:160
  (786 shorter events, 54.7 us)
Async XLA Ops:
  0.6 13.4 %copy-start.2 = (f32[5,16,2048]{2,1,0:T(8,128)S(1)}, f32[5,16,2048]{2,1,0:T(8,128)}, u32[]{:S(2)}) copy-start(f32[5,16,2048]{2,1,0:T(8,128)} %param.19) | copy-start | bytes 1966084
  7.1 7.1 %copy-start.7 = (f32[16,2048]{1,0:T(8,128)S(1)}, f32[16,2048]{1,0:T(8,128)}, u32[]{:S(2)}) copy-start(f32[16,2048]{1,0:T(8,128)} %param.20) | copy-start | bytes 393220
  7.1 7.1 %copy-start.8 = (f32[16,2048]{1,0:T(8,128)S(1)}, f32[16,2048]{1,0:T(8,128)}, u32[]{:S(2)}) copy-start(f32[16,2048]{1,0:T(8,128)} %param.21) | copy-start | bytes 393220
  7.1 7.2 %copy-start.9 = (f32[16,2048]{1,0:T(8,128)S(1)}, f32[16,2048]{1,0:T(8,128)}, u32[]{:S(2)}) copy-start(f32[16,2048]{1,0:T(8,128)} %param.22) | copy-start | bytes 393220
  7.1 7.2 %copy-start.6 = (f32[2,16,2048]{2,1,0:T(8,128)S(1)}, f32[2,16,2048]{2,1,0:T(8,128)}, u32[]{:S(2)}) copy-start(f32[2,16,2048]{2,1,0:T(8,128)} %param.23) | copy-start | bytes 786436
  7.1 82.3 %collective-permute-start.1 = (f32[3,24,2,2048]{3,2,1,0:T(2,128)}, f32[3,24,2,2048]{3,2,1,0:T(2,128)}, u32[]{:S(2)}, u32[]{:S(2)}) collective-permute-start(f32[3,24,2,2048]{3,2,1,0:T(2,128)} %get-tuple-element.308), channel_id=1, source_target_pairs={{1,0},{2,1},{3,2},{4,3},{5,4},{6,5},{7,6},{8,7},{9,8},{10,9},{11,1... | collective-permute-start | bytes 3538952 | tf_op jit(solution)/shard_map/ppermute | solution.py:28
  10.0 79.4 %collective-permute-start = (f32[3,24,2,2048]{3,2,1,0:T(2,128)}, f32[3,24,2,2048]{3,2,1,0:T(2,128)}, u32[]{:S(2)}, u32[]{:S(2)}) collective-permute-start(f32[3,24,2,2048]{3,2,1,0:T(2,128)} %get-tuple-element.307), channel_id=1, source_target_pairs={{0,1},{1,2},{2,3},{3,4},{4,5},{5,6},{6,7},{7,8},{8,9},{9,10},{10,1... | collective-permute-start | bytes 3538952 | tf_op jit(solution)/shard_map/ppermute | solution.py:27
  15.4 58.7 %copy-start.10 = (s32[1,16]{1,0:T(1,128)S(1)}, s32[1,16]{1,0:T(1,128)}, u32[]{:S(2)}) copy-start(s32[1,16]{1,0:T(1,128)} %param.25) | copy-start | bytes 196
  75.3 14.2 %slice-start = ((s8[9437184]{0:T(1024)(128)(4,1)}), s8[4194304]{0:T(1024)(128)(4,1)S(1)}, s32[]{:S(2)}) async-start(s8[9437184]{0:T(1024)(128)(4,1)} %bitcast.180), calls=%async_computation | async-start | bytes 8388608
  75.4 14.3 %slice-start.1 = ((s8[9437184]{0:T(1024)(128)(4,1)}), s8[4194304]{0:T(1024)(128)(4,1)S(1)}, s32[]{:S(2)}) async-start(s8[9437184]{0:T(1024)(128)(4,1)} %bitcast.180), calls=%async_computation.1 | async-start | bytes 8388608
  75.4 15.1 %slice-start.2 = ((s8[9437184]{0:T(1024)(128)(4,1)}), s8[1048576]{0:T(1024)(128)(4,1)S(1)}, s32[]{:S(2)}) async-start(s8[9437184]{0:T(1024)(128)(4,1)} %bitcast.180), calls=%async_computation.2 | async-start | bytes 2097152
  94.4 5.0 %copy-start = (f32[3,24,20,2048]{3,2,1,0:T(8,128)}, f32[3,24,20,2048]{3,2,1,0:T(8,128)S(1)}, u32[]{:S(2)}) copy-start(f32[3,24,20,2048]{3,2,1,0:T(8,128)S(1)} %pad_maximum_fusion) | copy-start | bytes 35389444
  100.2 4.7 %collective-permute-start.2 = (f32[3,24,20,2]{1,3,2,0:T(2,128)S(1)}, f32[3,24,20,2]{1,3,2,0:T(2,128)S(1)}, u32[]{:S(2)}, u32[]{:S(2)}) collective-permute-start(f32[3,24,20,2]{1,3,2,0:T(2,128)S(1)} %copy.102), channel_id=1, source_target_pairs={{0,16},{16,0},{1,17},{17,1},{2,18},{18,2},{3,19},{19,3},{4,20},{20... | collective-permute-start | bytes 34568 | tf_op jit(solution)/shard_map/ppermute | solution.py:27
  102.1 4.5 %collective-permute-start.3 = (f32[3,24,20,2]{1,3,2,0:T(2,128)S(1)}, f32[3,24,20,2]{1,3,2,0:T(2,128)S(1)}, u32[]{:S(2)}, u32[]{:S(2)}) collective-permute-start(f32[3,24,20,2]{1,3,2,0:T(2,128)S(1)} %copy.103), channel_id=1, source_target_pairs={{16,0},{0,16},{17,1},{1,17},{18,2},{2,18},{19,3},{3,19},{20,4},{4,... | collective-permute-start | bytes 34568 | tf_op jit(solution)/shard_map/ppermute | solution.py:28
  136.5 15.5 %slice-start.3 = ((s8[9437184]{0:T(1024)(128)(4,1)}), s8[4194304]{0:T(1024)(128)(4,1)S(1)}, s32[]{:S(2)}) async-start(s8[9437184]{0:T(1024)(128)(4,1)} %bitcast.182), calls=%async_computation.3 | async-start | bytes 8388608
  136.5 15.5 %slice-start.4 = ((s8[9437184]{0:T(1024)(128)(4,1)}), s8[4194304]{0:T(1024)(128)(4,1)S(1)}, s32[]{:S(2)}) async-start(s8[9437184]{0:T(1024)(128)(4,1)} %bitcast.182), calls=%async_computation.4 | async-start | bytes 8388608
  136.5 15.5 %slice-start.5 = ((s8[9437184]{0:T(1024)(128)(4,1)}), s8[1048576]{0:T(1024)(128)(4,1)S(1)}, s32[]{:S(2)}) async-start(s8[9437184]{0:T(1024)(128)(4,1)} %bitcast.182), calls=%async_computation.5 | async-start | bytes 2097152
  136.5 15.6 %copy-start.1 = (f32[16,2048]{1,0:T(8,128)S(1)}, f32[16,2048]{1,0:T(8,128)}, u32[]{:S(2)}) copy-start(f32[16,2048]{1,0:T(8,128)} %param.17) | copy-start | bytes 393220
  136.5 15.6 %copy-start.3 = (f32[1,16,2048]{2,1,0:T(8,128)S(1)}, f32[1,16,2048]{2,1,0:T(8,128)}, u32[]{:S(2)}) copy-start(f32[1,16,2048]{2,1,0:T(8,128)} %get-tuple-element.298) | copy-start | bytes 393220
  136.5 15.6 %copy-start.4 = (f32[1,16,2048]{2,1,0:T(8,128)S(1)}, f32[1,16,2048]{2,1,0:T(8,128)}, u32[]{:S(2)}) copy-start(f32[1,16,2048]{2,1,0:T(8,128)} %get-tuple-element.299) | copy-start | bytes 393220
  192.2 15.6 %slice-start.6 = ((s8[5013504]{0:T(1024)(128)(4,1)}), s8[4194304]{0:T(1024)(128)(4,1)S(1)}, s32[]{:S(2)}) async-start(s8[5013504]{0:T(1024)(128)(4,1)} %bitcast.185), calls=%async_computation.6 | async-start | bytes 8388608
  192.2 15.6 %slice-start.7 = ((s8[5013504]{0:T(1024)(128)(4,1)}), s8[819200]{0:T(1024)(128)(4,1)S(1)}, s32[]{:S(2)}) async-start(s8[5013504]{0:T(1024)(128)(4,1)} %bitcast.185), calls=%async_computation.7 | async-start | bytes 1638400
  205.9 1.0 copy-start.5
where the time goes:
time: 221 us; the launch traced here: 218 us
  other arithmetic  135 us (61%)
  local copies, waits for them, and re-layouts  66.7 us (30%)
  starting transfers between devices  6.92 us (3%)
  loops' own time  5.91 us (3%)
    sub x2, other arithmetic, laplace(): padded[..., 1:-1, 2:] + padded[..., 1:-1, :-2] + padded[..., 2:, 1:-1]  46.9 us
    concatenate x1, local copies, waits for them, and re-layouts, padded_2(): x = jnp.concatenate([before, x, after], axis=dim)  18.3 us
    sub x256, other arithmetic, behind_diff(): lax.slice_in_dim(field, 1, length, axis=axis)  14.7 us
    slice x1, local copies, waits for them, and re-layouts, vertical(): lower = jnp.concatenate([field[1:], field[-1:]], axis=0)  14.1 us
    sub x1, other arithmetic, per_device(): north = mixed[1] - coriolis * ocean_state[0]  13.7 us
    div x64, other arithmetic, subcycle(): (mass * vel_y + sub_step * (force_y + wind_y + drag_coef * ocean_y - turn...  12.8 us
    mul x64, other arithmetic, subcycle(): stress_yy = 0.5 * (sigma_one - sigma_two)  12.7 us
    unnamed x58, local copies, waits for them, and re-layouts  11.5 us
  transfers between devices with their start and end apart: 4, of which 2 were waited for; matrix products, arithmetic and copies ran while one was open for 34% of the time, Pallas kernels for 0%

commit v1 on v0

v1 whole, which is shorter than its diff:
```python
import jax
import jax.numpy as jnp
from jax import lax
from jax.experimental import pallas as pl
from jax.experimental.pallas import tpu as pltpu
from jax.sharding import PartitionSpec as P

BY = 16
BX = 128
SUBCYCLES = 64
UNROLL = 4
LANES = 128
HALF = 8

KV_MIX = 0.2
RELAX = 0.5
SUB_STEP = 0.3
TURNING = 0.3
CORIOLIS = 0.2

DECAY = 1.0 / (1.0 + RELAX)
VMEM_BYTES = 48 * 1024 * 1024

HBM = pltpu.HBM
VMEM = pltpu.VMEM
SMEM = pltpu.SMEM


def spec(space):
    return pl.BlockSpec(memory_space=space)


def cost(flops, nbytes):
    return pl.CostEstimate(flops=flops, bytes_accessed=nbytes, transcendentals=0)


def lane_index(rows):
    return lax.broadcasted_iota(jnp.int32, (rows, LANES), 1)


def pack_kernel(x, first, last, cols, corners, left, right, cleft, cright, row_sem, col_sem):
    fields, levels, rows, width = x.shape
    edge_rows = (0, rows - 1)
    copies = []
    col_copies = [
        pltpu.make_async_copy(x.at[:, :, :, 0:LANES], left, col_sem.at[0]),
        pltpu.make_async_copy(x.at[:, :, :, width - LANES : width], right, col_sem.at[1]),
    ]
    for f in range(fields):
        for j in range(2):
            index = f * 2 + j
            copies.append(
                pltpu.make_async_copy(x.at[f, :, j, :], first.at[f, j], row_sem.at[0, index])
            )
            copies.append(
                pltpu.make_async_copy(
                    x.at[f, :, rows - 2 + j, :], last.at[f, j], row_sem.at[1, index]
                )
            )
            row = edge_rows[j]
            col_copies.append(
                pltpu.make_async_copy(
                    x.at[f, :, row, 0:LANES], cleft.at[j, f], col_sem.at[2 + 2 * index]
                )
            )
            col_copies.append(
                pltpu.make_async_copy(
                    x.at[f, :, row, width - LANES : width],
                    cright.at[j, f],
                    col_sem.at[3 + 2 * index],
                )
            )
    for copy in copies + col_copies:
        copy.start()
    for copy in col_copies:
        copy.wait()
    lane = lane_index(rows)
    for f in range(fields):
        packed = jnp.zeros((rows, LANES), jnp.float32)
        for k in range(levels):
            edge = jnp.where(lane < LANES // 2, left[f, k], right[f, k])
            if k:
                edge = pltpu.roll(edge, 4 * k, axis=1)
            mine = ((lane + (2 - 4 * k)) & (LANES - 1)) < 4
            packed = jnp.where(mine, edge, packed)
        cols[f] = packed
        for j in range(2):
            corners[j, f] = jnp.where(
                lane_index(levels) < LANES // 2, cleft[j, f], cright[j, f]
            )
    for copy in copies:
        copy.wait()


def pack(ocean_state):
    fields, levels, rows, width = ocean_state.shape
    f32 = jnp.float32
    return pl.pallas_call(
        pack_kernel,
        name="pack_edges",
        out_shape=(
            jax.ShapeDtypeStruct((fields, 2, levels, width), f32),
            jax.ShapeDtypeStruct((fields, 2, levels, width), f32),
            jax.ShapeDtypeStruct((fields, rows, LANES), f32),
            jax.ShapeDtypeStruct((2, fields, levels, LANES), f32),
        ),
        in_specs=[spec(HBM)],
        out_specs=(spec(HBM), spec(HBM), spec(VMEM), spec(VMEM)),
        scratch_shapes=[
            pltpu.VMEM((fields, levels, rows, LANES), f32),
            pltpu.VMEM((fields, levels, rows, LANES), f32),
            pltpu.VMEM((2, fields, levels, LANES), f32),
            pltpu.VMEM((2, fields, levels, LANES), f32),
            pltpu.SemaphoreType.DMA((2, 2 * fields)),
            pltpu.SemaphoreType.DMA((2 + 4 * fields,)),
        ],
        compiler_params=pltpu.CompilerParams(vmem_limit_bytes=VMEM_BYTES),
        cost_estimate=cost(0, 4 * 2 * 4 * fields * levels * width),
    )(ocean_state)


def ice_kernel(
    count,
    listed,
    state,
    strength,
    mass,
    fraction,
    wind,
    surface,
    ice_out,
    stress_out,
    covered,
    su,
    sv,
    sx,
    sy,
    sxy,
    cp,
    cq,
    ca,
    cb,
    gx,
    gy,
):
    rows, width = mass.shape
    blocks = width // BX
    groups = blocks // HALF
    area = rows * HALF

    for s in range(blocks):
        covered[listed[0, s]] = jnp.where(s < count[0], 1, 0)

    def place(block):
        return pl.ds((block // HALF) * area + block % HALF, rows, stride=HALF)

    for b in range(blocks):
        at = slice(b * BX, (b + 1) * BX)
        to = place(b)
        m = mass[:, at]
        inverse = 1.0 / (m + SUB_STEP)
        push = SUB_STEP * inverse
        p = RELAX * strength[:, at]
        su[to, :] = state[0, :, at]
        sv[to, :] = state[1, :, at]
        sx[to, :] = state[2, :, at] + p
        sy[to, :] = state[3, :, at] + p
        sxy[to, :] = state[4, :, at]
        cp[to, :] = p
        cq[to, :] = p * (0.625 * DECAY / 1.25**0.5)
        ca[to, :] = m * inverse
        cb[to, :] = push
        gx[to, :] = wind[0, :, at] + surface[0, 0, :, at]
        gy[to, :] = wind[1, :, at] + surface[1, 0, :, at]

    lane = lane_index(HALF)
    final = lane == LANES - 1
    initial = lane == 0

    def ahead(q):
        return jnp.where(final, 0.0, pltpu.roll(q, LANES - 1, axis=1) - q)

    def behind(q):
        return q - jnp.where(initial, 0.0, pltpu.roll(q, 1, axis=1))

    def vec(g, y):
        return pl.ds(g * area + y * HALF, HALF)

    for g in range(groups):
        for y in range(rows):
            i = vec(g, y)
            p = cp[i, :]
            down = p if y == 0 else p - cp[vec(g, y - 1), :]
            gx[i, :] = cb[i, :] * (gx[i, :] - behind(p))
            gy[i, :] = cb[i, :] * (gy[i, :] - down)

    def sweep(step, carry):
        for _ in range(UNROLL):
            now = [(su[vec(g, 0), :], sv[vec(g, 0), :]) for g in range(groups)]
            above = [None] * groups
            for y in range(rows):
                for g in range(groups):
                    i = vec(g, y)
                    u, v = now[g]
                    ux = ahead(u)
                    shear = ahead(v)
                    if y < rows - 1:
                        j = vec(g, y + 1)
                        un, vn = su[j, :], sv[j, :]
                        now[g] = (un, vn)
                        vy = vn - v
                        shear = shear + (un - u)
                        a = ux + 0.6 * vy
                        b = 0.6 * ux + vy
                        d = ux * a + vy * b
                    else:
                        a = ux
                        b = 0.6 * ux
                        d = ux * a
                    small = 0.2 * shear
                    q = cq[i, :] * lax.rsqrt(d + (shear * small + 0.2))
                    xx = DECAY * sx[i, :] + q * a
                    yy = DECAY * sy[i, :] + q * b
                    xy = DECAY * sxy[i, :] + q * small
                    sx[i, :] = xx
                    sy[i, :] = yy
                    sxy[i, :] = xy
                    fx = behind(xx)
                    fy = behind(xy)
                    if y:
                        fx = fx + (xy - above[g][0])
                        fy = fy + (yy - above[g][1])
                    else:
                        fx = fx + xy
                        fy = fy + yy
                    above[g] = (xy, yy)
                    a0 = ca[i, :]
                    b0 = cb[i, :]
                    su[i, :] = a0 * (u + TURNING * SUB_STEP * v) + (b0 * fx + gx[i, :])
                    sv[i, :] = a0 * (v - TURNING * SUB_STEP * u) + (b0 * fy + gy[i, :])
        return carry

    lax.fori_loop(0, SUBCYCLES // UNROLL, sweep, 0)

    for b in range(blocks):
        at = slice(b * BX, (b + 1) * BX)
        fr = place(b)
        keep = covered[b] == 1
        u = su[fr, :]
        v = sv[fr, :]
        p = cp[fr, :]
        ice_out[0, :, at] = jnp.where(keep, u, state[0, :, at])
        ice_out[1, :, at] = jnp.where(keep, v, state[1, :, at])
        ice_out[2, :, at] = jnp.where(keep, sx[fr, :] - p, state[2, :, at])
        ice_out[3, :, at] = jnp.where(keep, sy[fr, :] - p, state[3, :, at])
        ice_out[4, :, at] = jnp.where(keep, sxy[fr, :], state[4, :, at])
        part = fraction[:, at]
        for d, vel in enumerate((u, v)):
            w = wind[d, :, at]
            merged = part * (vel - surface[d, 0, :, at]) + (1.0 - part) * w
            stress_out[d, :, at] = jnp.where(keep, merged, w)


def ice(ice_state, strength, ice_mass, ice_fraction, wind_stress, ice_count, ice_list, surface):
    rows, width = ice_mass.shape
    f32 = jnp.float32
    cells = (rows * width // BX, BX)
    return pl.pallas_call(
        ice_kernel,
        name="ice_subcycles",
        out_shape=(
            jax.ShapeDtypeStruct(ice_state.shape, f32),
            jax.ShapeDtypeStruct(wind_stress.shape, f32),
        ),
        in_specs=[spec(SMEM)] * 2 + [spec(VMEM)] * 6,
        out_specs=(spec(VMEM), spec(VMEM)),
        scratch_shapes=[pltpu.SMEM((width // BX,), jnp.int32)]
        + [pltpu.VMEM(cells, f32)] * 11,
        compiler_params=pltpu.CompilerParams(vmem_limit_bytes=VMEM_BYTES),
        cost_estimate=cost(SUBCYCLES * 50 * rows * width, 4 * 22 * rows * width),
    )(ice_count, ice_list, ice_state, strength, ice_mass, ice_fraction, wind_stress, surface)


def main_kernel(x_hbm, cols, bih, prev, cor, out_hbm, x, out, in_sem, out_sem):
    fields, levels, rows, width = x.shape
    tiles = width // LANES

    def fetch(k):
        return pltpu.make_async_copy(x_hbm.at[:, k], x.at[:, k], in_sem.at[k])

    def store(k):
        return pltpu.make_async_copy(out.at[:, k], out_hbm.at[:, k], out_sem.at[k])

    for k in range(levels):
        fetch(k).start()

    row = lax.broadcasted_iota(jnp.int32, (HALF, LANES), 0)
    lane = lane_index(HALF)
    top, bottom = row == 0, row == HALF - 1
    initial, final = lane == 0, lane == LANES - 1

    def down(pair):
        ra, rb = (pltpu.roll(h, 1, axis=0) for h in pair)
        return (jnp.where(top, 0.0, ra), jnp.where(top, ra, rb))

    def up(pair):
        ra, rb = (pltpu.roll(h, HALF - 1, axis=0) for h in pair)
        return (jnp.where(bottom, rb, ra), jnp.where(bottom, 0.0, rb))

    def rolled(pair):
        return tuple(
            (pltpu.roll(h, 1, axis=1), pltpu.roll(h, LANES - 1, axis=1)) for h in pair
        )

    def horizontal(west, here, east, centre):
        return tuple(
            jnp.where(initial, west[h][0], here[h][0])
            + jnp.where(final, east[h][1], here[h][1])
            - 4.0 * centre[h]
            for h in range(2)
        )

    def both(ref, *lead, at):
        return (ref[(*lead, slice(0, HALF), at)], ref[(*lead, slice(HALF, rows), at)])

    fetch(0).wait()

    def level(k, carry):
        @pl.when(k + 1 < levels)
        def _():
            fetch(k + 1).wait()

        before = jnp.maximum(k - 1, 0)
        after = jnp.minimum(k + 1, levels - 1)
        shift = lax.rem(LANES - 4 * k, LANES)
        for f in range(fields):
            edge_all = pltpu.roll(cols[f], shift, axis=1)
            edge = (edge_all[0:HALF], edge_all[HALF:rows])

            def load(c):
                if c < 0 or c >= tiles:
                    return edge
                return both(x, f, k, at=slice(c * LANES, (c + 1) * LANES))

            raw = {-1: edge, 0: load(0)}
            turned = {c: rolled(raw[c]) for c in (-1, 0)}
            lastt = load(tiles - 1)
            last_turned = rolled(lastt)
            first_pass = {-1: horizontal(last_turned, turned[-1], turned[0], raw[-1])}
            first_turned = {-1: rolled(first_pass[-1])}

            def advance(c):
                if c + 1 == tiles:
                    raw[c + 1], turned[c + 1] = raw[-1], turned[-1]
                elif c + 1 == tiles - 1:
                    raw[c + 1], turned[c + 1] = lastt, last_turned
                else:
                    raw[c + 1] = load(c + 1)
                    turned[c + 1] = rolled(raw[c + 1])
                if c == tiles:
                    return
                first_pass[c] = horizontal(turned[c - 1], turned[c], turned[c + 1], raw[c])
                first_turned[c] = rolled(first_pass[c])

            advance(0)
            for c in range(tiles):
                if c + 1 < tiles:
                    advance(c + 1)
                else:
                    first_turned[tiles] = first_turned[-1]
                at = slice(c * LANES, (c + 1) * LANES)
                q = raw[c]
                g = first_pass[c]
                second = horizontal(
                    first_turned[c - 1], first_turned[c], first_turned[c + 1], g
                )
                qd, qu = down(q), up(q)
                w = tuple((g[h] + g[h]) + (qd[h] + qu[h]) for h in range(2))
                wd, wu = down(w), up(w)
                coef = both(bih, at=at)
                qb = both(x, f, before, at=at)
                qa = both(x, f, after, at=at)
                for h in range(2):
                    edge_row = top if h == 0 else bottom
                    lap = second[h] + (wd[h] + wu[h]) + jnp.where(edge_row, q[h], 0.0)
                    res = (
                        (1.0 - 2.0 * KV_MIX) * q[h]
                        + KV_MIX * (qb[h] + qa[h])
                        - coef[h] * lap
                    )
                    rs = slice(h * HALF, (h + 1) * HALF)
                    if f == 0:
                        res = res + cor[rs, :] * x[1, k, rs, at]
                    elif f == 1:
                        res = res - cor[rs, :] * x[0, k, rs, at]
                    out[f, k, rs, at] = res

        @pl.when(k == 0)
        def _():
            for d in range(2):
                out[d, 0] = out[d, 0] + prev[d]

        store(k).start()
        return carry

    lax.fori_loop(0, levels, level, 0)
    for k in range(levels):
        store(k).wait()


def ocean(ocean_state, cols, biharmonic, prev_stress, coriolis):
    fields, levels, rows, width = ocean_state.shape
    f32 = jnp.float32
    return pl.pallas_call(
        main_kernel,
        name="ocean_tile",
        out_shape=jax.ShapeDtypeStruct(ocean_state.shape, f32),
        in_specs=[spec(HBM)] + [spec(VMEM)] * 4,
        out_specs=spec(HBM),
        scratch_shapes=[
            pltpu.VMEM(ocean_state.shape, f32),
            pltpu.VMEM(ocean_state.shape, f32),
            pltpu.SemaphoreType.DMA((levels,)),
            pltpu.SemaphoreType.DMA((levels,)),
        ],
        compiler_params=pltpu.CompilerParams(vmem_limit_bytes=VMEM_BYTES),
        cost_estimate=cost(30 * ocean_state.size, 8 * ocean_state.size),
    )(ocean_state, cols, biharmonic, prev_stress, coriolis)


def fix_kernel(base, above, below, cabove, cbelow, bih, out, ha, hb, oa, ob, in_sem, out_sem):
    fields, _, levels, width = ha.shape
    rows = base.shape[2]
    tiles = width // LANES
    fetches, stores = [], []
    for f in range(fields):
        mine, back = [], []
        for j in range(2):
            for side, (buf, first) in enumerate(((oa, 0), (ob, rows - 2))):
                n = (f * 2 + j) * 2 + side
                mine.append(
                    pltpu.make_async_copy(base.at[f, :, first + j, :], buf.at[f, j], in_sem.at[n])
                )
                back.append(
                    pltpu.make_async_copy(buf.at[f, j], out.at[f, :, first + j, :], out_sem.at[n])
                )
        n = 4 * fields + 2 * f
        mine.append(pltpu.make_async_copy(above.at[f], ha.at[f], in_sem.at[n]))
        mine.append(pltpu.make_async_copy(below.at[f], hb.at[f], in_sem.at[n + 1]))
        fetches.append(mine)
        stores.append(back)
        for copy in mine:
            copy.start()

    lane = lane_index(HALF)
    initial, final = lane == 0, lane == LANES - 1

    for f in range(fields):
        for copy in fetches[f]:
            copy.wait()
        for halo, corner, near, far, buf, n1, n2 in (
            (ha, cabove, 1, 0, oa, 0, 1),
            (hb, cbelow, 0, 1, ob, 1, 0),
        ):
            r1 = n1 if buf is oa else rows - 2 + n1
            r2 = n2 if buf is oa else rows - 2 + n2

            def octet(s, carry):
                ks = pl.ds(pl.multiple_of(s * HALF, HALF), HALF)
                ext = corner[f, ks, :]
                ext_e, ext_w = pltpu.roll(ext, 1, axis=1), pltpu.roll(ext, LANES - 1, axis=1)
                cur = halo[f, near, ks, 0:LANES]
                west = ext_e
                cur_e, cur_w = pltpu.roll(cur, 1, axis=1), pltpu.roll(cur, LANES - 1, axis=1)
                for c in range(tiles):
                    at = slice(c * LANES, (c + 1) * LANES)
                    if c + 1 < tiles:
                        nxt = halo[f, near, ks, (c + 1) * LANES : (c + 2) * LANES]
                        nxt_e = pltpu.roll(nxt, 1, axis=1)
                        nxt_w = pltpu.roll(nxt, LANES - 1, axis=1)
                    else:
                        nxt, nxt_e, nxt_w = ext, ext_e, ext_w
                    around = jnp.where(initial, west, cur_e) + jnp.where(final, nxt_w, cur_w)
                    lap = halo[f, far, ks, at] + 2.0 * around - 8.0 * cur
                    buf[f, n1, ks, at] = buf[f, n1, ks, at] - bih[r1 : r1 + 1, at] * lap
                    buf[f, n2, ks, at] = buf[f, n2, ks, at] - bih[r2 : r2 + 1, at] * cur
                    west = cur_e
                    cur, cur_e, cur_w = nxt, nxt_e, nxt_w
                return carry

            lax.fori_loop(0, levels // HALF, octet, 0)
        for copy in stores[f]:
            copy.start()
    for back in stores:
        for copy in back:
            copy.wait()


def fix(base, above, below, cabove, cbelow, biharmonic):
    fields, levels, rows, width = base.shape
    f32 = jnp.float32
    edge = pltpu.VMEM((fields, 2, levels, width), f32)
    return pl.pallas_call(
        fix_kernel,
        name="ocean_edges",
        out_shape=jax.ShapeDtypeStruct(base.shape, f32),
        in_specs=[spec(HBM)] * 3 + [spec(VMEM)] * 3,
        out_specs=spec(HBM),
        input_output_aliases={0: 0},
        scratch_shapes=[
            edge,
            edge,
            edge,
            edge,
            pltpu.SemaphoreType.DMA((6 * fields,)),
            pltpu.SemaphoreType.DMA((4 * fields,)),
        ],
        compiler_params=pltpu.CompilerParams(vmem_limit_bytes=VMEM_BYTES),
        cost_estimate=cost(0, 3 * 4 * 4 * fields * levels * width),
    )(base, above, below, cabove, cbelow, biharmonic)


def per_device(
    ocean_state,
    biharmonic,
    prev_stress,
    ice_state,
    strength,
    ice_mass,
    ice_fraction,
    wind_stress,
    ice_count,
    ice_list,
):
    tile_rows = ocean_state.shape[2]
    n_tile = lax.axis_size("tile")
    n_grp = lax.axis_size("grp")

    first, last, cols, corners = pack(ocean_state)

    def shift(value, tile_step, grp_step):
        pairs = []
        for g in range(n_grp):
            for t in range(n_tile):
                if 0 <= t + tile_step < n_tile:
                    target = (g + grp_step) % n_grp
                    pairs.append((g * n_tile + t, target * n_tile + t + tile_step))
        return lax.ppermute(value, ("grp", "tile"), pairs)

    lane = jnp.arange(LANES)

    def around(value, tile_step, eastern):
        west = shift(value, tile_step, 1)
        if n_grp == 2:
            return west
        return jnp.where(eastern, shift(value, tile_step, -1), west)

    above = shift(last, 1, 0)
    below = shift(first, -1, 0)
    cols = around(cols, 0, lane % 4 < 2)
    cabove = around(corners[1], 1, lane < LANES // 2)
    cbelow = around(corners[0], -1, lane < LANES // 2)

    ice_in = (ice_state, strength, ice_mass, ice_fraction, wind_stress, ice_count, ice_list)
    surface = ocean_state[0:2, 0:1]
    ice_out, stress_out = ice(*ice_in, surface)

    rows = (lax.axis_index("tile") * tile_rows + jnp.arange(tile_rows)).astype(jnp.float32) + 0.5
    coriolis = CORIOLIS * (2.0 * rows / (tile_rows * n_tile) - 1.0)
    coriolis = jnp.broadcast_to(coriolis[:, None], (tile_rows, LANES))
    base = ocean(ocean_state, cols, biharmonic, prev_stress, coriolis)
    ocean_out = fix(base, above, below, cabove, cbelow, biharmonic)
    return (ocean_out, ice_out, stress_out)


def solution(mesh):
    placed = (
        P(None, None, "tile", "grp"),
        P("tile", "grp"),
        P(None, "tile", "grp"),
        P(None, "tile", "grp"),
        P("tile", "grp"),
        P("tile", "grp"),
        P("tile", "grp"),
        P(None, "tile", "grp"),
        P(("grp", "tile")),
        P(("grp", "tile"), None),
    )
    return jax.shard_map(
        per_device,
        mesh=mesh,
        in_specs=placed,
        out_specs=(P(None, None, "tile", "grp"), P(None, "tile", "grp"), P(None, "tile", "grp")),
        check_vma=False,
    )
```

time: 221 us -> 203 us (0.919); the launches traced: 218 us -> 203 us
  Pallas kernels: 0 us -> 181 us
  other arithmetic: 135 us -> 0.01 us
  local copies, waits for them, and re-layouts: 66.7 us -> 4.44 us
  starting transfers between devices: 6.92 us -> 15.5 us
  loops' own time: 5.91 us -> 0 us
    pallas_call x0 -> x4, Pallas kernels: none -> 181 us  [the longest x1 73.4 us: pack(): pl.pallas_call(pack_kernel, name='pack_edges', out_shape=(jax.ShapeDtypeS...]
    sub x387 -> x0, other arithmetic: 85.7 us -> none  [the longest x2 46.9 us: laplace(): padded[..., 1:-1, 2:] + padded[..., 1:-1, :-2] + padded[..., 2:, 1:-1]]
    slice x137 -> x1, local copies, waits for them, and re-layouts: 24.4 us -> 0.97 us  [per_device(): surface = ocean_state[0:2, 0:1]]
    concatenate x1 -> x0, local copies, waits for them, and re-layouts: 18.3 us -> none  [padded_2(): x = jnp.concatenate([before, x, after], axis=dim)]
    mul x129 -> x1, other arithmetic: 14 us -> 0.01 us  [per_device(): coriolis = CORIOLIS * (2.0 * rows / (tile_rows * n_tile) - 1.0)]
    div x64 -> x0, other arithmetic: 12.8 us -> none  [subcycle(): (mass * vel_y + sub_step * (force_y + wind_y + drag_coef * ocean_y - turn...]
    another operation x3 -> x0, other arithmetic: 10.6 us -> none  [the longest x2 10.5 us: per_device(): ocean_out = jnp.stack([east, north, mixed[2]])]
    squeeze x1, local copies, waits for them, and re-layouts: 11.1 us -> 0.63 us  [per_device(): cbelow = around(corners[0], -1, lane < LANES // 2)]
  transfers between devices with their start and end apart: 4 -> 5, of which waited for: 2 -> 0; matrix products, arithmetic and copies ran while one was open for 34% -> 1% of each run, Pallas kernels for 0% -> 51%
where the time goes in v1:
time: 203 us
  Pallas kernels  181 us (89%)
  starting transfers between devices  15.5 us (8%)
  local copies, waits for them, and re-layouts  4.44 us (2%)
    pallas_call x1, Pallas kernels, pack(): pl.pallas_call(pack_kernel, name='pack_edges', out_shape=(jax.ShapeDtypeS...  73.4 us
    pallas_call x1, Pallas kernels, ocean(): pl.pallas_call(main_kernel, name='ocean_tile', out_shape=jax.ShapeDtypeSt...  64.6 us
    pallas_call x1, Pallas kernels, ice(): pl.pallas_call(ice_kernel, name='ice_subcycles', out_shape=(jax.ShapeDtyp...  37.8 us
    ppermute x5, starting transfers between devices, shift(): return lax.ppermute(value, ('grp', 'tile'), pairs)  15.5 us
    pallas_call x1, Pallas kernels, fix(): pl.pallas_call(fix_kernel, name='ocean_edges', out_shape=jax.ShapeDtypeSt...  5.36 us
  transfers between devices with their start and end apart: 5, of which 0 were waited for; matrix products, arithmetic and copies ran while one was open for 1% of the time, Pallas kernels for 51%

profile of v1, /device:TPU:24, one launch (start us, length us, event | category | flops | bytes accessed | tf_op | source)
XLA Modules:
  0.0 202.6 jit_solution(13638964940524412890)
XLA Ops:
  0.6 0.0 copy-start
  0.6 0.0 copy-start.4
  0.7 0.0 copy-start.7
  0.7 73.4 %pack_edges.1 = (f32[3,2,24,2048]{3,2,1,0:T(8,128)}, f32[3,2,24,2048]{3,2,1,0:T(8,128)}, f32[3,16,128]{2,1,0:T(8,128)}, f32[2,3,24,128]{3,2,1,0:T(8,128)S(1)}) custom-call(f32[3,24,16,2048]{3,2,1,0:T(8,128)} %x_hbm.1), custom_call_target="tpu_custom_call" | custom-call | bytes 4718592 | tf_op jit(solution)/shard_map/pack_edges/pallas_call | solution.py:98
  74.1 0.0 copy-start.1
  74.1 0.0 copy-start.2
  74.1 2.1 %collective-permute-start.1 = (f32[3,2,24,2048]{3,2,1,0:T(8,128)}, f32[3,2,24,2048]{3,2,1,0:T(8,128)S(1)}, u32[]{:S(2)}, u32[]{:S(2)}) collective-permute-start(f32[3,2,24,2048]{3,2,1,0:T(8,128)} %get-tuple-element.10), channel_id=1, source_target_pairs={{0,1},{1,2},{2,3},{3,4},{4,5},{5,6},{6,7},{7,8},{8,9},{9,10},{10,1... | collective-permute-start | bytes 3538952 | tf_op jit(solution)/shard_map/ppermute | solution.py:548
  76.2 4.5 %collective-permute-start.2 = (f32[3,2,24,2048]{3,2,1,0:T(8,128)}, f32[3,2,24,2048]{3,2,1,0:T(8,128)S(1)}, u32[]{:S(2)}, u32[]{:S(2)}) collective-permute-start(f32[3,2,24,2048]{3,2,1,0:T(8,128)} %get-tuple-element.11), channel_id=1, source_target_pairs={{1,0},{2,1},{3,2},{4,3},{5,4},{6,5},{7,6},{8,7},{9,8},{10,9},{11,1... | collective-permute-start | bytes 3538952 | tf_op jit(solution)/shard_map/ppermute | solution.py:548
  80.7 0.6 slice_bitcast_fusion
  81.3 2.0 collective-permute-start.3
  83.4 5.4 %collective-permute-start.4 = (f32[3,24,128]{2,1,0:T(8,128)}, f32[3,24,128]{2,1,0:T(8,128)}, u32[]{:S(2)}, u32[]{:S(2)}) collective-permute-start(f32[3,24,128]{2,1,0:T(8,128)} %get-tuple-element.15), channel_id=1, source_target_pairs={{1,16},{2,17},{3,18},{4,19},{5,20},{6,21},{7,22},{8,23},{9,24},{10... | collective-permute-start | bytes 110600 | tf_op jit(solution)/shard_map/ppermute | solution.py:548
  88.7 1.6 collective-permute-start
  90.3 1.0 slice.11.surface
  91.9 0.0 copy-done
  91.9 0.0 copy-done.4
  91.9 0.0 copy-done.7
  91.9 0.0 copy-start.3
  91.9 0.9 copy-done.3
  92.9 0.9 copy-done.5
  93.8 0.0 copy-start.6
  93.8 0.9 copy-done.6
  94.7 37.8 %ice_subcycles.1 = (f32[5,16,2048]{2,1,0:T(8,128)}, f32[2,16,2048]{2,1,0:T(8,128)}) custom-call(s32[1]{0:T(128)S(6)} %copy.15.count, s32[1,16]{1,0:T(1,128)S(1)} %copy-done.7, f32[5,16,2048]{2,1,0:T(8,128)S(1)} %copy-done, f32[16,2048]{1,0:T(8,128)S(1)} %copy-done.4, f32[16,2048]{1,0:T(8,128)S(1)} %copy-done.5, f32[16,2048]{1,0:T(8,128)S(1)} %copy-done.6, ...), custom_call_target="tpu_custom_call" | custom-call | flops 104857600 | bytes 2883584 | tf_op jit(solution)/shard_map/ice_subcycles/pallas_call | solution.py:268
  132.5 0.0 collective-permute-done.cols
  132.5 0.1 broadcast_in_dim.2.cor
  132.6 0.0 copy-done.1
  132.6 0.0 copy-done.2
  132.6 64.6 %ocean_tile.1.base = f32[3,24,16,2048]{3,2,1,0:T(8,128)} custom-call(f32[3,24,16,2048]{3,2,1,0:T(8,128)} %x_hbm.1, f32[3,16,128]{2,1,0:T(8,128)} %collective-permute-done.cols, f32[16,2048]{1,0:T(8,128)S(1)} %copy-done.1, f32[2,16,2048]{2,1,0:T(8,128)S(1)} %copy-done.2, f32[16,128]{1,0:T(8,128)S(1)} %broadcast_in_dim.2.cor), custom_call_target="tpu_custom_call" | custom-call | flops 70778880 | bytes 18874368 | tf_op jit(solution)/shard_map/ocean_tile/pallas_call | solution.py:414
  197.2 0.0 collective-permute-done.3.cabove
  197.2 0.0 collective-permute-done.4.cbelow
  197.3 0.0 collective-permute-done.1.above
  197.3 0.0 collective-permute-done.2.below
  197.3 5.4 %ocean_edges.1 = f32[3,24,16,2048]{3,2,1,0:T(8,128)} custom-call(f32[3,24,16,2048]{3,2,1,0:T(8,128)} %ocean_tile.1.base, f32[3,2,24,2048]{3,2,1,0:T(8,128)S(1)} %collective-permute-done.1.above, f32[3,2,24,2048]{3,2,1,0:T(8,128)S(1)} %collective-permute-done.2.below, f32[3,24,128]{2,1,0:T(8,128)} %collective-permute-done.3.cabove, ...), custom_call_target="tpu_custom_call", output_to_operand_aliasing={{}: (0, {})} | custom-call | bytes 7077888 | tf_op jit(solution)/shard_map/ocean_edges/pallas_call | solution.py:503
  (2 shorter events, 0.0 us)
Async XLA Ops:
  0.6 91.3 %copy-start = (f32[5,16,2048]{2,1,0:T(8,128)S(1)}, f32[5,16,2048]{2,1,0:T(8,128)}, u32[]{:S(2)}) copy-start(f32[5,16,2048]{2,1,0:T(8,128)} %state.1) | copy-start | bytes 1966084
  0.6 91.3 %copy-start.4 = (f32[16,2048]{1,0:T(8,128)S(1)}, f32[16,2048]{1,0:T(8,128)}, u32[]{:S(2)}) copy-start(f32[16,2048]{1,0:T(8,128)} %strength.1) | copy-start | bytes 393220
  0.7 91.3 %copy-start.7 = (s32[1,16]{1,0:T(1,128)S(1)}, s32[1,16]{1,0:T(1,128)}, u32[]{:S(2)}) copy-start(s32[1,16]{1,0:T(1,128)} %listed.1) | copy-start | bytes 196
  74.1 58.5 %copy-start.1 = (f32[16,2048]{1,0:T(8,128)S(1)}, f32[16,2048]{1,0:T(8,128)}, u32[]{:S(2)}) copy-start(f32[16,2048]{1,0:T(8,128)} %bih.3) | copy-start | bytes 393220
  74.1 58.5 %copy-start.2 = (f32[2,16,2048]{2,1,0:T(8,128)S(1)}, f32[2,16,2048]{2,1,0:T(8,128)}, u32[]{:S(2)}) copy-start(f32[2,16,2048]{2,1,0:T(8,128)} %prev.1) | copy-start | bytes 786436
  74.1 123.2 %collective-permute-start.1 = (f32[3,2,24,2048]{3,2,1,0:T(8,128)}, f32[3,2,24,2048]{3,2,1,0:T(8,128)S(1)}, u32[]{:S(2)}, u32[]{:S(2)}) collective-permute-start(f32[3,2,24,2048]{3,2,1,0:T(8,128)} %get-tuple-element.10), channel_id=1, source_target_pairs={{0,1},{1,2},{2,3},{3,4},{4,5},{5,6},{6,7},{7,8},{8,9},{9,10},{10,1... | collective-permute-start | bytes 3538952 | tf_op jit(solution)/shard_map/ppermute | solution.py:548
  76.2 121.1 %collective-permute-start.2 = (f32[3,2,24,2048]{3,2,1,0:T(8,128)}, f32[3,2,24,2048]{3,2,1,0:T(8,128)S(1)}, u32[]{:S(2)}, u32[]{:S(2)}) collective-permute-start(f32[3,2,24,2048]{3,2,1,0:T(8,128)} %get-tuple-element.11), channel_id=1, source_target_pairs={{1,0},{2,1},{3,2},{4,3},{5,4},{6,5},{7,6},{8,7},{9,8},{10,9},{11,1... | collective-permute-start | bytes 3538952 | tf_op jit(solution)/shard_map/ppermute | solution.py:548
  81.3 115.9 %collective-permute-start.3 = (f32[3,24,128]{2,1,0:T(8,128)}, f32[3,24,128]{2,1,0:T(8,128)}, u32[]{:S(2)}, u32[]{:S(2)}) collective-permute-start(f32[3,24,128]{2,1,0:T(8,128)} %get-tuple-element.16), channel_id=1, source_target_pairs={{0,17},{1,18},{2,19},{3,20},{4,21},{5,22},{6,23},{7,24},{8,25},{9,... | collective-permute-start | bytes 110600 | tf_op jit(solution)/shard_map/ppermute | solution.py:548
  83.4 113.9 %collective-permute-start.4 = (f32[3,24,128]{2,1,0:T(8,128)}, f32[3,24,128]{2,1,0:T(8,128)}, u32[]{:S(2)}, u32[]{:S(2)}) collective-permute-start(f32[3,24,128]{2,1,0:T(8,128)} %get-tuple-element.15), channel_id=1, source_target_pairs={{1,16},{2,17},{3,18},{4,19},{5,20},{6,21},{7,22},{8,23},{9,24},{10... | collective-permute-start | bytes 110600 | tf_op jit(solution)/shard_map/ppermute | solution.py:548
  88.7 43.8 %collective-permute-start = (f32[3,16,128]{2,1,0:T(8,128)}, f32[3,16,128]{2,1,0:T(8,128)}, u32[]{:S(2)}, u32[]{:S(2)}) collective-permute-start(f32[3,16,128]{2,1,0:T(8,128)} %get-tuple-element.9), channel_id=1, source_target_pairs={{0,16},{1,17},{2,18},{3,19},{4,20},{5,21},{6,22},{7,23},{8,24},{9,... | collective-permute-start | bytes 73736 | tf_op jit(solution)/shard_map/ppermute | solution.py:548
  91.9 1.0 copy-start.3
  92.9 0.9 copy-start.5
  93.8 0.9 copy-start.6

commit v2 on v1

v2 whole, which is shorter than its diff:
```python
import jax
import jax.numpy as jnp
import numpy as np
from jax import lax
from jax.experimental import pallas as pl
from jax.experimental.pallas import tpu as pltpu
from jax.sharding import PartitionSpec as P

BY = 16
BX = 128
SUBCYCLES = 64
UNROLL = 4
LANES = 128
HALF = 8

KV_MIX = 0.2
RELAX = 0.5
SUB_STEP = 0.3
TURNING = 0.3
CORIOLIS = 0.2

DECAY = 1.0 / (1.0 + RELAX)
VMEM_BYTES = 48 * 1024 * 1024

HBM = pltpu.HBM
VMEM = pltpu.VMEM
SMEM = pltpu.SMEM


def spec(space):
    return pl.BlockSpec(memory_space=space)


def cost(flops, nbytes):
    return pl.CostEstimate(flops=flops, bytes_accessed=nbytes, transcendentals=0)


def lane_index(rows):
    return lax.broadcasted_iota(jnp.int32, (rows, LANES), 1)


def pack_kernel(x, first, last, cols, ctop, cbottom, left, right, row_sem, col_sem):
    rows, width = x.shape[2:]
    copies = []
    for j in range(2):
        for side, (to, row) in enumerate(((first, j), (last, rows - 2 + j))):
            copies.append(
                pltpu.make_async_copy(x.at[:, :, row, :], to.at[:, j], row_sem.at[side, j])
            )
    col_copies = []
    for r in range(rows):
        for side, (to, start) in enumerate(((left, 0), (right, width - LANES))):
            col_copies.append(
                pltpu.make_async_copy(
                    x.at[:, :, r, start : start + LANES], to.at[:, r], col_sem.at[side, r]
                )
            )
    for copy in copies + col_copies:
        copy.start()
    for copy in col_copies:
        copy.wait()
    lane = lax.broadcasted_iota(jnp.int32, left.shape[2:], 1)
    for f in range(left.shape[0]):
        for r in range(rows):
            edge = jnp.where(lane < LANES // 2, left[f, r], right[f, r])
            cols[f, r] = edge
            if r == 0:
                ctop[f] = edge
            if r == rows - 1:
                cbottom[f] = edge
    for copy in copies:
        copy.wait()


def pack(ocean_state):
    fields, levels, rows, width = ocean_state.shape
    f32 = jnp.float32
    edge = (fields, rows, levels, LANES)
    return pl.pallas_call(
        pack_kernel,
        name="pack_edges",
        out_shape=(
            jax.ShapeDtypeStruct((fields, 2, levels, width), f32),
            jax.ShapeDtypeStruct((fields, 2, levels, width), f32),
            jax.ShapeDtypeStruct(edge, f32),
            jax.ShapeDtypeStruct((fields, levels, LANES), f32),
            jax.ShapeDtypeStruct((fields, levels, LANES), f32),
        ),
        in_specs=[spec(HBM)],
        out_specs=(spec(VMEM),) * 5,
        scratch_shapes=[
            pltpu.VMEM(edge, f32),
            pltpu.VMEM(edge, f32),
            pltpu.SemaphoreType.DMA((2, 2)),
            pltpu.SemaphoreType.DMA((2, rows)),
        ],
        compiler_params=pltpu.CompilerParams(vmem_limit_bytes=VMEM_BYTES),
        cost_estimate=cost(0, 4 * 2 * 4 * fields * levels * width),
    )(ocean_state)


def split(q, parts):
    out = []
    for _ in range(parts):
        part = q.astype(jnp.bfloat16)
        out.append(part)
        q = q - part.astype(jnp.float32)
    return out


def reorder(value, matrix):
    total = None
    for part in split(value, 3):
        term = jnp.dot(part, matrix, preferred_element_type=jnp.float32)
        total = term if total is None else total + term
    return total


def ice_kernel(
    count,
    listed,
    state,
    strength,
    mass,
    fraction,
    wind,
    surface,
    forward,
    backward,
    ice_out,
    stress_out,
    covered,
    su,
    sv,
    sx,
    sy,
    sxy,
    cp,
    cq,
    ca,
    cb,
    gx,
    gy,
):
    rows, width = mass.shape
    wide = 2 * BX
    pairs = width // wide
    area = rows * pairs
    blocks = width // BX

    for s in range(blocks):
        covered[listed[0, s]] = jnp.where(s < count[0], 1, 0)

    def chunk(j):
        return slice(j * wide, (j + 1) * wide)

    def place(j, odd):
        return pl.ds(odd * area + j, rows, stride=pairs)

    def enter(ref, get):
        value = jnp.concatenate([get(chunk(j)) for j in range(pairs)], axis=0)
        value = reorder(value, forward[...])
        for j in range(pairs):
            for odd in range(2):
                ref[place(j, odd), :] = value[
                    j * rows : (j + 1) * rows, odd * BX : (odd + 1) * BX
                ]

    def leave(ref):
        value = jnp.concatenate(
            [
                jnp.concatenate([ref[place(j, 0), :], ref[place(j, 1), :]], axis=1)
                for j in range(pairs)
            ],
            axis=0,
        )
        return reorder(value, backward[...])

    enter(su, lambda at: state[0, :, at])
    enter(sv, lambda at: state[1, :, at])
    enter(sx, lambda at: state[2, :, at])
    enter(sy, lambda at: state[3, :, at])
    enter(sxy, lambda at: state[4, :, at])
    enter(cp, lambda at: strength[:, at])
    enter(ca, lambda at: mass[:, at])
    enter(gx, lambda at: wind[0, :, at] + surface[0, 0, :, at])
    enter(gy, lambda at: wind[1, :, at] + surface[1, 0, :, at])

    lane = lane_index(pairs)
    final = (lane & (BX // 2 - 1)) == BX // 2 - 1
    initial = (lane & (BX // 2 - 1)) == 0

    def ahead(even, odd):
        return (
            odd - even,
            jnp.where(final, 0.0, pltpu.roll(even, LANES - 1, axis=1) - odd),
        )

    def behind(even, odd):
        return (
            even - jnp.where(initial, 0.0, pltpu.roll(odd, 1, axis=1)),
            odd - even,
        )

    def vec(odd, y):
        return pl.ds(odd * area + y * pairs, pairs)

    def row_of(ref, y):
        return (ref[vec(0, y), :], ref[vec(1, y), :])

    below = None
    for y in range(rows):
        p = tuple(RELAX * s for s in row_of(cp, y))
        across = behind(*p)
        for odd in range(2):
            i = vec(odd, y)
            m = ca[i, :]
            inverse = 1.0 / (m + SUB_STEP)
            push = SUB_STEP * inverse
            down = p[odd] if y == 0 else p[odd] - below[odd]
            gx[i, :] = push * (gx[i, :] - across[odd])
            gy[i, :] = push * (gy[i, :] - down)
            ca[i, :] = m * inverse
            cb[i, :] = push
            cq[i, :] = p[odd] * (0.625 * DECAY / 1.25**0.5)
            cp[i, :] = p[odd]
            sx[i, :] = sx[i, :] + p[odd]
            sy[i, :] = sy[i, :] + p[odd]
        below = p

    def sweep(step, carry):
        for _ in range(UNROLL):
            u, v = row_of(su, 0), row_of(sv, 0)
            above = None
            for y in range(rows):
                ux, vx = ahead(*u), ahead(*v)
                xx, yy, xy = [], [], []
                if y < rows - 1:
                    un, vn = row_of(su, y + 1), row_of(sv, y + 1)
                for odd in range(2):
                    i = vec(odd, y)
                    shear = vx[odd]
                    if y < rows - 1:
                        vy = vn[odd] - v[odd]
                        shear = shear + (un[odd] - u[odd])
                        a = ux[odd] + 0.6 * vy
                        b = 0.6 * ux[odd] + vy
                        d = ux[odd] * a + vy * b
                    else:
                        a = ux[odd]
                        b = 0.6 * a
                        d = a * a
                    small = 0.2 * shear
                    q = cq[i, :] * lax.rsqrt(d + (shear * small + 0.2))
                    xx.append(DECAY * sx[i, :] + q * a)
                    yy.append(DECAY * sy[i, :] + q * b)
                    xy.append(DECAY * sxy[i, :] + q * small)
                fx, fy = behind(*xx), behind(*xy)
                for odd in range(2):
                    i = vec(odd, y)
                    sx[i, :] = xx[odd]
                    sy[i, :] = yy[odd]
                    sxy[i, :] = xy[odd]
                    if y:
                        fxo = fx[odd] + (xy[odd] - above[0][odd])
                        fyo = fy[odd] + (yy[odd] - above[1][odd])
                    else:
                        fxo = fx[odd] + xy[odd]
                        fyo = fy[odd] + yy[odd]
                    a0 = ca[i, :]
                    b0 = cb[i, :]
                    uo, vo = u[odd], v[odd]
                    su[i, :] = a0 * (uo + TURNING * SUB_STEP * vo) + (b0 * fxo + gx[i, :])
                    sv[i, :] = a0 * (vo - TURNING * SUB_STEP * uo) + (b0 * fyo + gy[i, :])
                above = (xy, yy)
                if y < rows - 1:
                    u, v = un, vn
        return carry

    lax.fori_loop(0, SUBCYCLES // UNROLL, sweep, 0)

    sx[...] = sx[...] - cp[...]
    sy[...] = sy[...] - cp[...]
    for n, ref in enumerate((su, sv, sx, sy, sxy)):
        value = leave(ref)
        for b in range(blocks):
            at = slice(b * BX, (b + 1) * BX)
            new = value[(b // 2) * rows : (b // 2 + 1) * rows, (b % 2) * BX : (b % 2 + 1) * BX]
            keep = covered[b] == 1
            ice_out[n, :, at] = jnp.where(keep, new, state[n, :, at])
            if n < 2:
                part = fraction[:, at]
                w = wind[n, :, at]
                merged = part * (new - surface[n, 0, :, at]) + (1.0 - part) * w
                stress_out[n, :, at] = jnp.where(keep, merged, w)


def ice(ice_state, strength, ice_mass, ice_fraction, wind_stress, ice_count, ice_list, surface):
    rows, width = ice_mass.shape
    f32 = jnp.float32
    cells = (rows * width // BX, BX)
    wide = 2 * BX
    lanes = np.arange(wide)
    target = (lanes % 2) * BX + (lanes // BX) * (BX // 2) + (lanes % BX) // 2
    matrix = np.zeros((wide, wide), np.float32)
    matrix[lanes, target] = 1.0
    forward = jnp.asarray(matrix, jnp.bfloat16)
    backward = jnp.asarray(matrix.T, jnp.bfloat16)
    return pl.pallas_call(
        ice_kernel,
        name="ice_subcycles",
        out_shape=(
            jax.ShapeDtypeStruct(ice_state.shape, f32),
            jax.ShapeDtypeStruct(wind_stress.shape, f32),
        ),
        in_specs=[spec(SMEM)] * 2 + [spec(VMEM)] * 8,
        out_specs=(spec(VMEM), spec(VMEM)),
        scratch_shapes=[pltpu.SMEM((width // BX,), jnp.int32)]
        + [pltpu.VMEM(cells, f32)] * 11,
        compiler_params=pltpu.CompilerParams(vmem_limit_bytes=VMEM_BYTES),
        cost_estimate=cost(SUBCYCLES * 50 * rows * width, 4 * 22 * rows * width),
    )(
        ice_count,
        ice_list,
        ice_state,
        strength,
        ice_mass,
        ice_fraction,
        wind_stress,
        surface,
        forward,
        backward,
    )


WIDE = 256
FETCH = 512


def column_matrix():
    double = {0: 20.0, 1: -8.0, 2: 1.0}
    single = {0: -8.0, 1: 2.0}
    own = np.zeros((WIDE, 2 * WIDE), np.float32)
    side = np.zeros((LANES, 2 * WIDE), np.float32)
    for j in range(WIDE):
        for n, taps in enumerate((double, single)):
            for d, value in taps.items():
                for i in {j - d, j + d}:
                    if 0 <= i < WIDE:
                        own[i, n * WIDE + j] = value
                    else:
                        side[i % LANES, n * WIDE + j] = value
    return np.concatenate([own, own, side, side], axis=0)


def main_kernel(x_hbm, cols, bih, prev, cor, matrix, out_hbm, x, out, y, in_sem, out_sem):
    fields, rows, levels, width = x.shape
    steps = width // WIDE
    spans = width // FETCH
    each = FETCH // WIDE

    def fetches(s):
        at = slice(s * FETCH, (s + 1) * FETCH)
        return [
            pltpu.make_async_copy(x_hbm.at[:, :, r, at], x.at[:, r, :, at], in_sem.at[s, r])
            for r in range(rows)
        ]

    def stores(s):
        at = slice(s * FETCH, (s + 1) * FETCH)
        return [
            pltpu.make_async_copy(out.at[:, r, :, at], out_hbm.at[:, :, r, at], out_sem.at[s, r])
            for r in range(rows)
        ]

    for s in range(spans):
        for copy in fetches(s):
            copy.start()

    level = lax.broadcasted_iota(jnp.int32, (levels, WIDE), 0)
    lane = lax.broadcasted_iota(jnp.int32, (rows * levels, LANES), 1)
    surface, deepest = level == 0, level == levels - 1

    def merge(value):
        return value.reshape(rows * levels, value.shape[-1])

    waited = 0
    for m in range(steps):
        need = min((m + 1) // each, spans - 1)
        while waited <= need:
            for copy in fetches(waited):
                copy.wait()
            waited += 1
        at = slice(m * WIDE, (m + 1) * WIDE)
        for f in range(fields):
            slot = (m * fields + f) % 2
            own = merge(x[f, :, :, at])
            if m == 0:
                west = merge(cols[f])
            else:
                west = merge(x[f, :, :, m * WIDE - LANES : m * WIDE])
            if m == steps - 1:
                east = merge(cols[f])
            else:
                east = merge(x[f, :, :, (m + 1) * WIDE : (m + 1) * WIDE + LANES])
            side = jnp.where(lane < LANES // 2, east, west)
            y[slot] = jnp.dot(
                jnp.concatenate(split(own, 2) + split(side, 2), axis=1),
                matrix[...],
                preferred_element_type=jnp.float32,
            )

            def near(r):
                return y[slot, r * levels : (r + 1) * levels, WIDE : 2 * WIDE]

            for r in range(rows):
                q = x[f, r, :, at]
                lap = y[slot, r * levels : (r + 1) * levels, 0:WIDE]
                for step in (-1, 1):
                    if 0 <= r + step < rows:
                        lap = lap + near(r + step)
                    if 0 <= r + 2 * step < rows:
                        lap = lap + x[f, r + 2 * step, :, at]
                qb = jnp.where(surface, q, pltpu.roll(q, 1, axis=0))
                qa = jnp.where(deepest, q, pltpu.roll(q, levels - 1, axis=0))
                res = (1.0 - 2.0 * KV_MIX) * q + KV_MIX * (qb + qa) - bih[r : r + 1, at] * lap
                if f == 0:
                    res = res + cor[r] * x[1, r, :, at]
                elif f == 1:
                    res = res - cor[r] * x[0, r, :, at]
                if f < 2:
                    res = res + jnp.where(surface, prev[f, r : r + 1, at], 0.0)
                out[f, r, :, at] = res
        if m % each == each - 1:
            for copy in stores(m // each):
                copy.start()
    for s in range(spans):
        for copy in stores(s):
            copy.wait()


def ocean(ocean_state, cols, biharmonic, prev_stress, coriolis):
    fields, levels, rows, width = ocean_state.shape
    f32 = jnp.float32
    matrix = jnp.asarray(column_matrix(), jnp.bfloat16)
    held = (fields, rows, levels, width)
    return pl.pallas_call(
        main_kernel,
        name="ocean_tile",
        out_shape=jax.ShapeDtypeStruct(ocean_state.shape, f32),
        in_specs=[spec(HBM)] + [spec(VMEM)] * 3 + [spec(SMEM), spec(VMEM)],
        out_specs=spec(HBM),
        scratch_shapes=[
            pltpu.VMEM(held, f32),
            pltpu.VMEM(held, f32),
            pltpu.VMEM((2, rows * levels, 2 * WIDE), f32),
            pltpu.SemaphoreType.DMA((width // FETCH, rows)),
            pltpu.SemaphoreType.DMA((width // FETCH, rows)),
        ],
        compiler_params=pltpu.CompilerParams(vmem_limit_bytes=VMEM_BYTES),
        cost_estimate=cost(30 * ocean_state.size, 8 * ocean_state.size),
    )(ocean_state, cols, biharmonic, prev_stress, coriolis, matrix)


def fix_kernel(base, above, below, cabove, cbelow, bih, out, ha, hb, oa, ob, in_sem, out_sem):
    fields, _, levels, width = ha.shape
    rows = base.shape[2]
    tiles = width // LANES
    fetches, stores = [], []
    for f in range(fields):
        mine, back = [], []
        for j in range(2):
            for side, (buf, first) in enumerate(((oa, 0), (ob, rows - 2))):
                n = (f * 2 + j) * 2 + side
                mine.append(
                    pltpu.make_async_copy(base.at[f, :, first + j, :], buf.at[f, j], in_sem.at[n])
                )
                back.append(
                    pltpu.make_async_copy(buf.at[f, j], out.at[f, :, first + j, :], out_sem.at[n])
                )
        n = 4 * fields + 2 * f
        mine.append(pltpu.make_async_copy(above.at[f], ha.at[f], in_sem.at[n]))
        mine.append(pltpu.make_async_copy(below.at[f], hb.at[f], in_sem.at[n + 1]))
        fetches.append(mine)
        stores.append(back)
        for copy in mine:
            copy.start()

    lane = lane_index(HALF)
    initial, final = lane == 0, lane == LANES - 1

    for f in range(fields):
        for copy in fetches[f]:
            copy.wait()
        for halo, corner, near, far, buf, n1, n2 in (
            (ha, cabove, 1, 0, oa, 0, 1),
            (hb, cbelow, 0, 1, ob, 1, 0),
        ):
            r1 = n1 if buf is oa else rows - 2 + n1
            r2 = n2 if buf is oa else rows - 2 + n2

            def octet(s, carry):
                ks = pl.ds(pl.multiple_of(s * HALF, HALF), HALF)
                ext = corner[f, ks, :]
                ext_e, ext_w = pltpu.roll(ext, 1, axis=1), pltpu.roll(ext, LANES - 1, axis=1)
                cur = halo[f, near, ks, 0:LANES]
                west = ext_e
                cur_e, cur_w = pltpu.roll(cur, 1, axis=1), pltpu.roll(cur, LANES - 1, axis=1)
                for c in range(tiles):
                    at = slice(c * LANES, (c + 1) * LANES)
                    if c + 1 < tiles:
                        nxt = halo[f, near, ks, (c + 1) * LANES : (c + 2) * LANES]
                        nxt_e = pltpu.roll(nxt, 1, axis=1)
                        nxt_w = pltpu.roll(nxt, LANES - 1, axis=1)
                    else:
                        nxt, nxt_e, nxt_w = ext, ext_e, ext_w
                    around = jnp.where(initial, west, cur_e) + jnp.where(final, nxt_w, cur_w)
                    lap = halo[f, far, ks, at] + 2.0 * around - 8.0 * cur
                    buf[f, n1, ks, at] = buf[f, n1, ks, at] - bih[r1 : r1 + 1, at] * lap
                    buf[f, n2, ks, at] = buf[f, n2, ks, at] - bih[r2 : r2 + 1, at] * cur
                    west = cur_e
                    cur, cur_e, cur_w = nxt, nxt_e, nxt_w
                return carry

            lax.fori_loop(0, levels // HALF, octet, 0)
        for copy in stores[f]:
            copy.start()
    for back in stores:
        for copy in back:
            copy.wait()


def fix(base, above, below, cabove, cbelow, biharmonic):
    fields, levels, rows, width = base.shape
    f32 = jnp.float32
    edge = pltpu.VMEM((fields, 2, levels, width), f32)
    return pl.pallas_call(
        fix_kernel,
        name="ocean_edges",
        out_shape=jax.ShapeDtypeStruct(base.shape, f32),
        in_specs=[spec(HBM)] * 3 + [spec(VMEM)] * 3,
        out_specs=spec(HBM),
        input_output_aliases={0: 0},
        scratch_shapes=[
            edge,
            edge,
            edge,
            edge,
            pltpu.SemaphoreType.DMA((6 * fields,)),
            pltpu.SemaphoreType.DMA((4 * fields,)),
        ],
        compiler_params=pltpu.CompilerParams(vmem_limit_bytes=VMEM_BYTES),
        cost_estimate=cost(0, 3 * 4 * 4 * fields * levels * width),
    )(base, above, below, cabove, cbelow, biharmonic)


def per_device(
    ocean_state,
    biharmonic,
    prev_stress,
    ice_state,
    strength,
    ice_mass,
    ice_fraction,
    wind_stress,
    ice_count,
    ice_list,
):
    tile_rows = ocean_state.shape[2]
    n_tile = lax.axis_size("tile")
    n_grp = lax.axis_size("grp")

    first, last, cols, ctop, cbottom = pack(ocean_state)

    def shift(value, tile_step, grp_step):
        pairs = []
        for g in range(n_grp):
            for t in range(n_tile):
                if 0 <= t + tile_step < n_tile:
                    target = (g + grp_step) % n_grp
                    pairs.append((g * n_tile + t, target * n_tile + t + tile_step))
        return lax.ppermute(value, ("grp", "tile"), pairs)

    lane = jnp.arange(LANES)

    def around(value, tile_step, eastern):
        west = shift(value, tile_step, 1)
        if n_grp == 2:
            return west
        return jnp.where(eastern, shift(value, tile_step, -1), west)

    above = shift(last, 1, 0)
    below = shift(first, -1, 0)
    cols = around(cols, 0, lane < LANES // 2)
    cabove = around(cbottom, 1, lane < LANES // 2)
    cbelow = around(ctop, -1, lane < LANES // 2)

    ice_in = (ice_state, strength, ice_mass, ice_fraction, wind_stress, ice_count, ice_list)
    surface = ocean_state[0:2, 0:1]
    ice_out, stress_out = ice(*ice_in, surface)

    rows = (lax.axis_index("tile") * tile_rows + jnp.arange(tile_rows)).astype(jnp.float32) + 0.5
    coriolis = CORIOLIS * (2.0 * rows / (tile_rows * n_tile) - 1.0)
    base = ocean(ocean_state, cols, biharmonic, prev_stress, coriolis)
    ocean_out = fix(base, above, below, cabove, cbelow, biharmonic)
    return (ocean_out, ice_out, stress_out)


def solution(mesh):
    placed = (
        P(None, None, "tile", "grp"),
        P("tile", "grp"),
        P(None, "tile", "grp"),
        P(None, "tile", "grp"),
        P("tile", "grp"),
        P("tile", "grp"),
        P("tile", "grp"),
        P(None, "tile", "grp"),
        P(("grp", "tile")),
        P(("grp", "tile"), None),
    )
    return jax.shard_map(
        per_device,
        mesh=mesh,
        in_specs=placed,
        out_specs=(P(None, None, "tile", "grp"), P(None, "tile", "grp"), P(None, "tile", "grp")),
        check_vma=False,
    )
```

time: 203 us -> 65.1 us (0.32)
  Pallas kernels: 181 us -> 43.8 us
    pallas_call x1, Pallas kernels: 73.4 us -> 4.13 us  [pack(): pl.pallas_call(pack_kernel, name='pack_edges', out_shape=(jax.ShapeDtypeS...]
    pallas_call x1, Pallas kernels: 64.6 us -> 17.4 us  [ocean(): pl.pallas_call(main_kernel, name='ocean_tile', out_shape=jax.ShapeDtypeSt...]
    pallas_call x1, Pallas kernels: 37.8 us -> 16.9 us  [ice(): pl.pallas_call(ice_kernel, name='ice_subcycles', out_shape=(jax.ShapeDtyp...]
  transfers between devices with their start and end apart: 5 -> 5, of which waited for: 0 -> 0; matrix products, arithmetic and copies ran while one was open for 1% -> 2% of each run, Pallas kernels for 51% -> 53%
where the time goes in v2:
time: 65.1 us; the launch traced here: 64.7 us
  Pallas kernels  43.8 us (67%)
  starting transfers between devices  15.4 us (24%)
  local copies, waits for them, and re-layouts  3.81 us (6%)
  between operations  1.66 us (3%)
    pallas_call x1, Pallas kernels, ocean(): pl.pallas_call(main_kernel, name='ocean_tile', out_shape=jax.ShapeDtypeSt...  17.4 us
    pallas_call x1, Pallas kernels, ice(): pl.pallas_call(ice_kernel, name='ice_subcycles', out_shape=(jax.ShapeDtyp...  16.9 us
    ppermute x5, starting transfers between devices, shift(): return lax.ppermute(value, ('grp', 'tile'), pairs)  15.4 us
    pallas_call x1, Pallas kernels, fix(): pl.pallas_call(fix_kernel, name='ocean_edges', out_shape=jax.ShapeDtypeSt...  5.36 us
    pallas_call x1, Pallas kernels, pack(): pl.pallas_call(pack_kernel, name='pack_edges', out_shape=(jax.ShapeDtypeS...  4.13 us
    unnamed x22, local copies, waits for them, and re-layouts  2.75 us
  transfers between devices with their start and end apart: 5, of which 0 were waited for; matrix products, arithmetic and copies ran while one was open for 2% of the time, Pallas kernels for 53%

profile of v2, /device:TPU:24, one launch (start us, length us, event | category | flops | bytes accessed | tf_op | source)
XLA Modules:
  0.0 64.7 jit_solution(9207833195481417150)
XLA Ops:
  0.6 0.0 copy-start.1
  0.6 0.0 copy-start.5
  0.7 0.0 copy-start.6
  0.7 0.0 copy-start.4
  0.7 0.0 copy-start.10
  0.7 4.1 %pack_edges.1 = (f32[3,2,24,2048]{3,2,1,0:T(8,128)}, f32[3,2,24,2048]{3,2,1,0:T(8,128)}, f32[3,16,24,128]{3,2,1,0:T(8,128)}, f32[3,24,128]{2,1,0:T(8,128)}, f32[3,24,128]{2,1,0:T(8,128)}) custom-call(f32[3,24,16,2048]{3,2,1,0:T(8,128)} %x_hbm.1), custom_call_target="tpu_custom_call" | custom-call | bytes 4718592 | tf_op jit(solution)/shard_map/pack_edges/pallas_call | solution.py:79
  4.8 1.9 %collective-permute-start.1 = (f32[3,2,24,2048]{3,2,1,0:T(8,128)}, f32[3,2,24,2048]{3,2,1,0:T(8,128)S(1)}, u32[]{:S(2)}, u32[]{:S(2)}) collective-permute-start(f32[3,2,24,2048]{3,2,1,0:T(8,128)} %get-tuple-element.11), channel_id=1, source_target_pairs={{0,1},{1,2},{2,3},{3,4},{4,5},{5,6},{6,7},{7,8},{8,9},{9,10},{10,1... | collective-permute-start | bytes 3538952 | tf_op jit(solution)/shard_map/ppermute | solution.py:582
  6.8 4.5 %collective-permute-start.2 = (f32[3,2,24,2048]{3,2,1,0:T(8,128)}, f32[3,2,24,2048]{3,2,1,0:T(8,128)S(1)}, u32[]{:S(2)}, u32[]{:S(2)}) collective-permute-start(f32[3,2,24,2048]{3,2,1,0:T(8,128)} %get-tuple-element.12), channel_id=1, source_target_pairs={{1,0},{2,1},{3,2},{4,3},{5,4},{6,5},{7,6},{8,7},{9,8},{10,9},{11,1... | collective-permute-start | bytes 3538952 | tf_op jit(solution)/shard_map/ppermute | solution.py:582
  11.3 1.6 %collective-permute-start = (f32[3,16,24,128]{3,2,1,0:T(8,128)}, f32[3,16,24,128]{3,2,1,0:T(8,128)}, u32[]{:S(2)}, u32[]{:S(2)}) collective-permute-start(f32[3,16,24,128]{3,2,1,0:T(8,128)} %get-tuple-element.10), channel_id=1, source_target_pairs={{0,16},{1,17},{2,18},{3,19},{4,20},{5,21},{6,22},{7,23},{8,24},{9,... | collective-permute-start | bytes 1769480 | tf_op jit(solution)/shard_map/ppermute | solution.py:582
  12.9 1.9 %collective-permute-start.3 = (f32[3,24,128]{2,1,0:T(8,128)}, f32[3,24,128]{2,1,0:T(8,128)}, u32[]{:S(2)}, u32[]{:S(2)}) collective-permute-start(f32[3,24,128]{2,1,0:T(8,128)} %get-tuple-element.13), channel_id=1, source_target_pairs={{0,17},{1,18},{2,19},{3,20},{4,21},{5,22},{6,23},{7,24},{8,25},{9,... | collective-permute-start | bytes 110600 | tf_op jit(solution)/shard_map/ppermute | solution.py:582
  14.8 5.4 %collective-permute-start.4 = (f32[3,24,128]{2,1,0:T(8,128)}, f32[3,24,128]{2,1,0:T(8,128)}, u32[]{:S(2)}, u32[]{:S(2)}) collective-permute-start(f32[3,24,128]{2,1,0:T(8,128)} %get-tuple-element.14), channel_id=1, source_target_pairs={{1,16},{2,17},{3,18},{4,19},{5,20},{6,21},{7,22},{8,23},{9,24},{10... | collective-permute-start | bytes 110600 | tf_op jit(solution)/shard_map/ppermute | solution.py:582
  20.2 0.0 copy-start
  20.3 0.0 copy-start.2
  20.3 0.0 copy-start.3
  20.3 1.1 %slice.3.surface = f32[2,1,16,2048]{3,2,1,0:T(8,128)S(1)} slice(f32[3,24,16,2048]{3,2,1,0:T(8,128)} %x_hbm.1), slice={[0:2], [0:1], [0:16], [0:2048]} | slice | bytes 524288 | tf_op jit(solution)/shard_map/slice | solution.py:599
  22.0 0.0 copy-done.1
  22.0 0.0 copy-done.5
  22.0 0.0 copy-done.6
  22.0 0.0 copy-done.4
  22.0 0.0 copy-done.10
  22.0 0.0 copy-start.7
  22.1 0.9 %copy-done.7 = f32[16,2048]{1,0:T(8,128)S(1)} copy-done((f32[16,2048]{1,0:T(8,128)S(1)}, f32[16,2048]{1,0:T(8,128)}, u32[]{:S(2)}) %copy-start.7) | copy-done | bytes 131096
  23.0 0.9 %copy-done.8 = bf16[256,256]{1,0:T(8,128)(2,1)S(1)} copy-done((bf16[256,256]{1,0:T(8,128)(2,1)S(1)}, bf16[256,256]{1,0:T(8,128)(2,1)}, u32[]{:S(2)}) %copy-start.8) | copy-done | bytes 131096
  23.9 0.9 %copy-done.9 = bf16[256,256]{1,0:T(8,128)(2,1)S(1)} copy-done((bf16[256,256]{1,0:T(8,128)(2,1)S(1)}, bf16[256,256]{1,0:T(8,128)(2,1)}, u32[]{:S(2)}) %copy-start.9) | copy-done | bytes 131096
  24.8 16.9 %ice_subcycles.1 = (f32[5,16,2048]{2,1,0:T(8,128)}, f32[2,16,2048]{2,1,0:T(8,128)}) custom-call(s32[1]{0:T(128)S(6)} %copy.18.count, s32[1,16]{1,0:T(1,128)S(1)} %copy-done.10, f32[5,16,2048]{2,1,0:T(8,128)S(1)} %copy-done.1, f32[16,2048]{1,0:T(8,128)S(1)} %copy-done.5, f32[16,2048]{1,0:T(8,128)S(1)} %copy-done.6, f32[16,2048]{1,0:T(8,128)S(1)} %copy-done.7, ...), custom_call_target="tpu_custom_call" | custom-call | flops 104857600 | bytes 2883584 | tf_op jit(solution)/shard_map/ice_subcycles/pallas_call | solution.py:309
  41.6 0.0 collective-permute-done.cols
  41.7 17.4 %ocean_tile.1.base = f32[3,24,16,2048]{3,2,1,0:T(8,128)} custom-call(f32[3,24,16,2048]{3,2,1,0:T(8,128)} %x_hbm.1, f32[3,16,24,128]{3,2,1,0:T(8,128)} %collective-permute-done.cols, f32[16,2048]{1,0:T(8,128)S(1)} %copy-done.2, f32[2,16,2048]{2,1,0:T(8,128)S(1)} %copy-done.3, f32[16]{0:T(128)S(1)} %add_multiply_fusion.cor, bf16[768,512]{1,0:T(8,128)(2,1)S(1)} %copy-done), custom_call_target="tpu_custom_call" | custom-call | flops 70778880 | bytes 18874368 | tf_op jit(solution)/shard_map/ocean_tile/pallas_call | solution.py:447
  59.1 0.0 collective-permute-done.3.cabove
  59.1 0.0 collective-permute-done.4.cbelow
  59.1 0.0 collective-permute-done.1.above
  59.1 0.0 collective-permute-done.2.below
  59.1 5.4 %ocean_edges.1 = f32[3,24,16,2048]{3,2,1,0:T(8,128)} custom-call(f32[3,24,16,2048]{3,2,1,0:T(8,128)} %ocean_tile.1.base, f32[3,2,24,2048]{3,2,1,0:T(8,128)S(1)} %collective-permute-done.1.above, f32[3,2,24,2048]{3,2,1,0:T(8,128)S(1)} %collective-permute-done.2.below, f32[3,24,128]{2,1,0:T(8,128)} %collective-permute-done.3.cabove, ...), custom_call_target="tpu_custom_call", output_to_operand_aliasing={{}: (0, {})} | custom-call | bytes 7077888 | tf_op jit(solution)/shard_map/ocean_edges/pallas_call | solution.py:537
  (6 shorter events, 0.0 us)
Async XLA Ops:
  0.6 21.4 %copy-start.1 = (f32[5,16,2048]{2,1,0:T(8,128)S(1)}, f32[5,16,2048]{2,1,0:T(8,128)}, u32[]{:S(2)}) copy-start(f32[5,16,2048]{2,1,0:T(8,128)} %state.1) | copy-start | bytes 1966084
  0.6 21.4 %copy-start.5 = (f32[16,2048]{1,0:T(8,128)S(1)}, f32[16,2048]{1,0:T(8,128)}, u32[]{:S(2)}) copy-start(f32[16,2048]{1,0:T(8,128)} %strength.1) | copy-start | bytes 393220
  0.7 21.4 %copy-start.6 = (f32[16,2048]{1,0:T(8,128)S(1)}, f32[16,2048]{1,0:T(8,128)}, u32[]{:S(2)}) copy-start(f32[16,2048]{1,0:T(8,128)} %mass.1) | copy-start | bytes 393220
  0.7 21.4 %copy-start.4 = (f32[2,16,2048]{2,1,0:T(8,128)S(1)}, f32[2,16,2048]{2,1,0:T(8,128)}, u32[]{:S(2)}) copy-start(f32[2,16,2048]{2,1,0:T(8,128)} %wind.1) | copy-start | bytes 786436
  0.7 21.4 %copy-start.10 = (s32[1,16]{1,0:T(1,128)S(1)}, s32[1,16]{1,0:T(1,128)}, u32[]{:S(2)}) copy-start(s32[1,16]{1,0:T(1,128)} %listed.1) | copy-start | bytes 196
  4.8 54.3 %collective-permute-start.1 = (f32[3,2,24,2048]{3,2,1,0:T(8,128)}, f32[3,2,24,2048]{3,2,1,0:T(8,128)S(1)}, u32[]{:S(2)}, u32[]{:S(2)}) collective-permute-start(f32[3,2,24,2048]{3,2,1,0:T(8,128)} %get-tuple-element.11), channel_id=1, source_target_pairs={{0,1},{1,2},{2,3},{3,4},{4,5},{5,6},{6,7},{7,8},{8,9},{9,10},{10,1... | collective-permute-start | bytes 3538952 | tf_op jit(solution)/shard_map/ppermute | solution.py:582
  6.8 52.4 %collective-permute-start.2 = (f32[3,2,24,2048]{3,2,1,0:T(8,128)}, f32[3,2,24,2048]{3,2,1,0:T(8,128)S(1)}, u32[]{:S(2)}, u32[]{:S(2)}) collective-permute-start(f32[3,2,24,2048]{3,2,1,0:T(8,128)} %get-tuple-element.12), channel_id=1, source_target_pairs={{1,0},{2,1},{3,2},{4,3},{5,4},{6,5},{7,6},{8,7},{9,8},{10,9},{11,1... | collective-permute-start | bytes 3538952 | tf_op jit(solution)/shard_map/ppermute | solution.py:582
  11.3 30.3 %collective-permute-start = (f32[3,16,24,128]{3,2,1,0:T(8,128)}, f32[3,16,24,128]{3,2,1,0:T(8,128)}, u32[]{:S(2)}, u32[]{:S(2)}) collective-permute-start(f32[3,16,24,128]{3,2,1,0:T(8,128)} %get-tuple-element.10), channel_id=1, source_target_pairs={{0,16},{1,17},{2,18},{3,19},{4,20},{5,21},{6,22},{7,23},{8,24},{9,... | collective-permute-start | bytes 1769480 | tf_op jit(solution)/shard_map/ppermute | solution.py:582
  12.9 46.2 %collective-permute-start.3 = (f32[3,24,128]{2,1,0:T(8,128)}, f32[3,24,128]{2,1,0:T(8,128)}, u32[]{:S(2)}, u32[]{:S(2)}) collective-permute-start(f32[3,24,128]{2,1,0:T(8,128)} %get-tuple-element.13), channel_id=1, source_target_pairs={{0,17},{1,18},{2,19},{3,20},{4,21},{5,22},{6,23},{7,24},{8,25},{9,... | collective-permute-start | bytes 110600 | tf_op jit(solution)/shard_map/ppermute | solution.py:582
  14.8 44.3 %collective-permute-start.4 = (f32[3,24,128]{2,1,0:T(8,128)}, f32[3,24,128]{2,1,0:T(8,128)}, u32[]{:S(2)}, u32[]{:S(2)}) collective-permute-start(f32[3,24,128]{2,1,0:T(8,128)} %get-tuple-element.14), channel_id=1, source_target_pairs={{1,16},{2,17},{3,18},{4,19},{5,20},{6,21},{7,22},{8,23},{9,24},{10... | collective-permute-start | bytes 110600 | tf_op jit(solution)/shard_map/ppermute | solution.py:582
  20.2 21.4 %copy-start = (bf16[768,512]{1,0:T(8,128)(2,1)S(1)}, bf16[768,512]{1,0:T(8,128)(2,1)}, u32[]{:S(2)}) copy-start(bf16[768,512]{1,0:T(8,128)(2,1)} %constant.26.clone.matrix) | copy-start | bytes 2359300
  20.3 21.4 %copy-start.2 = (f32[16,2048]{1,0:T(8,128)S(1)}, f32[16,2048]{1,0:T(8,128)}, u32[]{:S(2)}) copy-start(f32[16,2048]{1,0:T(8,128)} %bih.3) | copy-start | bytes 393220
  20.3 21.4 %copy-start.3 = (f32[2,16,2048]{2,1,0:T(8,128)S(1)}, f32[2,16,2048]{2,1,0:T(8,128)}, u32[]{:S(2)}) copy-start(f32[2,16,2048]{2,1,0:T(8,128)} %prev.1) | copy-start | bytes 786436
  22.0 0.9 %copy-start.7 = (f32[16,2048]{1,0:T(8,128)S(1)}, f32[16,2048]{1,0:T(8,128)}, u32[]{:S(2)}) copy-start(f32[16,2048]{1,0:T(8,128)} %fraction.1) | copy-start | bytes 393220
  22.9 0.9 %copy-start.8 = (bf16[256,256]{1,0:T(8,128)(2,1)S(1)}, bf16[256,256]{1,0:T(8,128)(2,1)}, u32[]{:S(2)}) copy-start(bf16[256,256]{1,0:T(8,128)(2,1)} %constant.24.clone.forward) | copy-start | bytes 393220
  23.9 0.9 %copy-start.9 = (bf16[256,256]{1,0:T(8,128)(2,1)S(1)}, bf16[256,256]{1,0:T(8,128)(2,1)}, u32[]{:S(2)}) copy-start(bf16[256,256]{1,0:T(8,128)(2,1)} %constant.25.clone.backward) | copy-start | bytes 393220

commit v3 on v2

--- a/solution.py
+++ b/solution.py
@@ -1,6 +1,5 @@
 import jax
 import jax.numpy as jnp
-import numpy as np
 from jax import lax
 from jax.experimental import pallas as pl
 from jax.experimental.pallas import tpu as pltpu
@@ -39,13 +38,91 @@
     return lax.broadcasted_iota(jnp.int32, (rows, LANES), 1)
 
 
-def pack_kernel(x, first, last, cols, ctop, cbottom, left, right, row_sem, col_sem):
+WIDE = 256
+FETCH = 512
+GROUP = 4
+
+
+def iota(shape, dim):
+    return lax.broadcasted_iota(jnp.int32, shape, dim)
+
+
+def as_matrix(value):
+    return value.astype(jnp.float32).astype(jnp.bfloat16)
+
+
+def column_taps(source, shape):
+    place = iota(shape, 1)
+    d = jnp.abs(source - (place & (WIDE - 1)))
+    double = jnp.where(d == 0, 20, jnp.where(d == 1, -8, jnp.where(d == 2, 1, 0)))
+    single = jnp.where(d == 0, -8, jnp.where(d == 1, 2, 0))
+    return as_matrix(jnp.where(place < WIDE, double, single))
+
+
+def make_columns(matrix):
+    own = (WIDE, 2 * WIDE)
+    taps = column_taps(iota(own, 0), own)
+    matrix[0:WIDE, :] = taps
+    matrix[WIDE : 2 * WIDE, :] = taps
+    side = (LANES, 2 * WIDE)
+    lane = iota(side, 0)
+    taps = column_taps(jnp.where(lane < LANES // 2, lane + WIDE, lane - LANES), side)
+    matrix[2 * WIDE : 2 * WIDE + LANES, :] = taps
+    matrix[2 * WIDE + LANES : 2 * WIDE + 2 * LANES, :] = taps
+
+
+def make_mixing(mixing, levels):
+    height = GROUP * levels
+    shape = mixing.shape
+    a, c = iota(shape, 0), iota(shape, 1)
+    c = jnp.where(c >= height, c - height, c)
+
+    def parts(index):
+        group = jnp.zeros(shape, jnp.int32)
+        for n in range(1, GROUP):
+            group = group + jnp.where(index >= n * levels, 1, 0)
+        return group, index - levels * group
+
+    ga, la = parts(a)
+    gc, lc = parts(c)
+    value = (
+        jnp.where(lc == jnp.maximum(la - 1, 0), 1, 0)
+        + jnp.where(lc == jnp.minimum(la + 1, levels - 1), 1, 0)
+        - jnp.where(lc == la, 2, 0)
+    )
+    mixing[...] = as_matrix(jnp.where(ga == gc, value, 0))
+
+
+def make_orders(forward, backward):
+    shape = forward.shape
+
+    def target(i):
+        return ((i & 1) * BX) + ((i >> 7) * (BX // 2)) + ((i & (BX - 1)) >> 1)
+
+    forward[...] = as_matrix(jnp.where(target(iota(shape, 0)) == iota(shape, 1), 1, 0))
+    backward[...] = as_matrix(jnp.where(target(iota(shape, 1)) == iota(shape, 0), 1, 0))
+
+
+def pack_kernel(
+    x,
+    first,
+    last,
+    cols,
+    matrix,
+    mixing,
+    forward,
+    backward,
+    left,
+    right,
+    row_sem,
+    col_sem,
+):
     rows, width = x.shape[2:]
     copies = []
     for j in range(2):
         for side, (to, row) in enumerate(((first, j), (last, rows - 2 + j))):
             copies.append(
-                pltpu.make_async_copy(x.at[:, :, row, :], to.at[:, j], row_sem.at[side, j])
+                pltpu.make_async_copy(x.at[:, :, row, :], to.at[j], row_sem.at[side, j])
             )
     col_copies = []
     for r in range(rows):
@@ -57,17 +134,15 @@
             )
     for copy in copies + col_copies:
         copy.start()
+    make_columns(matrix)
+    make_mixing(mixing, x.shape[1])
+    make_orders(forward, backward)
     for copy in col_copies:
         copy.wait()
     lane = lax.broadcasted_iota(jnp.int32, left.shape[2:], 1)
     for f in range(left.shape[0]):
         for r in range(rows):
-            edge = jnp.where(lane < LANES // 2, left[f, r], right[f, r])
-            cols[f, r] = edge
-            if r == 0:
-                ctop[f] = edge
-            if r == rows - 1:
-                cbottom[f] = edge
+            cols[f, r] = jnp.where(lane < LANES // 2, left[f, r], right[f, r])
     for copy in copies:
         copy.wait()
 
@@ -80,14 +155,16 @@
         pack_kernel,
         name="pack_edges",
         out_shape=(
-            jax.ShapeDtypeStruct((fields, 2, levels, width), f32),
-            jax.ShapeDtypeStruct((fields, 2, levels, width), f32),
+            jax.ShapeDtypeStruct((2, fields, levels, width), f32),
+            jax.ShapeDtypeStruct((2, fields, levels, width), f32),
             jax.ShapeDtypeStruct(edge, f32),
-            jax.ShapeDtypeStruct((fields, levels, LANES), f32),
-            jax.ShapeDtypeStruct((fields, levels, LANES), f32),
+            jax.ShapeDtypeStruct((2 * (WIDE + LANES), 2 * WIDE), jnp.bfloat16),
+            jax.ShapeDtypeStruct((GROUP * levels, 2 * GROUP * levels), jnp.bfloat16),
+            jax.ShapeDtypeStruct((2 * BX, 2 * BX), jnp.bfloat16),
+            jax.ShapeDtypeStruct((2 * BX, 2 * BX), jnp.bfloat16),
         ),
         in_specs=[spec(HBM)],
-        out_specs=(spec(VMEM),) * 5,
+        out_specs=(spec(VMEM),) * 7,
         scratch_shapes=[
             pltpu.VMEM(edge, f32),
             pltpu.VMEM(edge, f32),
@@ -119,16 +196,23 @@
 def ice_kernel(
     count,
     listed,
+    state_hbm,
+    strength_hbm,
+    mass_hbm,
+    fraction_hbm,
+    wind_hbm,
+    ocean_hbm,
+    forward,
+    backward,
+    ice_out,
+    stress_out,
     state,
     strength,
     mass,
     fraction,
     wind,
     surface,
-    forward,
-    backward,
-    ice_out,
-    stress_out,
+    sem,
     covered,
     su,
     sv,
@@ -148,6 +232,23 @@
     area = rows * pairs
     blocks = width // BX
 
+    copies = [
+        pltpu.make_async_copy(source, to, sem.at[n])
+        for n, (source, to) in enumerate(
+            (
+                (state_hbm, state),
+                (strength_hbm, strength),
+                (mass_hbm, mass),
+                (wind_hbm, wind),
+                (ocean_hbm.at[0, 0], surface.at[0]),
+                (ocean_hbm.at[1, 0], surface.at[1]),
+                (fraction_hbm, fraction),
+            )
+        )
+    ]
+    for copy in copies:
+        copy.start()
+
     for s in range(blocks):
         covered[listed[0, s]] = jnp.where(s < count[0], 1, 0)
 
@@ -176,15 +277,18 @@
         )
         return reorder(value, backward[...])
 
+    copies[0].wait()
     enter(su, lambda at: state[0, :, at])
     enter(sv, lambda at: state[1, :, at])
     enter(sx, lambda at: state[2, :, at])
     enter(sy, lambda at: state[3, :, at])
     enter(sxy, lambda at: state[4, :, at])
+    for copy in copies[1:]:
+        copy.wait()
     enter(cp, lambda at: strength[:, at])
     enter(ca, lambda at: mass[:, at])
-    enter(gx, lambda at: wind[0, :, at] + surface[0, 0, :, at])
-    enter(gy, lambda at: wind[1, :, at] + surface[1, 0, :, at])
+    enter(gx, lambda at: wind[0, :, at] + surface[0, :, at])
+    enter(gy, lambda at: wind[1, :, at] + surface[1, :, at])
 
     lane = lane_index(pairs)
     final = (lane & (BX // 2 - 1)) == BX // 2 - 1
@@ -291,21 +395,14 @@
             if n < 2:
                 part = fraction[:, at]
                 w = wind[n, :, at]
-                merged = part * (new - surface[n, 0, :, at]) + (1.0 - part) * w
+                merged = part * (new - surface[n, :, at]) + (1.0 - part) * w
                 stress_out[n, :, at] = jnp.where(keep, merged, w)
 
 
-def ice(ice_state, strength, ice_mass, ice_fraction, wind_stress, ice_count, ice_list, surface):
+def ice(ice_state, strength, ice_mass, ice_fraction, wind_stress, ice_count, ice_list, ocean_state, forward, backward):
     rows, width = ice_mass.shape
     f32 = jnp.float32
     cells = (rows * width // BX, BX)
-    wide = 2 * BX
-    lanes = np.arange(wide)
-    target = (lanes % 2) * BX + (lanes // BX) * (BX // 2) + (lanes % BX) // 2
-    matrix = np.zeros((wide, wide), np.float32)
-    matrix[lanes, target] = 1.0
-    forward = jnp.asarray(matrix, jnp.bfloat16)
-    backward = jnp.asarray(matrix.T, jnp.bfloat16)
     return pl.pallas_call(
         ice_kernel,
         name="ice_subcycles",
@@ -313,9 +410,18 @@
             jax.ShapeDtypeStruct(ice_state.shape, f32),
             jax.ShapeDtypeStruct(wind_stress.shape, f32),
         ),
-        in_specs=[spec(SMEM)] * 2 + [spec(VMEM)] * 8,
+        in_specs=[spec(SMEM)] * 2 + [spec(HBM)] * 6 + [spec(VMEM)] * 2,
         out_specs=(spec(VMEM), spec(VMEM)),
-        scratch_shapes=[pltpu.SMEM((width // BX,), jnp.int32)]
+        scratch_shapes=[
+            pltpu.VMEM(ice_state.shape, f32),
+            pltpu.VMEM((rows, width), f32),
+            pltpu.VMEM((rows, width), f32),
+            pltpu.VMEM((rows, width), f32),
+            pltpu.VMEM((2, rows, width), f32),
+            pltpu.VMEM((2, rows, width), f32),
+            pltpu.SemaphoreType.DMA((7,)),
+            pltpu.SMEM((width // BX,), jnp.int32),
+        ]
         + [pltpu.VMEM(cells, f32)] * 11,
         compiler_params=pltpu.CompilerParams(vmem_limit_bytes=VMEM_BYTES),
         cost_estimate=cost(SUBCYCLES * 50 * rows * width, 4 * 22 * rows * width),
@@ -327,33 +433,15 @@
         ice_mass,
         ice_fraction,
         wind_stress,
-        surface,
+        ocean_state,
         forward,
         backward,
     )
 
 
-WIDE = 256
-FETCH = 512
-
-
-def column_matrix():
-    double = {0: 20.0, 1: -8.0, 2: 1.0}
-    single = {0: -8.0, 1: 2.0}
-    own = np.zeros((WIDE, 2 * WIDE), np.float32)
-    side = np.zeros((LANES, 2 * WIDE), np.float32)
-    for j in range(WIDE):
-        for n, taps in enumerate((double, single)):
-            for d, value in taps.items():
-                for i in {j - d, j + d}:
-                    if 0 <= i < WIDE:
-                        own[i, n * WIDE + j] = value
-                    else:
-                        side[i % LANES, n * WIDE + j] = value
-    return np.concatenate([own, own, side, side], axis=0)
-
-
-def main_kernel(x_hbm, cols, bih, prev, cor, matrix, out_hbm, x, out, y, in_sem, out_sem):
+def main_kernel(
+    x_hbm, cols, bih, prev, cor, matrix, mixing, out_hbm, x, out, y, z, in_sem, out_sem
+):
     fields, rows, levels, width = x.shape
     steps = width // WIDE
     spans = width // FETCH
@@ -377,9 +465,8 @@
         for copy in fetches(s):
             copy.start()
 
-    level = lax.broadcasted_iota(jnp.int32, (levels, WIDE), 0)
+    level = lax.broadcasted_iota(jnp.int32, (HALF, WIDE), 0)
     lane = lax.broadcasted_iota(jnp.int32, (rows * levels, LANES), 1)
-    surface, deepest = level == 0, level == levels - 1
 
     def merge(value):
         return value.reshape(rows * levels, value.shape[-1])
@@ -404,11 +491,20 @@
             else:
                 east = merge(x[f, :, :, (m + 1) * WIDE : (m + 1) * WIDE + LANES])
             side = jnp.where(lane < LANES // 2, east, west)
+            parts = split(own, 2)
             y[slot] = jnp.dot(
-                jnp.concatenate(split(own, 2) + split(side, 2), axis=1),
+                jnp.concatenate(parts + split(side, 2), axis=1),
                 matrix[...],
                 preferred_element_type=jnp.float32,
             )
+            height = GROUP * levels
+            for n in range(rows // GROUP):
+                group = slice(n * height, (n + 1) * height)
+                z[slot, group, :] = jnp.dot(
+                    mixing[...],
+                    jnp.concatenate([part[group] for part in parts], axis=0),
+                    preferred_element_type=jnp.float32,
+                )
 
             def near(r):
                 return y[slot, r * levels : (r + 1) * levels, WIDE : 2 * WIDE]
@@ -421,16 +517,17 @@
                         lap = lap + near(r + step)
                     if 0 <= r + 2 * step < rows:
                         lap = lap + x[f, r + 2 * step, :, at]
-                qb = jnp.where(surface, q, pltpu.roll(q, 1, axis=0))
-                qa = jnp.where(deepest, q, pltpu.roll(q, levels - 1, axis=0))
-                res = (1.0 - 2.0 * KV_MIX) * q + KV_MIX * (qb + qa) - bih[r : r + 1, at] * lap
+                mixed = z[slot, r * levels : (r + 1) * levels, :]
+                res = q + KV_MIX * mixed - bih[r : r + 1, at] * lap
                 if f == 0:
                     res = res + cor[r] * x[1, r, :, at]
                 elif f == 1:
                     res = res - cor[r] * x[0, r, :, at]
+                out[f, r, :, at] = res
                 if f < 2:
-                    res = res + jnp.where(surface, prev[f, r : r + 1, at], 0.0)
-                out[f, r, :, at] = res
+                    out[f, r, 0:HALF, at] = res[0:HALF] + jnp.where(
+                        level == 0, prev[f, r : r + 1, at], 0.0
+                    )
         if m % each == each - 1:
             for copy in stores(m // each):
                 copy.start()
@@ -439,33 +536,57 @@
             copy.wait()
 
 
-def ocean(ocean_state, cols, biharmonic, prev_stress, coriolis):
+def ocean(ocean_state, cols, biharmonic, prev_stress, coriolis, matrix, mixing):
     fields, levels, rows, width = ocean_state.shape
     f32 = jnp.float32
-    matrix = jnp.asarray(column_matrix(), jnp.bfloat16)
     held = (fields, rows, levels, width)
     return pl.pallas_call(
         main_kernel,
         name="ocean_tile",
         out_shape=jax.ShapeDtypeStruct(ocean_state.shape, f32),
-        in_specs=[spec(HBM)] + [spec(VMEM)] * 3 + [spec(SMEM), spec(VMEM)],
+        in_specs=[spec(HBM)] + [spec(VMEM)] * 3 + [spec(SMEM)] + [spec(VMEM)] * 2,
         out_specs=spec(HBM),
         scratch_shapes=[
             pltpu.VMEM(held, f32),
             pltpu.VMEM(held, f32),
             pltpu.VMEM((2, rows * levels, 2 * WIDE), f32),
+            pltpu.VMEM((2, rows * levels, WIDE), f32),
             pltpu.SemaphoreType.DMA((width // FETCH, rows)),
             pltpu.SemaphoreType.DMA((width // FETCH, rows)),
         ],
         compiler_params=pltpu.CompilerParams(vmem_limit_bytes=VMEM_BYTES),
         cost_estimate=cost(30 * ocean_state.size, 8 * ocean_state.size),
-    )(ocean_state, cols, biharmonic, prev_stress, coriolis, matrix)
-
-
-def fix_kernel(base, above, below, cabove, cbelow, bih, out, ha, hb, oa, ob, in_sem, out_sem):
-    fields, _, levels, width = ha.shape
+    )(ocean_state, cols, biharmonic, prev_stress, coriolis, matrix, mixing)
+
+
+def ends_kernel(above, below, out):
+    width = above.shape[3]
+    lane = lax.broadcasted_iota(jnp.int32, out.shape[2:], 1)
+    for n, (halo, near) in enumerate(((above, 1), (below, 0))):
+        for f in range(above.shape[1]):
+            out[n, f] = jnp.where(
+                lane < LANES // 2,
+                halo[near, f, :, 0:LANES],
+                halo[near, f, :, width - LANES : width],
+            )
+
+
+def ends(above, below):
+    _, fields, levels, _ = above.shape
+    return pl.pallas_call(
+        ends_kernel,
+        name="received_ends",
+        out_shape=jax.ShapeDtypeStruct((2, fields, levels, LANES), jnp.float32),
+        in_specs=[spec(VMEM)] * 2,
+        out_specs=spec(VMEM),
+        compiler_params=pltpu.CompilerParams(vmem_limit_bytes=VMEM_BYTES),
+    )(above, below)
+
+
+def fix_kernel(base, above, below, corners, bih, matrix, out, oa, ob, y, in_sem, out_sem):
+    _, fields, levels, width = above.shape
     rows = base.shape[2]
-    tiles = width // LANES
+    steps = width // WIDE
     fetches, stores = [], []
     for f in range(fields):
         mine, back = [], []
@@ -478,51 +599,48 @@
                 back.append(
                     pltpu.make_async_copy(buf.at[f, j], out.at[f, :, first + j, :], out_sem.at[n])
                 )
-        n = 4 * fields + 2 * f
-        mine.append(pltpu.make_async_copy(above.at[f], ha.at[f], in_sem.at[n]))
-        mine.append(pltpu.make_async_copy(below.at[f], hb.at[f], in_sem.at[n + 1]))
         fetches.append(mine)
         stores.append(back)
         for copy in mine:
             copy.start()
 
-    lane = lane_index(HALF)
-    initial, final = lane == 0, lane == LANES - 1
+    sides = ((above, 1), (below, 0))
+    height = 2 * fields * levels
+    lane = lax.broadcasted_iota(jnp.int32, (height, LANES), 1)
+
+    def nearest(start, size):
+        at = slice(start, start + size)
+        return jnp.concatenate(
+            [halo[near, f, :, at] for f in range(fields) for halo, near in sides], axis=0
+        )
+
+    ends = jnp.concatenate([corners[n, f] for f in range(fields) for n in range(2)], axis=0)
+    for m in range(steps):
+        west = ends if m == 0 else nearest(m * WIDE - LANES, LANES)
+        east = ends if m == steps - 1 else nearest((m + 1) * WIDE, LANES)
+        own = nearest(m * WIDE, WIDE)
+        side = jnp.where(lane < LANES // 2, east, west)
+        y[:, m * WIDE : (m + 1) * WIDE] = jnp.dot(
+            jnp.concatenate(split(own, 2) + split(side, 2), axis=1),
+            matrix[:, WIDE : 2 * WIDE],
+            preferred_element_type=jnp.float32,
+        )
 
     for f in range(fields):
         for copy in fetches[f]:
             copy.wait()
-        for halo, corner, near, far, buf, n1, n2 in (
-            (ha, cabove, 1, 0, oa, 0, 1),
-            (hb, cbelow, 0, 1, ob, 1, 0),
+        for n, (halo, near, buf, n1, first) in enumerate(
+            ((above, 1, oa, 0, 0), (below, 0, ob, 1, rows - 2))
         ):
-            r1 = n1 if buf is oa else rows - 2 + n1
-            r2 = n2 if buf is oa else rows - 2 + n2
-
-            def octet(s, carry):
-                ks = pl.ds(pl.multiple_of(s * HALF, HALF), HALF)
-                ext = corner[f, ks, :]
-                ext_e, ext_w = pltpu.roll(ext, 1, axis=1), pltpu.roll(ext, LANES - 1, axis=1)
-                cur = halo[f, near, ks, 0:LANES]
-                west = ext_e
-                cur_e, cur_w = pltpu.roll(cur, 1, axis=1), pltpu.roll(cur, LANES - 1, axis=1)
-                for c in range(tiles):
-                    at = slice(c * LANES, (c + 1) * LANES)
-                    if c + 1 < tiles:
-                        nxt = halo[f, near, ks, (c + 1) * LANES : (c + 2) * LANES]
-                        nxt_e = pltpu.roll(nxt, 1, axis=1)
-                        nxt_w = pltpu.roll(nxt, LANES - 1, axis=1)
-                    else:
-                        nxt, nxt_e, nxt_w = ext, ext_e, ext_w
-                    around = jnp.where(initial, west, cur_e) + jnp.where(final, nxt_w, cur_w)
-                    lap = halo[f, far, ks, at] + 2.0 * around - 8.0 * cur
-                    buf[f, n1, ks, at] = buf[f, n1, ks, at] - bih[r1 : r1 + 1, at] * lap
-                    buf[f, n2, ks, at] = buf[f, n2, ks, at] - bih[r2 : r2 + 1, at] * cur
-                    west = cur_e
-                    cur, cur_e, cur_w = nxt, nxt_e, nxt_w
-                return carry
-
-            lax.fori_loop(0, levels // HALF, octet, 0)
+            n2 = 1 - n1
+            start = (2 * f + n) * levels
+            for m in range(steps):
+                at = slice(m * WIDE, (m + 1) * WIDE)
+                lap = halo[1 - near, f, :, at] + y[start : start + levels, at]
+                b1 = bih[first + n1 : first + n1 + 1, at]
+                b2 = bih[first + n2 : first + n2 + 1, at]
+                buf[f, n1, :, at] = buf[f, n1, :, at] - b1 * lap
+                buf[f, n2, :, at] = buf[f, n2, :, at] - b2 * halo[near, f, :, at]
         for copy in stores[f]:
             copy.start()
     for back in stores:
@@ -530,7 +648,7 @@
             copy.wait()
 
 
-def fix(base, above, below, cabove, cbelow, biharmonic):
+def fix(base, above, below, corners, biharmonic, matrix):
     fields, levels, rows, width = base.shape
     f32 = jnp.float32
     edge = pltpu.VMEM((fields, 2, levels, width), f32)
@@ -538,20 +656,19 @@
         fix_kernel,
         name="ocean_edges",
         out_shape=jax.ShapeDtypeStruct(base.shape, f32),
-        in_specs=[spec(HBM)] * 3 + [spec(VMEM)] * 3,
+        in_specs=[spec(HBM)] + [spec(VMEM)] * 5,
         out_specs=spec(HBM),
         input_output_aliases={0: 0},
         scratch_shapes=[
             edge,
             edge,
-            edge,
-            edge,
-            pltpu.SemaphoreType.DMA((6 * fields,)),
+            pltpu.VMEM((2 * fields * levels, width), f32),
+            pltpu.SemaphoreType.DMA((4 * fields,)),
             pltpu.SemaphoreType.DMA((4 * fields,)),
         ],
         compiler_params=pltpu.CompilerParams(vmem_limit_bytes=VMEM_BYTES),
         cost_estimate=cost(0, 3 * 4 * 4 * fields * levels * width),
-    )(base, above, below, cabove, cbelow, biharmonic)
+    )(base, above, below, corners, biharmonic, matrix)
 
 
 def per_device(
@@ -570,7 +687,7 @@
     n_tile = lax.axis_size("tile")
     n_grp = lax.axis_size("grp")
 
-    first, last, cols, ctop, cbottom = pack(ocean_state)
+    first, last, cols, matrix, mixing, forward, backward = pack(ocean_state)
 
     def shift(value, tile_step, grp_step):
         pairs = []
@@ -581,28 +698,32 @@
                     pairs.append((g * n_tile + t, target * n_tile + t + tile_step))
         return lax.ppermute(value, ("grp", "tile"), pairs)
 
-    lane = jnp.arange(LANES)
-
-    def around(value, tile_step, eastern):
-        west = shift(value, tile_step, 1)
+    def around(value):
+        west = shift(value, 0, 1)
         if n_grp == 2:
             return west
-        return jnp.where(eastern, shift(value, tile_step, -1), west)
+        return jnp.where(jnp.arange(LANES) < LANES // 2, shift(value, 0, -1), west)
 
     above = shift(last, 1, 0)
     below = shift(first, -1, 0)
-    cols = around(cols, 0, lane < LANES // 2)
-    cabove = around(cbottom, 1, lane < LANES // 2)
-    cbelow = around(ctop, -1, lane < LANES // 2)
+    cols = around(cols)
 
     ice_in = (ice_state, strength, ice_mass, ice_fraction, wind_stress, ice_count, ice_list)
-    surface = ocean_state[0:2, 0:1]
-    ice_out, stress_out = ice(*ice_in, surface)
+    ice_out, stress_out = ice(*ice_in, ocean_state, forward, backward)
 
     rows = (lax.axis_index("tile") * tile_rows + jnp.arange(tile_rows)).astype(jnp.float32) + 0.5
     coriolis = CORIOLIS * (2.0 * rows / (tile_rows * n_tile) - 1.0)
-    base = ocean(ocean_state, cols, biharmonic, prev_stress, coriolis)
-    ocean_out = fix(base, above, below, cabove, cbelow, biharmonic)
+
+    above, below, ice_out, stress_out = lax.optimization_barrier(
+        (above, below, ice_out, stress_out)
+    )
+
+    corners = ends(above, below)
+    corners, cols = lax.optimization_barrier((corners, cols))
+    corners = around(corners)
+
+    base = ocean(ocean_state, cols, biharmonic, prev_stress, coriolis, matrix, mixing)
+    ocean_out = fix(base, above, below, corners, biharmonic, matrix)
     return (ocean_out, ice_out, stress_out)
 
 

time: 65.1 us -> 61 us (0.937)
  starting transfers between devices: 15.4 us -> 8.6 us
  local copies, waits for them, and re-layouts: 3.81 us -> 6.99 us
    ppermute x5 -> x4, starting transfers between devices: 15.4 us -> 8.6 us  [shift(): return lax.ppermute(value, ('grp', 'tile'), pairs)]
    unnamed x22 -> x28, local copies, waits for them, and re-layouts: 2.75 us -> 6.99 us
    pallas_call x1, Pallas kernels: 5.36 us -> 3.12 us  [fix(): pl.pallas_call(fix_kernel, name='ocean_edges', out_shape=jax.ShapeDtypeSt...]
    pallas_call x1, Pallas kernels: 16.9 us -> 18 us  [ice(): pl.pallas_call(ice_kernel, name='ice_subcycles', out_shape=(jax.ShapeDtyp...]
    slice x1 -> x0, local copies, waits for them, and re-layouts: 1.06 us -> none  [per_device(): surface = ocean_state[0:2, 0:1]]
  transfers between devices with their start and end apart: 5 -> 4, of which waited for: 0 -> 0; matrix products, arithmetic and copies ran while one was open for 2% -> 0% of each run, Pallas kernels for 53% -> 60%
where the time goes in v3:
time: 61 us; the launch traced here: 60.4 us
  Pallas kernels  43.2 us (71%)
  starting transfers between devices  8.6 us (14%)
  local copies, waits for them, and re-layouts  6.99 us (11%)
  between operations  1.62 us (3%)
    pallas_call x1, Pallas kernels, ocean(): pl.pallas_call(main_kernel, name='ocean_tile', out_shape=jax.ShapeDtypeSt...  18 us
    pallas_call x1, Pallas kernels, ice(): pl.pallas_call(ice_kernel, name='ice_subcycles', out_shape=(jax.ShapeDtyp...  18 us
    ppermute x4, starting transfers between devices, shift(): return lax.ppermute(value, ('grp', 'tile'), pairs)  8.6 us
    unnamed x28, local copies, waits for them, and re-layouts  6.99 us
    pallas_call x1, Pallas kernels, pack(): pl.pallas_call(pack_kernel, name='pack_edges', out_shape=(jax.ShapeDtypeS...  4.1 us
    pallas_call x1, Pallas kernels, fix(): pl.pallas_call(fix_kernel, name='ocean_edges', out_shape=jax.ShapeDtypeSt...  3.12 us
  transfers between devices with their start and end apart: 4, of which 0 were waited for; matrix products, arithmetic and copies ran while one was open for 0% of the time, Pallas kernels for 60%

profile of v3, /device:TPU:24, one launch (start us, length us, event | category | flops | bytes accessed | tf_op | source)
XLA Modules:
  0.0 60.4 jit_solution(3804368812180229885)
XLA Ops:
  0.6 0.0 copy-start.13
  0.6 0.0 copy-start.3
  0.7 0.0 copy-start.4
  0.7 4.1 %pack_edges.1 = (f32[2,3,24,2048]{3,2,1,0:T(8,128)}, f32[2,3,24,2048]{3,2,1,0:T(8,128)}, f32[3,16,24,128]{3,2,1,0:T(8,128)}, bf16[768,512]{1,0:T(8,128)(2,1)S(1)...) custom-call(f32[3,24,16,2048]{3,2,1,0:T(8,128)} %x_hbm.1), custom_call_target="tpu_custom_call" | custom-call | bytes 4718592 | tf_op jit(solution)/shard_map/pack_edges/pallas_call | solution.py:154
  4.8 0.0 copy-start.7
  4.8 0.6 %copy-done.7 = bf16[256,256]{1,0:T(8,128)(2,1)} copy-done((bf16[256,256]{1,0:T(8,128)(2,1)}, bf16[256,256]{1,0:T(8,128)(2,1)S(1)}, u32[]{:S(2)}) %copy-start.7) | copy-done | bytes 131096
  5.4 0.7 %copy-done.9 = bf16[256,256]{1,0:T(8,128)(2,1)} copy-done((bf16[256,256]{1,0:T(8,128)(2,1)}, bf16[256,256]{1,0:T(8,128)(2,1)S(1)}, u32[]{:S(2)}) %copy-start.9) | copy-done | bytes 131096
  6.1 0.6 %copy-done.11 = bf16[96,192]{1,0:T(8,128)(2,1)} copy-done((bf16[96,192]{1,0:T(8,128)(2,1)}, bf16[96,192]{1,0:T(8,128)(2,1)S(1)}, u32[]{:S(2)}) %copy-start.11) | copy-done | bytes 36888
  6.7 1.9 %collective-permute-start = (f32[2,3,24,2048]{3,2,1,0:T(8,128)}, f32[2,3,24,2048]{3,2,1,0:T(8,128)S(1)}, u32[]{:S(2)}, u32[]{:S(2)}) collective-permute-start(f32[2,3,24,2048]{3,2,1,0:T(8,128)} %get-tuple-element.18), channel_id=1, source_target_pairs={{0,1},{1,2},{2,3},{3,4},{4,5},{5,6},{6,7},{7,8},{8,9},{9,10},{10,1... | collective-permute-start | bytes 3538952 | tf_op jit(solution)/shard_map/ppermute | solution.py:699
  8.6 4.5 %collective-permute-start.1 = (f32[2,3,24,2048]{3,2,1,0:T(8,128)}, f32[2,3,24,2048]{3,2,1,0:T(8,128)S(1)}, u32[]{:S(2)}, u32[]{:S(2)}) collective-permute-start(f32[2,3,24,2048]{3,2,1,0:T(8,128)} %get-tuple-element.19), channel_id=1, source_target_pairs={{1,0},{2,1},{3,2},{4,3},{5,4},{6,5},{7,6},{8,7},{9,8},{10,9},{11,1... | collective-permute-start | bytes 3538952 | tf_op jit(solution)/shard_map/ppermute | solution.py:699
  13.2 1.6 %collective-permute-start.2 = (f32[3,16,24,128]{3,2,1,0:T(8,128)}, f32[3,16,24,128]{3,2,1,0:T(8,128)}, u32[]{:S(2)}, u32[]{:S(2)}) collective-permute-start(f32[3,16,24,128]{3,2,1,0:T(8,128)} %get-tuple-element.26), channel_id=1, source_target_pairs={{0,16},{1,17},{2,18},{3,19},{4,20},{5,21},{6,22},{7,23},{8,24},{9,... | collective-permute-start | bytes 1769480 | tf_op jit(solution)/shard_map/ppermute | solution.py:699
  15.4 0.0 copy-done.13
  15.4 0.0 copy-done.3
  15.4 0.0 copy-done.4
  15.4 0.0 copy-start
  15.4 1.1 %copy-done = f32[5,16,2048]{2,1,0:T(8,128)S(1)} copy-done((f32[5,16,2048]{2,1,0:T(8,128)S(1)}, f32[5,16,2048]{2,1,0:T(8,128)}, u32[]{:S(2)}) %copy-start) | copy-done | bytes 655384
  16.5 0.9 %copy-done.5 = f32[16,2048]{1,0:T(8,128)S(1)} copy-done((f32[16,2048]{1,0:T(8,128)S(1)}, f32[16,2048]{1,0:T(8,128)}, u32[]{:S(2)}) %copy-start.5) | copy-done | bytes 131096
  17.4 0.9 %copy-done.6 = f32[16,2048]{1,0:T(8,128)S(1)} copy-done((f32[16,2048]{1,0:T(8,128)S(1)}, f32[16,2048]{1,0:T(8,128)}, u32[]{:S(2)}) %copy-start.6) | copy-done | bytes 131096
  18.3 0.9 %copy-done.8 = bf16[256,256]{1,0:T(8,128)(2,1)S(1)} copy-done((bf16[256,256]{1,0:T(8,128)(2,1)S(1)}, bf16[256,256]{1,0:T(8,128)(2,1)}, u32[]{:S(2)}) %copy-start.8) | copy-done | bytes 131096
  19.2 0.9 %copy-done.10 = bf16[256,256]{1,0:T(8,128)(2,1)S(1)} copy-done((bf16[256,256]{1,0:T(8,128)(2,1)S(1)}, bf16[256,256]{1,0:T(8,128)(2,1)}, u32[]{:S(2)}) %copy-start.10) | copy-done | bytes 131096
  20.1 18.0 %ice_subcycles.1 = (f32[5,16,2048]{2,1,0:T(8,128)}, f32[2,16,2048]{2,1,0:T(8,128)}) custom-call(s32[1]{0:T(128)S(6)} %copy.15.count, s32[1,16]{1,0:T(1,128)S(1)} %copy-done.13, f32[5,16,2048]{2,1,0:T(8,128)S(1)} %copy-done, f32[16,2048]{1,0:T(8,128)S(1)} %copy-done.4, f32[16,2048]{1,0:T(8,128)S(1)} %copy-done.5, f32[16,2048]{1,0:T(8,128)S(1)} %copy-done.6, ...), custom_call_target="tpu_custom_call" | custom-call | flops 104857600 | bytes 2883584 | tf_op jit(solution)/shard_map/ice_subcycles/pallas_call | solution.py:406
  38.1 0.0 collective-permute-done.above
  38.1 0.0 collective-permute-done.1.below
  38.1 0.0 copy-start.1
  38.1 0.0 copy-start.2
  38.2 0.0 collective-permute-done.2.cols
  38.2 0.6 collective-permute-start.3
  38.8 0.2 copy-done.1
  39.0 0.1 copy-done.2
  39.1 18.0 %ocean_tile.1.base = f32[3,24,16,2048]{3,2,1,0:T(8,128)} custom-call(f32[3,24,16,2048]{3,2,1,0:T(8,128)} %x_hbm.1, f32[3,16,24,128]{3,2,1,0:T(8,128)} %collective-permute-done.2.cols, f32[16,2048]{1,0:T(8,128)S(1)} %copy-done.1, f32[2,16,2048]{2,1,0:T(8,128)S(1)} %copy-done.2, f32[16]{0:T(128)S(1)} %add_multiply_fusion.cor, ...), custom_call_target="tpu_custom_call" | custom-call | flops 70778880 | bytes 18874368 | tf_op jit(solution)/shard_map/ocean_tile/pallas_call | solution.py:543
  57.1 0.0 collective-permute-done.3.corners
  57.1 3.1 %ocean_edges.1 = f32[3,24,16,2048]{3,2,1,0:T(8,128)} custom-call(f32[3,24,16,2048]{3,2,1,0:T(8,128)} %ocean_tile.1.base, f32[2,3,24,2048]{3,2,1,0:T(8,128)S(1)} %collective-permute-done.above, f32[2,3,24,2048]{3,2,1,0:T(8,128)S(1)} %collective-permute-done.1.below, ...), custom_call_target="tpu_custom_call", output_to_operand_aliasing={{}: (0, {})} | custom-call | bytes 7077888 | tf_op jit(solution)/shard_map/ocean_edges/pallas_call | solution.py:655
  (10 shorter events, 0.0 us)
Async XLA Ops:
  0.6 14.7 %copy-start.13 = (s32[1,16]{1,0:T(1,128)S(1)}, s32[1,16]{1,0:T(1,128)}, u32[]{:S(2)}) copy-start(s32[1,16]{1,0:T(1,128)} %listed.1) | copy-start | bytes 196
  0.6 14.7 %copy-start.3 = (f32[2,16,2048]{2,1,0:T(8,128)S(1)}, f32[2,16,2048]{2,1,0:T(8,128)}, u32[]{:S(2)}) copy-start(f32[2,16,2048]{2,1,0:T(8,128)} %wind_hbm.1) | copy-start | bytes 786436
  0.7 14.7 %copy-start.4 = (f32[16,2048]{1,0:T(8,128)S(1)}, f32[16,2048]{1,0:T(8,128)}, u32[]{:S(2)}) copy-start(f32[16,2048]{1,0:T(8,128)} %strength_hbm.1) | copy-start | bytes 393220
  4.8 0.7 %copy-start.7 = (bf16[256,256]{1,0:T(8,128)(2,1)}, bf16[256,256]{1,0:T(8,128)(2,1)S(1)}, u32[]{:S(2)}) copy-start(bf16[256,256]{1,0:T(8,128)(2,1)S(1)} %get-tuple-element.20.forward) | copy-start | bytes 393220
  5.4 0.7 %copy-start.9 = (bf16[256,256]{1,0:T(8,128)(2,1)}, bf16[256,256]{1,0:T(8,128)(2,1)S(1)}, u32[]{:S(2)}) copy-start(bf16[256,256]{1,0:T(8,128)(2,1)S(1)} %get-tuple-element.21.backward) | copy-start | bytes 393220
  6.1 0.6 %copy-start.11 = (bf16[96,192]{1,0:T(8,128)(2,1)}, bf16[96,192]{1,0:T(8,128)(2,1)S(1)}, u32[]{:S(2)}) copy-start(bf16[96,192]{1,0:T(8,128)(2,1)S(1)} %get-tuple-element.29.mixing) | copy-start | bytes 110596
  6.7 31.4 %collective-permute-start = (f32[2,3,24,2048]{3,2,1,0:T(8,128)}, f32[2,3,24,2048]{3,2,1,0:T(8,128)S(1)}, u32[]{:S(2)}, u32[]{:S(2)}) collective-permute-start(f32[2,3,24,2048]{3,2,1,0:T(8,128)} %get-tuple-element.18), channel_id=1, source_target_pairs={{0,1},{1,2},{2,3},{3,4},{4,5},{5,6},{6,7},{7,8},{8,9},{9,10},{10,1... | collective-permute-start | bytes 3538952 | tf_op jit(solution)/shard_map/ppermute | solution.py:699
  8.6 29.5 %collective-permute-start.1 = (f32[2,3,24,2048]{3,2,1,0:T(8,128)}, f32[2,3,24,2048]{3,2,1,0:T(8,128)S(1)}, u32[]{:S(2)}, u32[]{:S(2)}) collective-permute-start(f32[2,3,24,2048]{3,2,1,0:T(8,128)} %get-tuple-element.19), channel_id=1, source_target_pairs={{1,0},{2,1},{3,2},{4,3},{5,4},{6,5},{7,6},{8,7},{9,8},{10,9},{11,1... | collective-permute-start | bytes 3538952 | tf_op jit(solution)/shard_map/ppermute | solution.py:699
  13.2 25.0 %collective-permute-start.2 = (f32[3,16,24,128]{3,2,1,0:T(8,128)}, f32[3,16,24,128]{3,2,1,0:T(8,128)}, u32[]{:S(2)}, u32[]{:S(2)}) collective-permute-start(f32[3,16,24,128]{3,2,1,0:T(8,128)} %get-tuple-element.26), channel_id=1, source_target_pairs={{0,16},{1,17},{2,18},{3,19},{4,20},{5,21},{6,22},{7,23},{8,24},{9,... | collective-permute-start | bytes 1769480 | tf_op jit(solution)/shard_map/ppermute | solution.py:699
  15.4 1.1 %copy-start = (f32[5,16,2048]{2,1,0:T(8,128)S(1)}, f32[5,16,2048]{2,1,0:T(8,128)}, u32[]{:S(2)}) copy-start(f32[5,16,2048]{2,1,0:T(8,128)} %state_hbm.1) | copy-start | bytes 1966084
  16.5 0.9 %copy-start.5 = (f32[16,2048]{1,0:T(8,128)S(1)}, f32[16,2048]{1,0:T(8,128)}, u32[]{:S(2)}) copy-start(f32[16,2048]{1,0:T(8,128)} %mass_hbm.1) | copy-start | bytes 393220
  17.4 0.9 %copy-start.6 = (f32[16,2048]{1,0:T(8,128)S(1)}, f32[16,2048]{1,0:T(8,128)}, u32[]{:S(2)}) copy-start(f32[16,2048]{1,0:T(8,128)} %fraction_hbm.1) | copy-start | bytes 393220
  18.3 0.9 %copy-start.8 = (bf16[256,256]{1,0:T(8,128)(2,1)S(1)}, bf16[256,256]{1,0:T(8,128)(2,1)}, u32[]{:S(2)}) copy-start(bf16[256,256]{1,0:T(8,128)(2,1)} %copy-done.7) | copy-start | bytes 393220
  19.2 0.9 %copy-start.10 = (bf16[256,256]{1,0:T(8,128)(2,1)S(1)}, bf16[256,256]{1,0:T(8,128)(2,1)}, u32[]{:S(2)}) copy-start(bf16[256,256]{1,0:T(8,128)(2,1)} %copy-done.9) | copy-start | bytes 393220
  38.1 0.9 %copy-start.1 = (f32[16,2048]{1,0:T(8,128)S(1)}, f32[16,2048]{1,0:T(8,128)}, u32[]{:S(2)}) copy-start(f32[16,2048]{1,0:T(8,128)} %bih.3) | copy-start | bytes 393220
  38.1 1.0 %copy-start.2 = (f32[2,16,2048]{2,1,0:T(8,128)S(1)}, f32[2,16,2048]{2,1,0:T(8,128)}, u32[]{:S(2)}) copy-start(f32[2,16,2048]{2,1,0:T(8,128)} %prev.1) | copy-start | bytes 786436
  38.1 1.0 %copy-start.12 = (bf16[96,192]{1,0:T(8,128)(2,1)S(1)}, bf16[96,192]{1,0:T(8,128)(2,1)}, u32[]{:S(2)}) copy-start(bf16[96,192]{1,0:T(8,128)(2,1)} %copy-done.11) | copy-start | bytes 110596
  38.2 18.9 %collective-permute-start.3 = (f32[2,3,24,128]{3,2,1,0:T(8,128)S(1)}, f32[2,3,24,128]{3,2,1,0:T(8,128)S(1)}, u32[]{:S(2)}, u32[]{:S(2)}) collective-permute-start(f32[2,3,24,128]{3,2,1,0:T(8,128)S(1)} %received_ends.1), channel_id=1, source_target_pairs={{0,16},{1,17},{2,18},{3,19},{4,20},{5,21},{6,22},{7,23},{8,24},{9,... | collective-permute-start | bytes 221192 | tf_op jit(solution)/shard_map/ppermute | solution.py:699

commit v4 on v3

--- a/solution.py
+++ b/solution.py
@@ -20,6 +20,7 @@
 
 DECAY = 1.0 / (1.0 + RELAX)
 VMEM_BYTES = 48 * 1024 * 1024
+SMALL_BYTES = 24 * 1024 * 1024
 
 HBM = pltpu.HBM
 VMEM = pltpu.VMEM
@@ -39,7 +40,6 @@
 
 
 WIDE = 256
-FETCH = 512
 GROUP = 4
 
 
@@ -105,13 +105,10 @@
 
 def pack_kernel(
     x,
+    flat,
     first,
     last,
     cols,
-    matrix,
-    mixing,
-    forward,
-    backward,
     left,
     right,
     row_sem,
@@ -124,27 +121,27 @@
             copies.append(
                 pltpu.make_async_copy(x.at[:, :, row, :], to.at[j], row_sem.at[side, j])
             )
-    col_copies = []
-    for r in range(rows):
-        for side, (to, start) in enumerate(((left, 0), (right, width - LANES))):
-            col_copies.append(
-                pltpu.make_async_copy(
-                    x.at[:, :, r, start : start + LANES], to.at[:, r], col_sem.at[side, r]
-                )
-            )
+    col_copies = [
+        pltpu.make_async_copy(flat.at[:, :, start : start + LANES], to, col_sem.at[side])
+        for side, (to, start) in enumerate(((left, 0), (right, width - LANES)))
+    ]
     for copy in copies + col_copies:
         copy.start()
-    make_columns(matrix)
-    make_mixing(mixing, x.shape[1])
-    make_orders(forward, backward)
     for copy in col_copies:
         copy.wait()
-    lane = lax.broadcasted_iota(jnp.int32, left.shape[2:], 1)
+    lane = lax.broadcasted_iota(jnp.int32, cols.shape[2:], 1)
+    levels = x.shape[1]
     for f in range(left.shape[0]):
         for r in range(rows):
-            cols[f, r] = jnp.where(lane < LANES // 2, left[f, r], right[f, r])
+            at = pl.ds(r, levels, stride=rows)
+            cols[f, r] = jnp.where(lane < LANES // 2, left[f, at, :], right[f, at, :])
     for copy in copies:
         copy.wait()
+
+
+def flatten(array):
+    fields, levels, rows, width = array.shape
+    return array.reshape(fields, levels * rows, width)
 
 
 def pack(ocean_state):
@@ -158,22 +155,18 @@
             jax.ShapeDtypeStruct((2, fields, levels, width), f32),
             jax.ShapeDtypeStruct((2, fields, levels, width), f32),
             jax.ShapeDtypeStruct(edge, f32),
-            jax.ShapeDtypeStruct((2 * (WIDE + LANES), 2 * WIDE), jnp.bfloat16),
-            jax.ShapeDtypeStruct((GROUP * levels, 2 * GROUP * levels), jnp.bfloat16),
-            jax.ShapeDtypeStruct((2 * BX, 2 * BX), jnp.bfloat16),
-            jax.ShapeDtypeStruct((2 * BX, 2 * BX), jnp.bfloat16),
         ),
-        in_specs=[spec(HBM)],
-        out_specs=(spec(VMEM),) * 7,
+        in_specs=[spec(HBM)] * 2,
+        out_specs=(spec(VMEM),) * 3,
         scratch_shapes=[
-            pltpu.VMEM(edge, f32),
-            pltpu.VMEM(edge, f32),
+            pltpu.VMEM((fields, levels * rows, LANES), f32),
+            pltpu.VMEM((fields, levels * rows, LANES), f32),
             pltpu.SemaphoreType.DMA((2, 2)),
-            pltpu.SemaphoreType.DMA((2, rows)),
+            pltpu.SemaphoreType.DMA((2,)),
         ],
         compiler_params=pltpu.CompilerParams(vmem_limit_bytes=VMEM_BYTES),
         cost_estimate=cost(0, 4 * 2 * 4 * fields * levels * width),
-    )(ocean_state)
+    )(ocean_state, flatten(ocean_state))
 
 
 def split(q, parts):
@@ -202,10 +195,10 @@
     fraction_hbm,
     wind_hbm,
     ocean_hbm,
+    ice_out,
+    stress_out,
     forward,
     backward,
-    ice_out,
-    stress_out,
     state,
     strength,
     mass,
@@ -249,6 +242,7 @@
     for copy in copies:
         copy.start()
 
+    make_orders(forward, backward)
     for s in range(blocks):
         covered[listed[0, s]] = jnp.where(s < count[0], 1, 0)
 
@@ -399,7 +393,7 @@
                 stress_out[n, :, at] = jnp.where(keep, merged, w)
 
 
-def ice(ice_state, strength, ice_mass, ice_fraction, wind_stress, ice_count, ice_list, ocean_state, forward, backward):
+def ice(ice_state, strength, ice_mass, ice_fraction, wind_stress, ice_count, ice_list, ocean_state):
     rows, width = ice_mass.shape
     f32 = jnp.float32
     cells = (rows * width // BX, BX)
@@ -410,9 +404,11 @@
             jax.ShapeDtypeStruct(ice_state.shape, f32),
             jax.ShapeDtypeStruct(wind_stress.shape, f32),
         ),
-        in_specs=[spec(SMEM)] * 2 + [spec(HBM)] * 6 + [spec(VMEM)] * 2,
+        in_specs=[spec(SMEM)] * 2 + [spec(HBM)] * 6,
         out_specs=(spec(VMEM), spec(VMEM)),
         scratch_shapes=[
+            pltpu.VMEM((2 * BX, 2 * BX), jnp.bfloat16),
+            pltpu.VMEM((2 * BX, 2 * BX), jnp.bfloat16),
             pltpu.VMEM(ice_state.shape, f32),
             pltpu.VMEM((rows, width), f32),
             pltpu.VMEM((rows, width), f32),
@@ -434,36 +430,43 @@
         ice_fraction,
         wind_stress,
         ocean_state,
-        forward,
-        backward,
     )
 
 
 def main_kernel(
-    x_hbm, cols, bih, prev, cor, matrix, mixing, out_hbm, x, out, y, z, in_sem, out_sem
+    x_hbm,
+    cols,
+    bih,
+    prev,
+    cor,
+    out_hbm,
+    x,
+    raw,
+    out,
+    y,
+    z,
+    matrix,
+    mixing,
+    in_sem,
+    out_sem,
 ):
     fields, rows, levels, width = x.shape
     steps = width // WIDE
-    spans = width // FETCH
-    each = FETCH // WIDE
-
-    def fetches(s):
-        at = slice(s * FETCH, (s + 1) * FETCH)
-        return [
-            pltpu.make_async_copy(x_hbm.at[:, :, r, at], x.at[:, r, :, at], in_sem.at[s, r])
-            for r in range(rows)
-        ]
-
-    def stores(s):
-        at = slice(s * FETCH, (s + 1) * FETCH)
-        return [
-            pltpu.make_async_copy(out.at[:, r, :, at], out_hbm.at[:, :, r, at], out_sem.at[s, r])
-            for r in range(rows)
-        ]
-
-    for s in range(spans):
-        for copy in fetches(s):
-            copy.start()
+    tiles = width // LANES
+    each = WIDE // LANES
+
+    def fetch(c):
+        at = slice(c * LANES, (c + 1) * LANES)
+        return pltpu.make_async_copy(x_hbm.at[:, :, at], raw.at[:, c], in_sem.at[c])
+
+    def store(c):
+        at = slice(c * LANES, (c + 1) * LANES)
+        return pltpu.make_async_copy(out.at[:, c], out_hbm.at[:, :, at], out_sem.at[c])
+
+    for c in range(tiles):
+        fetch(c).start()
+    make_columns(matrix)
+    make_mixing(mixing, levels)
 
     level = lax.broadcasted_iota(jnp.int32, (HALF, WIDE), 0)
     lane = lax.broadcasted_iota(jnp.int32, (rows * levels, LANES), 1)
@@ -473,10 +476,12 @@
 
     waited = 0
     for m in range(steps):
-        need = min((m + 1) // each, spans - 1)
-        while waited <= need:
-            for copy in fetches(waited):
-                copy.wait()
+        while waited < min((m + 1) * each + 1, tiles):
+            fetch(waited).wait()
+            to = slice(waited * LANES, (waited + 1) * LANES)
+            for f in range(fields):
+                for r in range(rows):
+                    x[f, r, :, to] = raw[f, waited, pl.ds(r, levels, stride=rows), :]
             waited += 1
         at = slice(m * WIDE, (m + 1) * WIDE)
         for f in range(fields):
@@ -523,40 +528,44 @@
                     res = res + cor[r] * x[1, r, :, at]
                 elif f == 1:
                     res = res - cor[r] * x[0, r, :, at]
-                out[f, r, :, at] = res
                 if f < 2:
-                    out[f, r, 0:HALF, at] = res[0:HALF] + jnp.where(
-                        level == 0, prev[f, r : r + 1, at], 0.0
-                    )
-        if m % each == each - 1:
-            for copy in stores(m // each):
-                copy.start()
-    for s in range(spans):
-        for copy in stores(s):
-            copy.wait()
-
-
-def ocean(ocean_state, cols, biharmonic, prev_stress, coriolis, matrix, mixing):
+                    head = res[0:HALF] + jnp.where(level == 0, prev[f, r : r + 1, at], 0.0)
+                    res = jnp.concatenate([head, res[HALF:]], axis=0)
+                for n in range(each):
+                    out[f, m * each + n, pl.ds(r, levels, stride=rows), :] = res[
+                        :, n * LANES : (n + 1) * LANES
+                    ]
+        for n in range(each):
+            store(m * each + n).start()
+    for c in range(tiles):
+        store(c).wait()
+
+
+def ocean(ocean_state, cols, biharmonic, prev_stress, coriolis):
     fields, levels, rows, width = ocean_state.shape
     f32 = jnp.float32
-    held = (fields, rows, levels, width)
-    return pl.pallas_call(
+    tiled = (fields, width // LANES, levels * rows, LANES)
+    base = pl.pallas_call(
         main_kernel,
         name="ocean_tile",
-        out_shape=jax.ShapeDtypeStruct(ocean_state.shape, f32),
-        in_specs=[spec(HBM)] + [spec(VMEM)] * 3 + [spec(SMEM)] + [spec(VMEM)] * 2,
+        out_shape=jax.ShapeDtypeStruct((fields, levels * rows, width), f32),
+        in_specs=[spec(HBM)] + [spec(VMEM)] * 3 + [spec(SMEM)],
         out_specs=spec(HBM),
         scratch_shapes=[
-            pltpu.VMEM(held, f32),
-            pltpu.VMEM(held, f32),
+            pltpu.VMEM((fields, rows, levels, width), f32),
+            pltpu.VMEM(tiled, f32),
+            pltpu.VMEM(tiled, f32),
             pltpu.VMEM((2, rows * levels, 2 * WIDE), f32),
             pltpu.VMEM((2, rows * levels, WIDE), f32),
-            pltpu.SemaphoreType.DMA((width // FETCH, rows)),
-            pltpu.SemaphoreType.DMA((width // FETCH, rows)),
+            pltpu.VMEM((2 * (WIDE + LANES), 2 * WIDE), jnp.bfloat16),
+            pltpu.VMEM((GROUP * levels, 2 * GROUP * levels), jnp.bfloat16),
+            pltpu.SemaphoreType.DMA((width // LANES,)),
+            pltpu.SemaphoreType.DMA((width // LANES,)),
         ],
         compiler_params=pltpu.CompilerParams(vmem_limit_bytes=VMEM_BYTES),
         cost_estimate=cost(30 * ocean_state.size, 8 * ocean_state.size),
-    )(ocean_state, cols, biharmonic, prev_stress, coriolis, matrix, mixing)
+    )(flatten(ocean_state), cols, biharmonic, prev_stress, coriolis)
+    return base.reshape(ocean_state.shape)
 
 
 def ends_kernel(above, below, out):
@@ -579,11 +588,11 @@
         out_shape=jax.ShapeDtypeStruct((2, fields, levels, LANES), jnp.float32),
         in_specs=[spec(VMEM)] * 2,
         out_specs=spec(VMEM),
-        compiler_params=pltpu.CompilerParams(vmem_limit_bytes=VMEM_BYTES),
+        compiler_params=pltpu.CompilerParams(vmem_limit_bytes=SMALL_BYTES),
     )(above, below)
 
 
-def fix_kernel(base, above, below, corners, bih, matrix, out, oa, ob, y, in_sem, out_sem):
+def fix_kernel(base, above, below, corners, bih, out, oa, ob, y, matrix, in_sem, out_sem):
     _, fields, levels, width = above.shape
     rows = base.shape[2]
     steps = width // WIDE
@@ -604,6 +613,7 @@
         for copy in mine:
             copy.start()
 
+    make_columns(matrix)
     sides = ((above, 1), (below, 0))
     height = 2 * fields * levels
     lane = lax.broadcasted_iota(jnp.int32, (height, LANES), 1)
@@ -648,7 +658,7 @@
             copy.wait()
 
 
-def fix(base, above, below, corners, biharmonic, matrix):
+def fix(base, above, below, corners, biharmonic):
     fields, levels, rows, width = base.shape
     f32 = jnp.float32
     edge = pltpu.VMEM((fields, 2, levels, width), f32)
@@ -656,19 +666,20 @@
         fix_kernel,
         name="ocean_edges",
         out_shape=jax.ShapeDtypeStruct(base.shape, f32),
-        in_specs=[spec(HBM)] + [spec(VMEM)] * 5,
+        in_specs=[spec(HBM)] + [spec(VMEM)] * 4,
         out_specs=spec(HBM),
         input_output_aliases={0: 0},
         scratch_shapes=[
             edge,
             edge,
             pltpu.VMEM((2 * fields * levels, width), f32),
+            pltpu.VMEM((2 * (WIDE + LANES), 2 * WIDE), jnp.bfloat16),
             pltpu.SemaphoreType.DMA((4 * fields,)),
             pltpu.SemaphoreType.DMA((4 * fields,)),
         ],
-        compiler_params=pltpu.CompilerParams(vmem_limit_bytes=VMEM_BYTES),
+        compiler_params=pltpu.CompilerParams(vmem_limit_bytes=SMALL_BYTES),
         cost_estimate=cost(0, 3 * 4 * 4 * fields * levels * width),
-    )(base, above, below, corners, biharmonic, matrix)
+    )(base, above, below, corners, biharmonic)
 
 
 def per_device(
@@ -687,7 +698,7 @@
     n_tile = lax.axis_size("tile")
     n_grp = lax.axis_size("grp")
 
-    first, last, cols, matrix, mixing, forward, backward = pack(ocean_state)
+    first, last, cols = pack(ocean_state)
 
     def shift(value, tile_step, grp_step):
         pairs = []
@@ -709,21 +720,17 @@
     cols = around(cols)
 
     ice_in = (ice_state, strength, ice_mass, ice_fraction, wind_stress, ice_count, ice_list)
-    ice_out, stress_out = ice(*ice_in, ocean_state, forward, backward)
+    ice_out, stress_out = ice(*ice_in, ocean_state)
 
     rows = (lax.axis_index("tile") * tile_rows + jnp.arange(tile_rows)).astype(jnp.float32) + 0.5
     coriolis = CORIOLIS * (2.0 * rows / (tile_rows * n_tile) - 1.0)
 
-    above, below, ice_out, stress_out = lax.optimization_barrier(
-        (above, below, ice_out, stress_out)
-    )
-
-    corners = ends(above, below)
-    corners, cols = lax.optimization_barrier((corners, cols))
-    corners = around(corners)
-
-    base = ocean(ocean_state, cols, biharmonic, prev_stress, coriolis, matrix, mixing)
-    ocean_out = fix(base, above, below, corners, biharmonic, matrix)
+    cols, ice_out, stress_out = lax.optimization_barrier((cols, ice_out, stress_out))
+    base = ocean(ocean_state, cols, biharmonic, prev_stress, coriolis)
+
+    above, below, base = lax.optimization_barrier((above, below, base))
+    corners = around(ends(above, below))
+    ocean_out = fix(base, above, below, corners, biharmonic)
     return (ocean_out, ice_out, stress_out)
 
 

time: 61 us -> 59.9 us (0.982)
  local copies, waits for them, and re-layouts: 6.99 us -> 0.93 us
  waiting for transfers between devices: 0.01 us -> 3.81 us
  Pallas kernels: 43.2 us -> 44.6 us
    unnamed x28 -> x16, local copies, waits for them, and re-layouts: 6.99 us -> 0.93 us
    ppermute x4, waiting for transfers between devices: 0.01 us -> 3.81 us  [shift(): return lax.ppermute(value, ('grp', 'tile'), pairs)]
    pallas_call x1, Pallas kernels: 18 us -> 19.4 us  [ocean(): pl.pallas_call(main_kernel, name='ocean_tile', out_shape=jax.ShapeDtypeSt...]
  transfers between devices with their start and end apart: 4 -> 4, of which waited for: 0 -> 1; matrix products, arithmetic and copies ran while one was open for 0% -> 0% of each run, Pallas kernels for 60% -> 63%
where the time goes in v4:
time: 59.9 us; the launch traced here: 59.6 us
  Pallas kernels  44.6 us (74%)
  starting transfers between devices  8.63 us (14%)
  waiting for transfers between devices  3.81 us (6%)
  between operations  1.65 us (3%)
  local copies, waits for them, and re-layouts  0.93 us (2%)
    pallas_call x1, Pallas kernels, ocean(): pl.pallas_call(main_kernel, name='ocean_tile', out_shape=jax.ShapeDtypeSt...  19.4 us
    pallas_call x1, Pallas kernels, ice(): pl.pallas_call(ice_kernel, name='ice_subcycles', out_shape=(jax.ShapeDtyp...  18 us
    ppermute x4, starting transfers between devices, shift(): return lax.ppermute(value, ('grp', 'tile'), pairs)  8.63 us
    pallas_call x1, Pallas kernels, pack(): pl.pallas_call(pack_kernel, name='pack_edges', out_shape=(jax.ShapeDtypeS...  4.12 us
    ppermute x4, waiting for transfers between devices, shift(): return lax.ppermute(value, ('grp', 'tile'), pairs)  3.81 us
    pallas_call x1, Pallas kernels, fix(): pl.pallas_call(fix_kernel, name='ocean_edges', out_shape=jax.ShapeDtypeSt...  3.13 us
  transfers between devices with their start and end apart: 4, of which 1 were waited for; matrix products, arithmetic and copies ran while one was open for 0% of the time, Pallas kernels for 63%

profile of v4, /device:TPU:24, one launch (start us, length us, event | category | flops | bytes accessed | tf_op | source)
XLA Modules:
  0.0 59.6 jit_solution(11895412190618520353)
XLA Ops:
  0.6 0.0 copy-start
  0.6 0.0 copy-start.3
  0.7 0.0 copy-start.4
  0.7 0.0 copy-start.5
  0.7 0.0 copy-start.7
  0.7 4.1 %pack_edges.1 = (f32[2,3,24,2048]{3,2,1,0:T(8,128)}, f32[2,3,24,2048]{3,2,1,0:T(8,128)}, f32[3,16,24,128]{3,2,1,0:T(8,128)}) custom-call(f32[3,24,16,2048]{3,2,1,0:T(8,128)} %ocean_hbm.1, f32[3,384,2048]{2,1,0:T(8,128)} %bitcast.2), custom_call_target="tpu_custom_call" | custom-call | bytes 4718592 | tf_op jit(solution)/shard_map/pack_edges/pallas_call | solution.py:151
  4.8 1.9 %collective-permute-start = (f32[2,3,24,2048]{3,2,1,0:T(8,128)}, f32[2,3,24,2048]{3,2,1,0:T(8,128)S(1)}, u32[]{:S(2)}, u32[]{:S(2)}) collective-permute-start(f32[2,3,24,2048]{3,2,1,0:T(8,128)} %get-tuple-element.14), channel_id=1, source_target_pairs={{0,1},{1,2},{2,3},{3,4},{4,5},{5,6},{6,7},{7,8},{8,9},{9,10},{10,1... | collective-permute-start | bytes 3538952 | tf_op jit(solution)/shard_map/ppermute | solution.py:710
  6.7 4.5 %collective-permute-start.1 = (f32[2,3,24,2048]{3,2,1,0:T(8,128)}, f32[2,3,24,2048]{3,2,1,0:T(8,128)S(1)}, u32[]{:S(2)}, u32[]{:S(2)}) collective-permute-start(f32[2,3,24,2048]{3,2,1,0:T(8,128)} %get-tuple-element.15), channel_id=1, source_target_pairs={{1,0},{2,1},{3,2},{4,3},{5,4},{6,5},{7,6},{8,7},{9,8},{10,9},{11,1... | collective-permute-start | bytes 3538952 | tf_op jit(solution)/shard_map/ppermute | solution.py:710
  11.3 1.6 %collective-permute-start.2 = (f32[3,16,24,128]{3,2,1,0:T(8,128)}, f32[3,16,24,128]{3,2,1,0:T(8,128)}, u32[]{:S(2)}, u32[]{:S(2)}) collective-permute-start(f32[3,16,24,128]{3,2,1,0:T(8,128)} %get-tuple-element.16), channel_id=1, source_target_pairs={{0,16},{1,17},{2,18},{3,19},{4,20},{5,21},{6,22},{7,23},{8,24},{9,... | collective-permute-start | bytes 1769480 | tf_op jit(solution)/shard_map/ppermute | solution.py:710
  13.5 0.0 copy-done
  13.5 0.0 copy-done.3
  13.5 0.0 copy-done.4
  13.5 0.0 copy-done.5
  13.5 0.0 copy-done.7
  13.5 0.0 copy-start.6
  13.6 0.9 %copy-done.6 = f32[16,2048]{1,0:T(8,128)S(1)} copy-done((f32[16,2048]{1,0:T(8,128)S(1)}, f32[16,2048]{1,0:T(8,128)}, u32[]{:S(2)}) %copy-start.6) | copy-done | bytes 131096
  14.4 0.0 copy-start.1
  14.5 0.0 copy-start.2
  14.5 18.0 %ice_subcycles.1 = (f32[5,16,2048]{2,1,0:T(8,128)}, f32[2,16,2048]{2,1,0:T(8,128)}) custom-call(s32[1]{0:T(128)S(6)} %copy.15.count, s32[1,16]{1,0:T(1,128)S(1)} %copy-done.7, f32[5,16,2048]{2,1,0:T(8,128)S(1)} %copy-done, f32[16,2048]{1,0:T(8,128)S(1)} %copy-done.4, f32[16,2048]{1,0:T(8,128)S(1)} %copy-done.5, f32[16,2048]{1,0:T(8,128)S(1)} %copy-done.6, ...), custom_call_target="tpu_custom_call" | custom-call | flops 104857600 | bytes 2883584 | tf_op jit(solution)/shard_map/ice_subcycles/pallas_call | solution.py:400
  32.4 0.0 collective-permute-done.2.cols
  32.5 0.0 copy-done.1
  32.5 0.0 copy-done.2
  32.5 19.4 %ocean_tile.1 = f32[3,384,2048]{2,1,0:T(8,128)} custom-call(f32[3,384,2048]{2,1,0:T(8,128)} %bitcast.3, f32[3,16,24,128]{3,2,1,0:T(8,128)} %collective-permute-done.2.cols, f32[16,2048]{1,0:T(8,128)S(1)} %copy-done.1, f32[2,16,2048]{2,1,0:T(8,128)S(1)} %copy-done.2, f32[16]{0:T(128)S(1)} %add_multiply_fusion.cor), custom_call_target="tpu_custom_call" | custom-call | flops 70778880 | bytes 18874368 | tf_op jit(solution)/shard_map/ocean_tile/pallas_call | solution.py:548
  51.9 0.0 collective-permute-done.above
  51.9 0.0 collective-permute-done.1.below
  51.9 0.6 %collective-permute-start.3 = (f32[2,3,24,128]{3,2,1,0:T(8,128)S(1)}, f32[2,3,24,128]{3,2,1,0:T(8,128)S(1)}, u32[]{:S(2)}, u32[]{:S(2)}) collective-permute-start(f32[2,3,24,128]{3,2,1,0:T(8,128)S(1)} %received_ends.1), channel_id=1, source_target_pairs={{0,16},{1,17},{2,18},{3,19},{4,20},{5,21},{6,22},{7,23},{8,24},{9,... | collective-permute-start | bytes 221192 | tf_op jit(solution)/shard_map/ppermute | solution.py:710
  52.5 3.8 %collective-permute-done.3.corners = f32[2,3,24,128]{3,2,1,0:T(8,128)S(1)} collective-permute-done((f32[2,3,24,128]{3,2,1,0:T(8,128)S(1)}, f32[2,3,24,128]{3,2,1,0:T(8,128)S(1)}, u32[]{:S(2)}, u32[]{:S(2)}) %collective-permute-start.3) | collective-permute-done | bytes 73760 | tf_op jit(solution)/shard_map/ppermute | solution.py:710
  56.3 3.1 %ocean_edges.1 = f32[3,24,16,2048]{3,2,1,0:T(8,128)} custom-call(f32[3,24,16,2048]{3,2,1,0:T(8,128)} %bitcast.4, f32[2,3,24,2048]{3,2,1,0:T(8,128)S(1)} %collective-permute-done.above, f32[2,3,24,2048]{3,2,1,0:T(8,128)S(1)} %collective-permute-done.1.below, f32[2,3,24,128]{3,2,1,0:T(8,128)S(1)} %collective-permute-done.3.corners, ...), custom_call_target="tpu_custom_call", output_to_operand_aliasing={{}: (0, {})} | custom-call | bytes 7077888 | tf_op jit(solution)/shard_map/ocean_edges/pallas_call | solution.py:665
  (2 shorter events, 0.0 us)
Async XLA Ops:
  0.6 12.9 %copy-start = (f32[5,16,2048]{2,1,0:T(8,128)S(1)}, f32[5,16,2048]{2,1,0:T(8,128)}, u32[]{:S(2)}) copy-start(f32[5,16,2048]{2,1,0:T(8,128)} %state_hbm.1) | copy-start | bytes 1966084
  0.6 12.9 %copy-start.3 = (f32[2,16,2048]{2,1,0:T(8,128)S(1)}, f32[2,16,2048]{2,1,0:T(8,128)}, u32[]{:S(2)}) copy-start(f32[2,16,2048]{2,1,0:T(8,128)} %wind_hbm.1) | copy-start | bytes 786436
  0.7 12.9 %copy-start.4 = (f32[16,2048]{1,0:T(8,128)S(1)}, f32[16,2048]{1,0:T(8,128)}, u32[]{:S(2)}) copy-start(f32[16,2048]{1,0:T(8,128)} %strength_hbm.1) | copy-start | bytes 393220
  0.7 12.9 %copy-start.5 = (f32[16,2048]{1,0:T(8,128)S(1)}, f32[16,2048]{1,0:T(8,128)}, u32[]{:S(2)}) copy-start(f32[16,2048]{1,0:T(8,128)} %mass_hbm.1) | copy-start | bytes 393220
  0.7 12.9 %copy-start.7 = (s32[1,16]{1,0:T(1,128)S(1)}, s32[1,16]{1,0:T(1,128)}, u32[]{:S(2)}) copy-start(s32[1,16]{1,0:T(1,128)} %listed.1) | copy-start | bytes 196
  4.8 47.1 %collective-permute-start = (f32[2,3,24,2048]{3,2,1,0:T(8,128)}, f32[2,3,24,2048]{3,2,1,0:T(8,128)S(1)}, u32[]{:S(2)}, u32[]{:S(2)}) collective-permute-start(f32[2,3,24,2048]{3,2,1,0:T(8,128)} %get-tuple-element.14), channel_id=1, source_target_pairs={{0,1},{1,2},{2,3},{3,4},{4,5},{5,6},{6,7},{7,8},{8,9},{9,10},{10,1... | collective-permute-start | bytes 3538952 | tf_op jit(solution)/shard_map/ppermute | solution.py:710
  6.7 45.1 %collective-permute-start.1 = (f32[2,3,24,2048]{3,2,1,0:T(8,128)}, f32[2,3,24,2048]{3,2,1,0:T(8,128)S(1)}, u32[]{:S(2)}, u32[]{:S(2)}) collective-permute-start(f32[2,3,24,2048]{3,2,1,0:T(8,128)} %get-tuple-element.15), channel_id=1, source_target_pairs={{1,0},{2,1},{3,2},{4,3},{5,4},{6,5},{7,6},{8,7},{9,8},{10,9},{11,1... | collective-permute-start | bytes 3538952 | tf_op jit(solution)/shard_map/ppermute | solution.py:710
  11.3 21.2 %collective-permute-start.2 = (f32[3,16,24,128]{3,2,1,0:T(8,128)}, f32[3,16,24,128]{3,2,1,0:T(8,128)}, u32[]{:S(2)}, u32[]{:S(2)}) collective-permute-start(f32[3,16,24,128]{3,2,1,0:T(8,128)} %get-tuple-element.16), channel_id=1, source_target_pairs={{0,16},{1,17},{2,18},{3,19},{4,20},{5,21},{6,22},{7,23},{8,24},{9,... | collective-permute-start | bytes 1769480 | tf_op jit(solution)/shard_map/ppermute | solution.py:710
  13.5 0.9 %copy-start.6 = (f32[16,2048]{1,0:T(8,128)S(1)}, f32[16,2048]{1,0:T(8,128)}, u32[]{:S(2)}) copy-start(f32[16,2048]{1,0:T(8,128)} %fraction_hbm.1) | copy-start | bytes 393220
  14.4 18.0 %copy-start.1 = (f32[16,2048]{1,0:T(8,128)S(1)}, f32[16,2048]{1,0:T(8,128)}, u32[]{:S(2)}) copy-start(f32[16,2048]{1,0:T(8,128)} %bih.3) | copy-start | bytes 393220
  14.5 18.0 %copy-start.2 = (f32[2,16,2048]{2,1,0:T(8,128)S(1)}, f32[2,16,2048]{2,1,0:T(8,128)}, u32[]{:S(2)}) copy-start(f32[2,16,2048]{2,1,0:T(8,128)} %prev.1) | copy-start | bytes 786436
  51.9 4.4 %collective-permute-start.3 = (f32[2,3,24,128]{3,2,1,0:T(8,128)S(1)}, f32[2,3,24,128]{3,2,1,0:T(8,128)S(1)}, u32[]{:S(2)}, u32[]{:S(2)}) collective-permute-start(f32[2,3,24,128]{3,2,1,0:T(8,128)S(1)} %received_ends.1), channel_id=1, source_target_pairs={{0,16},{1,17},{2,18},{3,19},{4,20},{5,21},{6,22},{7,23},{8,24},{9,... | collective-permute-start | bytes 221192 | tf_op jit(solution)/shard_map/ppermute | solution.py:710

commit v5 on v4

--- a/solution.py
+++ b/solution.py
@@ -40,7 +40,6 @@
 
 
 WIDE = 256
-GROUP = 4
 
 
 def iota(shape, dim):
@@ -53,44 +52,24 @@
 
 def column_taps(source, shape):
     place = iota(shape, 1)
-    d = jnp.abs(source - (place & (WIDE - 1)))
+    wide = shape[1] // 2
+    d = jnp.abs(source - (place & (wide - 1)))
     double = jnp.where(d == 0, 20, jnp.where(d == 1, -8, jnp.where(d == 2, 1, 0)))
     single = jnp.where(d == 0, -8, jnp.where(d == 1, 2, 0))
-    return as_matrix(jnp.where(place < WIDE, double, single))
+    return as_matrix(jnp.where(place < wide, double, single))
 
 
 def make_columns(matrix):
-    own = (WIDE, 2 * WIDE)
+    wide = matrix.shape[1] // 2
+    own = (wide, 2 * wide)
     taps = column_taps(iota(own, 0), own)
-    matrix[0:WIDE, :] = taps
-    matrix[WIDE : 2 * WIDE, :] = taps
-    side = (LANES, 2 * WIDE)
+    matrix[0:wide, :] = taps
+    matrix[wide : 2 * wide, :] = taps
+    side = (LANES, 2 * wide)
     lane = iota(side, 0)
-    taps = column_taps(jnp.where(lane < LANES // 2, lane + WIDE, lane - LANES), side)
-    matrix[2 * WIDE : 2 * WIDE + LANES, :] = taps
-    matrix[2 * WIDE + LANES : 2 * WIDE + 2 * LANES, :] = taps
-
-
-def make_mixing(mixing, levels):
-    height = GROUP * levels
-    shape = mixing.shape
-    a, c = iota(shape, 0), iota(shape, 1)
-    c = jnp.where(c >= height, c - height, c)
-
-    def parts(index):
-        group = jnp.zeros(shape, jnp.int32)
-        for n in range(1, GROUP):
-            group = group + jnp.where(index >= n * levels, 1, 0)
-        return group, index - levels * group
-
-    ga, la = parts(a)
-    gc, lc = parts(c)
-    value = (
-        jnp.where(lc == jnp.maximum(la - 1, 0), 1, 0)
-        + jnp.where(lc == jnp.minimum(la + 1, levels - 1), 1, 0)
-        - jnp.where(lc == la, 2, 0)
-    )
-    mixing[...] = as_matrix(jnp.where(ga == gc, value, 0))
+    taps = column_taps(jnp.where(lane < LANES // 2, lane + wide, lane - LANES), side)
+    matrix[2 * wide : 2 * wide + LANES, :] = taps
+    matrix[2 * wide + LANES : 2 * wide + 2 * LANES, :] = taps
 
 
 def make_orders(forward, backward):
@@ -444,16 +423,12 @@
     raw,
     out,
     y,
-    z,
     matrix,
-    mixing,
     in_sem,
     out_sem,
 ):
     fields, rows, levels, width = x.shape
-    steps = width // WIDE
     tiles = width // LANES
-    each = WIDE // LANES
 
     def fetch(c):
         at = slice(c * LANES, (c + 1) * LANES)
@@ -466,77 +441,73 @@
     for c in range(tiles):
         fetch(c).start()
     make_columns(matrix)
-    make_mixing(mixing, levels)
-
-    level = lax.broadcasted_iota(jnp.int32, (HALF, WIDE), 0)
+
     lane = lax.broadcasted_iota(jnp.int32, (rows * levels, LANES), 1)
 
-    def merge(value):
-        return value.reshape(rows * levels, value.shape[-1])
+    def tile(f, c):
+        value = cols[f] if c < 0 or c >= tiles else x[f, :, :, c * LANES : (c + 1) * LANES]
+        return value.reshape(rows * levels, LANES)
+
+    def begin(c, f, slot):
+        side = jnp.where(lane < LANES // 2, tile(f, c + 1), tile(f, c - 1))
+        y[slot] = jnp.dot(
+            jnp.concatenate(split(tile(f, c), 2) + split(side, 2), axis=1),
+            matrix[...],
+            preferred_element_type=jnp.float32,
+        )
+
+    def finish(c, f, slot):
+        at = slice(c * LANES, (c + 1) * LANES)
+        for r in range(rows):
+            lap = y[slot, r * levels : (r + 1) * levels, 0:LANES]
+            for step in (-1, 1):
+                n = r + step
+                if 0 <= n < rows:
+                    lap = lap + y[slot, n * levels : (n + 1) * levels, LANES : 2 * LANES]
+                if 0 <= n + step < rows:
+                    lap = lap + x[f, n + step, :, at]
+            out[f, c, pl.ds(r, levels, stride=rows), :] = lap
+        for h in range(0, rows, HALF):
+            hs = slice(h, h + HALF)
+            coef = bih[hs, at]
+            turn = cor[hs, :]
+            before = here = raw[f, c, hs, :]
+            for k in range(levels):
+                ks = slice(k * rows + h, k * rows + h + HALF)
+                if k + 1 < levels:
+                    after = raw[f, c, (k + 1) * rows + h : (k + 1) * rows + h + HALF, :]
+                else:
+                    after = here
+                res = (1.0 - 2.0 * KV_MIX) * here + KV_MIX * (before + after)
+                res = res - coef * out[f, c, ks, :]
+                if f == 0:
+                    res = res + turn * raw[1, c, ks, :]
+                elif f == 1:
+                    res = res - turn * raw[0, c, ks, :]
+                if f < 2 and k == 0:
+                    res = res + prev[f, hs, at]
+                out[f, c, ks, :] = res
+                before, here = here, after
+        if f == fields - 1:
+            store(c).start()
 
     waited = 0
-    for m in range(steps):
-        while waited < min((m + 1) * each + 1, tiles):
+    pending = None
+    for c in range(tiles):
+        while waited < min(c + 2, tiles):
             fetch(waited).wait()
             to = slice(waited * LANES, (waited + 1) * LANES)
             for f in range(fields):
                 for r in range(rows):
                     x[f, r, :, to] = raw[f, waited, pl.ds(r, levels, stride=rows), :]
             waited += 1
-        at = slice(m * WIDE, (m + 1) * WIDE)
         for f in range(fields):
-            slot = (m * fields + f) % 2
-            own = merge(x[f, :, :, at])
-            if m == 0:
-                west = merge(cols[f])
-            else:
-                west = merge(x[f, :, :, m * WIDE - LANES : m * WIDE])
-            if m == steps - 1:
-                east = merge(cols[f])
-            else:
-                east = merge(x[f, :, :, (m + 1) * WIDE : (m + 1) * WIDE + LANES])
-            side = jnp.where(lane < LANES // 2, east, west)
-            parts = split(own, 2)
-            y[slot] = jnp.dot(
-                jnp.concatenate(parts + split(side, 2), axis=1),
-                matrix[...],
-                preferred_element_type=jnp.float32,
-            )
-            height = GROUP * levels
-            for n in range(rows // GROUP):
-                group = slice(n * height, (n + 1) * height)
-                z[slot, group, :] = jnp.dot(
-                    mixing[...],
-                    jnp.concatenate([part[group] for part in parts], axis=0),
-                    preferred_element_type=jnp.float32,
-                )
-
-            def near(r):
-                return y[slot, r * levels : (r + 1) * levels, WIDE : 2 * WIDE]
-
-            for r in range(rows):
-                q = x[f, r, :, at]
-                lap = y[slot, r * levels : (r + 1) * levels, 0:WIDE]
-                for step in (-1, 1):
-                    if 0 <= r + step < rows:
-                        lap = lap + near(r + step)
-                    if 0 <= r + 2 * step < rows:
-                        lap = lap + x[f, r + 2 * step, :, at]
-                mixed = z[slot, r * levels : (r + 1) * levels, :]
-                res = q + KV_MIX * mixed - bih[r : r + 1, at] * lap
-                if f == 0:
-                    res = res + cor[r] * x[1, r, :, at]
-                elif f == 1:
-                    res = res - cor[r] * x[0, r, :, at]
-                if f < 2:
-                    head = res[0:HALF] + jnp.where(level == 0, prev[f, r : r + 1, at], 0.0)
-                    res = jnp.concatenate([head, res[HALF:]], axis=0)
-                for n in range(each):
-                    out[f, m * each + n, pl.ds(r, levels, stride=rows), :] = res[
-                        :, n * LANES : (n + 1) * LANES
-                    ]
-        for n in range(each):
-            store(m * each + n).start()
+            job = (c, f, (c * fields + f) % 2)
+            begin(*job)
+            if pending is not None:
+                finish(*pending)
+            pending = job
+    finish(*pending)
     for c in range(tiles):
         store(c).wait()
 
@@ -549,16 +520,14 @@
         main_kernel,
         name="ocean_tile",
         out_shape=jax.ShapeDtypeStruct((fields, levels * rows, width), f32),
-        in_specs=[spec(HBM)] + [spec(VMEM)] * 3 + [spec(SMEM)],
+        in_specs=[spec(HBM)] + [spec(VMEM)] * 4,
         out_specs=spec(HBM),
         scratch_shapes=[
             pltpu.VMEM((fields, rows, levels, width), f32),
             pltpu.VMEM(tiled, f32),
             pltpu.VMEM(tiled, f32),
-            pltpu.VMEM((2, rows * levels, 2 * WIDE), f32),
-            pltpu.VMEM((2, rows * levels, WIDE), f32),
-            pltpu.VMEM((2 * (WIDE + LANES), 2 * WIDE), jnp.bfloat16),
-            pltpu.VMEM((GROUP * levels, 2 * GROUP * levels), jnp.bfloat16),
+            pltpu.VMEM((2, rows * levels, 2 * LANES), f32),
+            pltpu.VMEM((4 * LANES, 2 * LANES), jnp.bfloat16),
             pltpu.SemaphoreType.DMA((width // LANES,)),
             pltpu.SemaphoreType.DMA((width // LANES,)),
         ],
@@ -724,6 +693,7 @@
 
     rows = (lax.axis_index("tile") * tile_rows + jnp.arange(tile_rows)).astype(jnp.float32) + 0.5
     coriolis = CORIOLIS * (2.0 * rows / (tile_rows * n_tile) - 1.0)
+    coriolis = jnp.broadcast_to(coriolis[:, None], (tile_rows, LANES))
 
     cols, ice_out, stress_out = lax.optimization_barrier((cols, ice_out, stress_out))
     base = ocean(ocean_state, cols, biharmonic, prev_stress, coriolis)

time: 59.9 us -> 59.8 us (level)
  transfers between devices with their start and end apart: 4 -> 4, of which waited for: 1 -> 1; matrix products, arithmetic and copies ran while one was open for 0% -> 0% of each run, Pallas kernels for 63% -> 62%
where the time goes in v5:
time: 59.8 us; the launch traced here: 59.5 us
  Pallas kernels  44.4 us (74%)
  starting transfers between devices  8.65 us (14%)
  waiting for transfers between devices  3.79 us (6%)
  between operations  1.63 us (3%)
  local copies, waits for them, and re-layouts  1 us (2%)
    pallas_call x1, Pallas kernels, ocean(): pl.pallas_call(main_kernel, name='ocean_tile', out_shape=jax.ShapeDtypeSt...  19.2 us
    pallas_call x1, Pallas kernels, ice(): pl.pallas_call(ice_kernel, name='ice_subcycles', out_shape=(jax.ShapeDtyp...  18 us
    ppermute x4, starting transfers between devices, shift(): return lax.ppermute(value, ('grp', 'tile'), pairs)  8.65 us
    pallas_call x1, Pallas kernels, pack(): pl.pallas_call(pack_kernel, name='pack_edges', out_shape=(jax.ShapeDtypeS...  4.12 us
    ppermute x4, waiting for transfers between devices, shift(): return lax.ppermute(value, ('grp', 'tile'), pairs)  3.79 us
    pallas_call x1, Pallas kernels, fix(): pl.pallas_call(fix_kernel, name='ocean_edges', out_shape=jax.ShapeDtypeSt...  3.13 us
  transfers between devices with their start and end apart: 4, of which 1 were waited for; matrix products, arithmetic and copies ran while one was open for 0% of the time, Pallas kernels for 62%

profile of v5, /device:TPU:24, one launch (start us, length us, event | category | flops | bytes accessed | tf_op | source)
XLA Modules:
  0.0 59.5 jit_solution(16728914018156366321)
XLA Ops:
  0.6 0.0 copy-start
  0.6 0.0 copy-start.3
  0.7 0.0 copy-start.4
  0.7 0.0 copy-start.5
  0.7 0.0 copy-start.7
  0.7 4.1 %pack_edges.1 = (f32[2,3,24,2048]{3,2,1,0:T(8,128)}, f32[2,3,24,2048]{3,2,1,0:T(8,128)}, f32[3,16,24,128]{3,2,1,0:T(8,128)}) custom-call(f32[3,24,16,2048]{3,2,1,0:T(8,128)} %ocean_hbm.1, f32[3,384,2048]{2,1,0:T(8,128)} %bitcast.2), custom_call_target="tpu_custom_call" | custom-call | bytes 4718592 | tf_op jit(solution)/shard_map/pack_edges/pallas_call | solution.py:130
  4.8 1.9 %collective-permute-start = (f32[2,3,24,2048]{3,2,1,0:T(8,128)}, f32[2,3,24,2048]{3,2,1,0:T(8,128)S(1)}, u32[]{:S(2)}, u32[]{:S(2)}) collective-permute-start(f32[2,3,24,2048]{3,2,1,0:T(8,128)} %get-tuple-element.14), channel_id=1, source_target_pairs={{0,1},{1,2},{2,3},{3,4},{4,5},{5,6},{6,7},{7,8},{8,9},{9,10},{10,1... | collective-permute-start | bytes 3538952 | tf_op jit(solution)/shard_map/ppermute | solution.py:679
  6.7 4.5 %collective-permute-start.1 = (f32[2,3,24,2048]{3,2,1,0:T(8,128)}, f32[2,3,24,2048]{3,2,1,0:T(8,128)S(1)}, u32[]{:S(2)}, u32[]{:S(2)}) collective-permute-start(f32[2,3,24,2048]{3,2,1,0:T(8,128)} %get-tuple-element.15), channel_id=1, source_target_pairs={{1,0},{2,1},{3,2},{4,3},{5,4},{6,5},{7,6},{8,7},{9,8},{10,9},{11,1... | collective-permute-start | bytes 3538952 | tf_op jit(solution)/shard_map/ppermute | solution.py:679
  11.3 1.6 %collective-permute-start.2 = (f32[3,16,24,128]{3,2,1,0:T(8,128)}, f32[3,16,24,128]{3,2,1,0:T(8,128)}, u32[]{:S(2)}, u32[]{:S(2)}) collective-permute-start(f32[3,16,24,128]{3,2,1,0:T(8,128)} %get-tuple-element.16), channel_id=1, source_target_pairs={{0,16},{1,17},{2,18},{3,19},{4,20},{5,21},{6,22},{7,23},{8,24},{9,... | collective-permute-start | bytes 1769480 | tf_op jit(solution)/shard_map/ppermute | solution.py:679
  13.5 0.0 copy-done
  13.5 0.0 copy-done.3
  13.5 0.0 copy-done.4
  13.5 0.0 copy-done.5
  13.5 0.0 copy-done.7
  13.5 0.0 copy-start.6
  13.6 0.9 %copy-done.6 = f32[16,2048]{1,0:T(8,128)S(1)} copy-done((f32[16,2048]{1,0:T(8,128)S(1)}, f32[16,2048]{1,0:T(8,128)}, u32[]{:S(2)}) %copy-start.6) | copy-done | bytes 131096
  14.4 0.0 copy-start.1
  14.5 0.0 copy-start.2
  14.5 18.0 %ice_subcycles.1 = (f32[5,16,2048]{2,1,0:T(8,128)}, f32[2,16,2048]{2,1,0:T(8,128)}) custom-call(s32[1]{0:T(128)S(6)} %copy.15.count, s32[1,16]{1,0:T(1,128)S(1)} %copy-done.7, f32[5,16,2048]{2,1,0:T(8,128)S(1)} %copy-done, f32[16,2048]{1,0:T(8,128)S(1)} %copy-done.4, f32[16,2048]{1,0:T(8,128)S(1)} %copy-done.5, f32[16,2048]{1,0:T(8,128)S(1)} %copy-done.6, ...), custom_call_target="tpu_custom_call" | custom-call | flops 104857600 | bytes 2883584 | tf_op jit(solution)/shard_map/ice_subcycles/pallas_call | solution.py:379
  32.4 0.0 collective-permute-done.2.cols
  32.5 0.1 broadcast_in_dim.2.cor
  32.5 0.0 copy-done.1
  32.5 0.0 copy-done.2
  32.5 19.2 %ocean_tile.1 = f32[3,384,2048]{2,1,0:T(8,128)} custom-call(f32[3,384,2048]{2,1,0:T(8,128)} %bitcast.3, f32[3,16,24,128]{3,2,1,0:T(8,128)} %collective-permute-done.2.cols, f32[16,2048]{1,0:T(8,128)S(1)} %copy-done.1, f32[2,16,2048]{2,1,0:T(8,128)S(1)} %copy-done.2, f32[16,128]{1,0:T(8,128)S(1)} %broadcast_in_dim.2.cor), custom_call_target="tpu_custom_call" | custom-call | flops 70778880 | bytes 18874368 | tf_op jit(solution)/shard_map/ocean_tile/pallas_call | solution.py:519
  51.7 0.0 collective-permute-done.above
  51.7 0.0 collective-permute-done.1.below
  51.8 0.6 %collective-permute-start.3 = (f32[2,3,24,128]{3,2,1,0:T(8,128)S(1)}, f32[2,3,24,128]{3,2,1,0:T(8,128)S(1)}, u32[]{:S(2)}, u32[]{:S(2)}) collective-permute-start(f32[2,3,24,128]{3,2,1,0:T(8,128)S(1)} %received_ends.1), channel_id=1, source_target_pairs={{0,16},{1,17},{2,18},{3,19},{4,20},{5,21},{6,22},{7,23},{8,24},{9,... | collective-permute-start | bytes 221192 | tf_op jit(solution)/shard_map/ppermute | solution.py:679
  52.4 3.8 %collective-permute-done.3.corners = f32[2,3,24,128]{3,2,1,0:T(8,128)S(1)} collective-permute-done((f32[2,3,24,128]{3,2,1,0:T(8,128)S(1)}, f32[2,3,24,128]{3,2,1,0:T(8,128)S(1)}, u32[]{:S(2)}, u32[]{:S(2)}) %collective-permute-start.3) | collective-permute-done | bytes 73760 | tf_op jit(solution)/shard_map/ppermute | solution.py:679
  56.2 3.1 %ocean_edges.1 = f32[3,24,16,2048]{3,2,1,0:T(8,128)} custom-call(f32[3,24,16,2048]{3,2,1,0:T(8,128)} %bitcast.4, f32[2,3,24,2048]{3,2,1,0:T(8,128)S(1)} %collective-permute-done.above, f32[2,3,24,2048]{3,2,1,0:T(8,128)S(1)} %collective-permute-done.1.below, f32[2,3,24,128]{3,2,1,0:T(8,128)S(1)} %collective-permute-done.3.corners, ...), custom_call_target="tpu_custom_call", output_to_operand_aliasing={{}: (0, {})} | custom-call | bytes 7077888 | tf_op jit(solution)/shard_map/ocean_edges/pallas_call | solution.py:634
  (2 shorter events, 0.0 us)
Async XLA Ops:
  0.6 12.9 %copy-start = (f32[5,16,2048]{2,1,0:T(8,128)S(1)}, f32[5,16,2048]{2,1,0:T(8,128)}, u32[]{:S(2)}) copy-start(f32[5,16,2048]{2,1,0:T(8,128)} %state_hbm.1) | copy-start | bytes 1966084
  0.6 12.9 %copy-start.3 = (f32[2,16,2048]{2,1,0:T(8,128)S(1)}, f32[2,16,2048]{2,1,0:T(8,128)}, u32[]{:S(2)}) copy-start(f32[2,16,2048]{2,1,0:T(8,128)} %wind_hbm.1) | copy-start | bytes 786436
  0.7 12.9 %copy-start.4 = (f32[16,2048]{1,0:T(8,128)S(1)}, f32[16,2048]{1,0:T(8,128)}, u32[]{:S(2)}) copy-start(f32[16,2048]{1,0:T(8,128)} %strength_hbm.1) | copy-start | bytes 393220
  0.7 12.9 %copy-start.5 = (f32[16,2048]{1,0:T(8,128)S(1)}, f32[16,2048]{1,0:T(8,128)}, u32[]{:S(2)}) copy-start(f32[16,2048]{1,0:T(8,128)} %mass_hbm.1) | copy-start | bytes 393220
  0.7 12.9 %copy-start.7 = (s32[1,16]{1,0:T(1,128)S(1)}, s32[1,16]{1,0:T(1,128)}, u32[]{:S(2)}) copy-start(s32[1,16]{1,0:T(1,128)} %listed.1) | copy-start | bytes 196
  4.8 46.9 %collective-permute-start = (f32[2,3,24,2048]{3,2,1,0:T(8,128)}, f32[2,3,24,2048]{3,2,1,0:T(8,128)S(1)}, u32[]{:S(2)}, u32[]{:S(2)}) collective-permute-start(f32[2,3,24,2048]{3,2,1,0:T(8,128)} %get-tuple-element.14), channel_id=1, source_target_pairs={{0,1},{1,2},{2,3},{3,4},{4,5},{5,6},{6,7},{7,8},{8,9},{9,10},{10,1... | collective-permute-start | bytes 3538952 | tf_op jit(solution)/shard_map/ppermute | solution.py:679
  6.7 45.0 %collective-permute-start.1 = (f32[2,3,24,2048]{3,2,1,0:T(8,128)}, f32[2,3,24,2048]{3,2,1,0:T(8,128)S(1)}, u32[]{:S(2)}, u32[]{:S(2)}) collective-permute-start(f32[2,3,24,2048]{3,2,1,0:T(8,128)} %get-tuple-element.15), channel_id=1, source_target_pairs={{1,0},{2,1},{3,2},{4,3},{5,4},{6,5},{7,6},{8,7},{9,8},{10,9},{11,1... | collective-permute-start | bytes 3538952 | tf_op jit(solution)/shard_map/ppermute | solution.py:679
  11.3 21.2 %collective-permute-start.2 = (f32[3,16,24,128]{3,2,1,0:T(8,128)}, f32[3,16,24,128]{3,2,1,0:T(8,128)}, u32[]{:S(2)}, u32[]{:S(2)}) collective-permute-start(f32[3,16,24,128]{3,2,1,0:T(8,128)} %get-tuple-element.16), channel_id=1, source_target_pairs={{0,16},{1,17},{2,18},{3,19},{4,20},{5,21},{6,22},{7,23},{8,24},{9,... | collective-permute-start | bytes 1769480 | tf_op jit(solution)/shard_map/ppermute | solution.py:679
  13.5 0.9 %copy-start.6 = (f32[16,2048]{1,0:T(8,128)S(1)}, f32[16,2048]{1,0:T(8,128)}, u32[]{:S(2)}) copy-start(f32[16,2048]{1,0:T(8,128)} %fraction_hbm.1) | copy-start | bytes 393220
  14.4 18.1 %copy-start.1 = (f32[16,2048]{1,0:T(8,128)S(1)}, f32[16,2048]{1,0:T(8,128)}, u32[]{:S(2)}) copy-start(f32[16,2048]{1,0:T(8,128)} %bih.3) | copy-start | bytes 393220
  14.5 18.1 %copy-start.2 = (f32[2,16,2048]{2,1,0:T(8,128)S(1)}, f32[2,16,2048]{2,1,0:T(8,128)}, u32[]{:S(2)}) copy-start(f32[2,16,2048]{2,1,0:T(8,128)} %prev.1) | copy-start | bytes 786436
  51.8 4.4 %collective-permute-start.3 = (f32[2,3,24,128]{3,2,1,0:T(8,128)S(1)}, f32[2,3,24,128]{3,2,1,0:T(8,128)S(1)}, u32[]{:S(2)}, u32[]{:S(2)}) collective-permute-start(f32[2,3,24,128]{3,2,1,0:T(8,128)S(1)} %received_ends.1), channel_id=1, source_target_pairs={{0,16},{1,17},{2,18},{3,19},{4,20},{5,21},{6,22},{7,23},{8,24},{9,... | collective-permute-start | bytes 221192 | tf_op jit(solution)/shard_map/ppermute | solution.py:679

commit v6 on v5

--- a/solution.py
+++ b/solution.py
@@ -428,28 +428,33 @@
     out_sem,
 ):
     fields, rows, levels, width = x.shape
-    tiles = width // LANES
+    tiles = width // LANES - 1
+
+    def lanes(c):
+        start = c * LANES
+        return pl.ds(start if isinstance(c, int) else pl.multiple_of(start, LANES), LANES)
 
     def fetch(c):
-        at = slice(c * LANES, (c + 1) * LANES)
+        at = lanes(c)
         return pltpu.make_async_copy(x_hbm.at[:, :, at], raw.at[:, c], in_sem.at[c])
 
     def store(c):
-        at = slice(c * LANES, (c + 1) * LANES)
+        at = lanes(c)
         return pltpu.make_async_copy(out.at[:, c], out_hbm.at[:, :, at], out_sem.at[c])
 
     for c in range(tiles):
         fetch(c).start()
     make_columns(matrix)
+    x[:, :, :, lanes(tiles)] = cols[...]
 
     lane = lax.broadcasted_iota(jnp.int32, (rows * levels, LANES), 1)
 
     def tile(f, c):
-        value = cols[f] if c < 0 or c >= tiles else x[f, :, :, c * LANES : (c + 1) * LANES]
-        return value.reshape(rows * levels, LANES)
+        return x[f, :, :, lanes(c)].reshape(rows * levels, LANES)
 
     def begin(c, f, slot):
-        side = jnp.where(lane < LANES // 2, tile(f, c + 1), tile(f, c - 1))
+        west = jnp.where(c == 0, tiles, c - 1)
+        side = jnp.where(lane < LANES // 2, tile(f, c + 1), tile(f, west))
         y[slot] = jnp.dot(
             jnp.concatenate(split(tile(f, c), 2) + split(side, 2), axis=1),
             matrix[...],
@@ -457,7 +462,7 @@
         )
 
     def finish(c, f, slot):
-        at = slice(c * LANES, (c + 1) * LANES)
+        at = lanes(c)
         for r in range(rows):
             lap = y[slot, r * levels : (r + 1) * levels, 0:LANES]
             for step in (-1, 1):
@@ -488,26 +493,28 @@
                     res = res + prev[f, hs, at]
                 out[f, c, ks, :] = res
                 before, here = here, after
-        if f == fields - 1:
-            store(c).start()
-
-    waited = 0
-    pending = None
-    for c in range(tiles):
-        while waited < min(c + 2, tiles):
-            fetch(waited).wait()
-            to = slice(waited * LANES, (waited + 1) * LANES)
-            for f in range(fields):
-                for r in range(rows):
-                    x[f, r, :, to] = raw[f, waited, pl.ds(r, levels, stride=rows), :]
-            waited += 1
+    def turn_rows(c):
+        fetch(c).wait()
         for f in range(fields):
-            job = (c, f, (c * fields + f) % 2)
-            begin(*job)
-            if pending is not None:
-                finish(*pending)
-            pending = job
-    finish(*pending)
+            for r in range(rows):
+                x[f, r, :, lanes(c)] = raw[f, c, pl.ds(r, levels, stride=rows), :]
+
+    turn_rows(0)
+
+    def column(c, carry):
+        @pl.when(c + 1 < tiles)
+        def _():
+            turn_rows(c + 1)
+
+        begin(c, 0, 0)
+        for f in range(fields):
+            if f + 1 < fields:
+                begin(c, f + 1, f + 1)
+            finish(c, f, f)
+        store(c).start()
+        return carry
+
+    lax.fori_loop(0, tiles, column, 0)
     for c in range(tiles):
         store(c).wait()
 
@@ -523,10 +530,10 @@
         in_specs=[spec(HBM)] + [spec(VMEM)] * 4,
         out_specs=spec(HBM),
         scratch_shapes=[
-            pltpu.VMEM((fields, rows, levels, width), f32),
+            pltpu.VMEM((fields, rows, levels, width + LANES), f32),
             pltpu.VMEM(tiled, f32),
             pltpu.VMEM(tiled, f32),
-            pltpu.VMEM((2, rows * levels, 2 * LANES), f32),
+            pltpu.VMEM((fields, rows * levels, 2 * LANES), f32),
             pltpu.VMEM((4 * LANES, 2 * LANES), jnp.bfloat16),
             pltpu.SemaphoreType.DMA((width // LANES,)),
             pltpu.SemaphoreType.DMA((width // LANES,)),

time: 59.8 us -> 59 us (0.987)
  Pallas kernels: 44.4 us -> 43.7 us
where the time goes in v6:
time: 59 us; the launch traced here: 58.6 us
  Pallas kernels  43.7 us (74%)
  starting transfers between devices  8.63 us (15%)
  waiting for transfers between devices  3.81 us (6%)
  between operations  1.45 us (2%)
  local copies, waits for them, and re-layouts  1 us (2%)
    pallas_call x1, Pallas kernels, ocean(): pl.pallas_call(main_kernel, name='ocean_tile', out_shape=jax.ShapeDtypeSt...  18.7 us
    pallas_call x1, Pallas kernels, ice(): pl.pallas_call(ice_kernel, name='ice_subcycles', out_shape=(jax.ShapeDtyp...  17.8 us
    ppermute x4, starting transfers between devices, shift(): return lax.ppermute(value, ('grp', 'tile'), pairs)  8.63 us
    pallas_call x1, Pallas kernels, pack(): pl.pallas_call(pack_kernel, name='pack_edges', out_shape=(jax.ShapeDtypeS...  4.12 us
    ppermute x4, waiting for transfers between devices, shift(): return lax.ppermute(value, ('grp', 'tile'), pairs)  3.81 us
    pallas_call x1, Pallas kernels, fix(): pl.pallas_call(fix_kernel, name='ocean_edges', out_shape=jax.ShapeDtypeSt...  3.13 us
  transfers between devices with their start and end apart: 4, of which 1 were waited for; matrix products, arithmetic and copies ran while one was open for 0% of the time, Pallas kernels for 62%

profile of v6, /device:TPU:24, one launch (start us, length us, event | category | flops | bytes accessed | tf_op | source)
XLA Modules:
  0.0 58.6 jit_solution(6684477824118296672)
XLA Ops:
  0.6 0.0 copy-start
  0.6 0.0 copy-start.3
  0.7 0.0 copy-start.4
  0.7 0.0 copy-start.5
  0.7 0.0 copy-start.7
  0.7 4.1 %pack_edges.1 = (f32[2,3,24,2048]{3,2,1,0:T(8,128)}, f32[2,3,24,2048]{3,2,1,0:T(8,128)}, f32[3,16,24,128]{3,2,1,0:T(8,128)}) custom-call(f32[3,24,16,2048]{3,2,1,0:T(8,128)} %ocean_hbm.1, f32[3,384,2048]{2,1,0:T(8,128)} %bitcast.2), custom_call_target="tpu_custom_call" | custom-call | bytes 4718592 | tf_op jit(solution)/shard_map/pack_edges/pallas_call | solution.py:130
  4.8 1.9 %collective-permute-start = (f32[2,3,24,2048]{3,2,1,0:T(8,128)}, f32[2,3,24,2048]{3,2,1,0:T(8,128)S(1)}, u32[]{:S(2)}, u32[]{:S(2)}) collective-permute-start(f32[2,3,24,2048]{3,2,1,0:T(8,128)} %get-tuple-element.14), channel_id=1, source_target_pairs={{0,1},{1,2},{2,3},{3,4},{4,5},{5,6},{6,7},{7,8},{8,9},{9,10},{10,1... | collective-permute-start | bytes 3538952 | tf_op jit(solution)/shard_map/ppermute | solution.py:686
  6.7 4.5 %collective-permute-start.1 = (f32[2,3,24,2048]{3,2,1,0:T(8,128)}, f32[2,3,24,2048]{3,2,1,0:T(8,128)S(1)}, u32[]{:S(2)}, u32[]{:S(2)}) collective-permute-start(f32[2,3,24,2048]{3,2,1,0:T(8,128)} %get-tuple-element.15), channel_id=1, source_target_pairs={{1,0},{2,1},{3,2},{4,3},{5,4},{6,5},{7,6},{8,7},{9,8},{10,9},{11,1... | collective-permute-start | bytes 3538952 | tf_op jit(solution)/shard_map/ppermute | solution.py:686
  11.3 1.6 %collective-permute-start.2 = (f32[3,16,24,128]{3,2,1,0:T(8,128)}, f32[3,16,24,128]{3,2,1,0:T(8,128)}, u32[]{:S(2)}, u32[]{:S(2)}) collective-permute-start(f32[3,16,24,128]{3,2,1,0:T(8,128)} %get-tuple-element.16), channel_id=1, source_target_pairs={{0,16},{1,17},{2,18},{3,19},{4,20},{5,21},{6,22},{7,23},{8,24},{9,... | collective-permute-start | bytes 1769480 | tf_op jit(solution)/shard_map/ppermute | solution.py:686
  13.5 0.0 copy-done
  13.5 0.0 copy-done.3
  13.5 0.0 copy-done.4
  13.5 0.0 copy-done.5
  13.5 0.0 copy-done.7
  13.5 0.0 copy-start.6
  13.6 0.9 %copy-done.6 = f32[16,2048]{1,0:T(8,128)S(1)} copy-done((f32[16,2048]{1,0:T(8,128)S(1)}, f32[16,2048]{1,0:T(8,128)}, u32[]{:S(2)}) %copy-start.6) | copy-done | bytes 131096
  14.4 0.0 copy-start.1
  14.5 0.0 copy-start.2
  14.5 17.8 %ice_subcycles.1 = (f32[5,16,2048]{2,1,0:T(8,128)}, f32[2,16,2048]{2,1,0:T(8,128)}) custom-call(s32[1]{0:T(128)S(6)} %copy.15.count, s32[1,16]{1,0:T(1,128)S(1)} %copy-done.7, f32[5,16,2048]{2,1,0:T(8,128)S(1)} %copy-done, f32[16,2048]{1,0:T(8,128)S(1)} %copy-done.4, f32[16,2048]{1,0:T(8,128)S(1)} %copy-done.5, f32[16,2048]{1,0:T(8,128)S(1)} %copy-done.6, ...), custom_call_target="tpu_custom_call" | custom-call | flops 104857600 | bytes 2883584 | tf_op jit(solution)/shard_map/ice_subcycles/pallas_call | solution.py:379
  32.3 0.0 collective-permute-done.2.cols
  32.3 0.1 broadcast_in_dim.2.cor
  32.3 0.0 copy-done.1
  32.4 0.0 copy-done.2
  32.4 18.7 %ocean_tile.1 = f32[3,384,2048]{2,1,0:T(8,128)} custom-call(f32[3,384,2048]{2,1,0:T(8,128)} %bitcast.3, f32[3,16,24,128]{3,2,1,0:T(8,128)} %collective-permute-done.2.cols, f32[16,2048]{1,0:T(8,128)S(1)} %copy-done.1, f32[2,16,2048]{2,1,0:T(8,128)S(1)} %copy-done.2, f32[16,128]{1,0:T(8,128)S(1)} %broadcast_in_dim.2.cor), custom_call_target="tpu_custom_call" | custom-call | flops 70778880 | bytes 18874368 | tf_op jit(solution)/shard_map/ocean_tile/pallas_call | solution.py:526
  51.0 0.0 collective-permute-done.above
  51.1 0.0 collective-permute-done.1.below
  51.1 0.6 %collective-permute-start.3 = (f32[2,3,24,128]{3,2,1,0:T(8,128)S(1)}, f32[2,3,24,128]{3,2,1,0:T(8,128)S(1)}, u32[]{:S(2)}, u32[]{:S(2)}) collective-permute-start(f32[2,3,24,128]{3,2,1,0:T(8,128)S(1)} %received_ends.1), channel_id=1, source_target_pairs={{0,16},{1,17},{2,18},{3,19},{4,20},{5,21},{6,22},{7,23},{8,24},{9,... | collective-permute-start | bytes 221192 | tf_op jit(solution)/shard_map/ppermute | solution.py:686
  51.7 3.8 %collective-permute-done.3.corners = f32[2,3,24,128]{3,2,1,0:T(8,128)S(1)} collective-permute-done((f32[2,3,24,128]{3,2,1,0:T(8,128)S(1)}, f32[2,3,24,128]{3,2,1,0:T(8,128)S(1)}, u32[]{:S(2)}, u32[]{:S(2)}) %collective-permute-start.3) | collective-permute-done | bytes 73760 | tf_op jit(solution)/shard_map/ppermute | solution.py:686
  55.5 3.1 %ocean_edges.1 = f32[3,24,16,2048]{3,2,1,0:T(8,128)} custom-call(f32[3,24,16,2048]{3,2,1,0:T(8,128)} %bitcast.4, f32[2,3,24,2048]{3,2,1,0:T(8,128)S(1)} %collective-permute-done.above, f32[2,3,24,2048]{3,2,1,0:T(8,128)S(1)} %collective-permute-done.1.below, f32[2,3,24,128]{3,2,1,0:T(8,128)S(1)} %collective-permute-done.3.corners, ...), custom_call_target="tpu_custom_call", output_to_operand_aliasing={{}: (0, {})} | custom-call | bytes 7077888 | tf_op jit(solution)/shard_map/ocean_edges/pallas_call | solution.py:641
  (2 shorter events, 0.0 us)
Async XLA Ops:
  0.6 12.9 %copy-start = (f32[5,16,2048]{2,1,0:T(8,128)S(1)}, f32[5,16,2048]{2,1,0:T(8,128)}, u32[]{:S(2)}) copy-start(f32[5,16,2048]{2,1,0:T(8,128)} %state_hbm.1) | copy-start | bytes 1966084
  0.6 12.9 %copy-start.3 = (f32[2,16,2048]{2,1,0:T(8,128)S(1)}, f32[2,16,2048]{2,1,0:T(8,128)}, u32[]{:S(2)}) copy-start(f32[2,16,2048]{2,1,0:T(8,128)} %wind_hbm.1) | copy-start | bytes 786436
  0.7 12.9 %copy-start.4 = (f32[16,2048]{1,0:T(8,128)S(1)}, f32[16,2048]{1,0:T(8,128)}, u32[]{:S(2)}) copy-start(f32[16,2048]{1,0:T(8,128)} %strength_hbm.1) | copy-start | bytes 393220
  0.7 12.9 %copy-start.5 = (f32[16,2048]{1,0:T(8,128)S(1)}, f32[16,2048]{1,0:T(8,128)}, u32[]{:S(2)}) copy-start(f32[16,2048]{1,0:T(8,128)} %mass_hbm.1) | copy-start | bytes 393220
  0.7 12.9 %copy-start.7 = (s32[1,16]{1,0:T(1,128)S(1)}, s32[1,16]{1,0:T(1,128)}, u32[]{:S(2)}) copy-start(s32[1,16]{1,0:T(1,128)} %listed.1) | copy-start | bytes 196
  4.8 46.2 %collective-permute-start = (f32[2,3,24,2048]{3,2,1,0:T(8,128)}, f32[2,3,24,2048]{3,2,1,0:T(8,128)S(1)}, u32[]{:S(2)}, u32[]{:S(2)}) collective-permute-start(f32[2,3,24,2048]{3,2,1,0:T(8,128)} %get-tuple-element.14), channel_id=1, source_target_pairs={{0,1},{1,2},{2,3},{3,4},{4,5},{5,6},{6,7},{7,8},{8,9},{9,10},{10,1... | collective-permute-start | bytes 3538952 | tf_op jit(solution)/shard_map/ppermute | solution.py:686
  6.7 44.3 %collective-permute-start.1 = (f32[2,3,24,2048]{3,2,1,0:T(8,128)}, f32[2,3,24,2048]{3,2,1,0:T(8,128)S(1)}, u32[]{:S(2)}, u32[]{:S(2)}) collective-permute-start(f32[2,3,24,2048]{3,2,1,0:T(8,128)} %get-tuple-element.15), channel_id=1, source_target_pairs={{1,0},{2,1},{3,2},{4,3},{5,4},{6,5},{7,6},{8,7},{9,8},{10,9},{11,1... | collective-permute-start | bytes 3538952 | tf_op jit(solution)/shard_map/ppermute | solution.py:686
  11.3 21.0 %collective-permute-start.2 = (f32[3,16,24,128]{3,2,1,0:T(8,128)}, f32[3,16,24,128]{3,2,1,0:T(8,128)}, u32[]{:S(2)}, u32[]{:S(2)}) collective-permute-start(f32[3,16,24,128]{3,2,1,0:T(8,128)} %get-tuple-element.16), channel_id=1, source_target_pairs={{0,16},{1,17},{2,18},{3,19},{4,20},{5,21},{6,22},{7,23},{8,24},{9,... | collective-permute-start | bytes 1769480 | tf_op jit(solution)/shard_map/ppermute | solution.py:686
  13.5 0.9 %copy-start.6 = (f32[16,2048]{1,0:T(8,128)S(1)}, f32[16,2048]{1,0:T(8,128)}, u32[]{:S(2)}) copy-start(f32[16,2048]{1,0:T(8,128)} %fraction_hbm.1) | copy-start | bytes 393220
  14.4 17.9 %copy-start.1 = (f32[16,2048]{1,0:T(8,128)S(1)}, f32[16,2048]{1,0:T(8,128)}, u32[]{:S(2)}) copy-start(f32[16,2048]{1,0:T(8,128)} %bih.3) | copy-start | bytes 393220
  14.5 17.9 %copy-start.2 = (f32[2,16,2048]{2,1,0:T(8,128)S(1)}, f32[2,16,2048]{2,1,0:T(8,128)}, u32[]{:S(2)}) copy-start(f32[2,16,2048]{2,1,0:T(8,128)} %prev.1) | copy-start | bytes 786436
  51.1 4.4 %collective-permute-start.3 = (f32[2,3,24,128]{3,2,1,0:T(8,128)S(1)}, f32[2,3,24,128]{3,2,1,0:T(8,128)S(1)}, u32[]{:S(2)}, u32[]{:S(2)}) collective-permute-start(f32[2,3,24,128]{3,2,1,0:T(8,128)S(1)} %received_ends.1), channel_id=1, source_target_pairs={{0,16},{1,17},{2,18},{3,19},{4,20},{5,21},{6,22},{7,23},{8,24},{9,... | collective-permute-start | bytes 221192 | tf_op jit(solution)/shard_map/ppermute | solution.py:686
